TPU v7x, 32 devices: a whole 2x2x4 slice. The times are simulated.
32 devices in a mesh: members: 2 (over y), sub: 4 (over z), lev: 4 (over x, core).
Axes of the slice: x: 2, y: 2, z: 4, core: 2. Of those that a mesh axis runs over, the one named last changes fastest.
Arguments:
- tracer: float32 [96, 32, 512], P(('members', 'lev'), None, 'sub'), parts along dimension 0, may hold values from -6 to 6
- zonal_flow: float32 [96, 32, 512], P(('members', 'lev'), None, 'sub'), parts along dimension 0, may hold values from -1 to 1
- meridional_flow: float32 [96, 32, 512], P(('members', 'lev'), None, 'sub'), parts along dimension 0, may hold values from -1 to 1
- cotangent: float32 [96, 32, 512], P(('members', 'lev'), None, 'sub'), parts along dimension 0, may hold values from -6 to 6
- thickness: float32 [48], replicated, may hold values from 0.5 to 2
- wet_levels: int32 [32, 512], P(None, 'sub'), may hold values from 0 to 48
Outputs:
- next_tracer: float32 [96, 32, 512], P(('members', 'lev'), None, 'sub'), parts along dimension 0
- tracer_adjoint: float32 [96, 32, 512], P(('members', 'lev'), None, 'sub'), parts along dimension 0
- surface_adjoint: float32 [64, 512], P('members', 'sub'), parts along dimension 0
There are 2 independent parts, one for each index of `members`. A program takes and returns all parts, laid end to end along the dimension named above; an argument that names none is the same for every part. Nothing has to cross between parts.
Inputs may be any that keep to these rules, and one draw needn't show every extreme that they name: Level k (counted from 0) of a column is wet when k < wet_levels, land otherwise; 0 marks a land column.
All inputs are finite; a program needn't handle non-finite values.
Results may differ from a plain program's by a relative error of at most 0.0001.
Values sent between devices are 32-bit elements; how exact they have to be, the bound alone decides.
No kernel may reach another device: no remote copies, remote signals or barrier semaphores. Data moves between devices by JAX's collectives and lax.ppermute only.
A program may use at most 64 MiB of HBM per device.

v0:
```python
import jax
import jax.numpy as jnp
from jax import lax
from jax.sharding import PartitionSpec as P

ITERS = 3


ADVECT_STEP = 0.25
MIX_RATE = 2.0


def with_halo(cells, sides, width):
    for axis, dim in sides:
        count = lax.axis_size(axis)
        head = lax.slice_in_dim(cells, 0, width, axis=dim)
        tail = lax.slice_in_dim(cells, cells.shape[dim] - width, cells.shape[dim], axis=dim)
        cells = jnp.concatenate(
            [
                lax.ppermute(tail, axis, [(i, (i + 1) % count) for i in range(count)]),
                cells,
                lax.ppermute(head, axis, [((i + 1) % count, i) for i in range(count)]),
            ],
            axis=dim,
        )
    return cells


def thomas(lower_band, diagonal, upper_band, right_side):
    count = len(diagonal)
    ratios = []
    partial_value = []
    divisor = diagonal[0]
    ratios.append(upper_band[0] / divisor)
    partial_value.append(right_side[0] / divisor)
    for k in range(1, count):
        divisor = diagonal[k] - lower_band[k] * ratios[k - 1]
        ratios.append(upper_band[k] / divisor)
        partial_value.append((right_side[k] - lower_band[k] * partial_value[k - 1]) / divisor)
    result_rows = [None] * count
    result_rows[count - 1] = partial_value[count - 1]
    for k in range(count - 2, -1, -1):
        result_rows[k] = partial_value[k] - ratios[k] * result_rows[k + 1]
    return jnp.stack(result_rows)


def mix_columns(forward, cotangent, thickness, wet_mask):
    count = forward.shape[0]
    empty_level = jnp.zeros_like(forward[0])
    conduct = [empty_level]
    for k in range(1, count):
        spacing = 0.5 * (thickness[k - 1] + thickness[k])
        gradient = (forward[k] - forward[k - 1]) / spacing
        conduct.append(MIX_RATE * wet_mask[k] * (0.2 + 1.0 / (1.0 + gradient * gradient)) / spacing)
    conduct.append(empty_level)
    diagonal = [1.0 + (conduct[k] + conduct[k + 1]) / thickness[k] for k in range(count)]
    lower_band = [-conduct[k] / thickness[k] for k in range(count)]
    upper_band = [-conduct[k + 1] / thickness[k] for k in range(count)]
    lower_trans = [empty_level] + [-conduct[k] / thickness[k - 1] for k in range(1, count)]
    upper_trans = [-conduct[k + 1] / thickness[k + 1] for k in range(count - 1)] + [empty_level]
    mixed = thomas(lower_band, diagonal, upper_band, [forward[k] for k in range(count)])
    adjoint = thomas(lower_trans, diagonal, upper_trans, [cotangent[k] for k in range(count)])
    return (mixed, adjoint)


def barotropic(surface_field, damping):
    padded = with_halo(surface_field, (("sub", 1),), 1)
    beside = padded[:, :-2] + padded[:, 2:]
    beside = beside + jnp.roll(surface_field, 1, axis=0) + jnp.roll(surface_field, -1, axis=0)
    return (4.0 + damping) * surface_field - beside


def paired_sums(residual, image_field):
    return lax.psum((jnp.sum(residual * residual), jnp.sum(residual * image_field)), "sub")


def on_device(tracer, zonal_flow, meridional_flow, cotangent, thickness, wet_levels):
    own_count = tracer.shape[0]
    level_count = thickness.shape[0]
    first_level = lax.axis_index("lev") * own_count
    own_levels = first_level + jnp.arange(own_count, dtype=jnp.int32)
    wet_mask = (own_levels.reshape(own_count, 1, 1) < wet_levels[None]).astype(jnp.float32)
    all_levels = jnp.arange(level_count, dtype=jnp.int32).reshape(level_count, 1, 1)
    column_wet = (all_levels < wet_levels[None]).astype(jnp.float32)
    stacked = jnp.stack([tracer, zonal_flow])
    padded = with_halo(stacked, (("sub", 3),), 1)
    c_west = padded[0, :, :, :-2]
    c_east = padded[0, :, :, 2:]
    u_next = padded[1, :, :, 2:]
    flux_west = zonal_flow * (c_west + tracer) * 0.5
    flux_east = u_next * (tracer + c_east) * 0.5
    flux_y = meridional_flow * (jnp.roll(tracer, 1, axis=1) + tracer) * 0.5
    change = flux_east - flux_west + (jnp.roll(flux_y, -1, axis=1) - flux_y)
    forward = wet_mask * (tracer - ADVECT_STEP * change)
    gathered = (
        lax.all_gather(forward, "lev", axis=0, tiled=True),
        lax.all_gather(cotangent, "lev", axis=0, tiled=True),
    )
    mixed, adjoint = mix_columns(gathered[0], gathered[1], thickness, column_wet)
    next_tracer = lax.dynamic_slice_in_dim(mixed, first_level, own_count, 0)
    mixed_adjoint = lax.dynamic_slice_in_dim(adjoint, first_level, own_count, 0)
    pulled = wet_mask * mixed_adjoint
    padded_adj = with_halo(pulled, (("sub", 2),), 1)
    b_west = padded_adj[:, :, :-2]
    b_east = padded_adj[:, :, 2:]
    b_south = jnp.roll(pulled, 1, axis=1)
    b_north = jnp.roll(pulled, -1, axis=1)
    v_next = jnp.roll(meridional_flow, -1, axis=1)
    zonal_part = zonal_flow * (pulled - b_west) + u_next * (b_east - pulled)
    merid_part = meridional_flow * (pulled - b_south) + v_next * (b_north - pulled)
    tracer_adjoint = pulled + ADVECT_STEP * 0.5 * zonal_part + ADVECT_STEP * 0.5 * merid_part
    own_thick = lax.dynamic_slice_in_dim(thickness, first_level, own_count, 0).reshape(
        own_count, 1, 1
    )
    source = lax.psum(jnp.sum(own_thick * mixed_adjoint, axis=0), "lev")
    damping = 0.3 + jnp.sum(thickness.reshape(level_count, 1, 1) * column_wet, axis=0) / level_count
    surface = jnp.zeros_like(source)
    residual = source
    image_field = barotropic(residual, damping)
    norm_now, product = paired_sums(residual, image_field)
    step_size = norm_now / product
    direction, along = (residual, image_field)
    for sweep in range(ITERS):
        surface = surface + step_size * direction
        residual = residual - step_size * along
        if sweep + 1 < ITERS:
            image_field = barotropic(residual, damping)
            norm_next, product = paired_sums(residual, image_field)
            growth = norm_next / norm_now
            step_size = norm_next / (product - growth * norm_next / step_size)
            direction = residual + growth * direction
            along = image_field + growth * along
            norm_now = norm_next
    return (next_tracer, tracer_adjoint, surface)


def solution(mesh):
    return jax.shard_map(
        on_device,
        mesh=mesh,
        in_specs=(
            P(("members", "lev"), None, "sub"),
            P(("members", "lev"), None, "sub"),
            P(("members", "lev"), None, "sub"),
            P(("members", "lev"), None, "sub"),
            P(),
            P(None, "sub"),
        ),
        out_specs=(
            P(("members", "lev"), None, "sub"),
            P(("members", "lev"), None, "sub"),
            P("members", "sub"),
        ),
        check_vma=False,
    )
```

profile of v0, /device:TPU:0, one launch (start us, length us, event | category | flops | bytes accessed | tf_op | source)
XLA Modules:
  0.0 406.0 jit_solution(8491139523155195986)
XLA Ops:
  0.7 2.1 slice_maximum_fusion
  2.8 5.0 %collective-permute-start = (f32[2,12,32,1]{3,2,1,0:T(8,128)}, f32[2,12,32,1]{3,2,1,0:T(8,128)S(1)}, u32[]{:S(2)}, u32[]{:S(2)}) collective-permute-start(f32[2,12,32,1]{3,2,1,0:T(8,128)} %get-tuple-element.283), channel_id=1, source_target_pairs={{4,0},{8,4},{12,8},{0,12},{5,1},{9,5},{13,9},{1,13},{6,2},{10,6},{... | collective-permute-start | bytes 9224 | tf_op jit(solution)/shard_map/ppermute | solution.py:22
  7.8 0.7 fusion.544
  8.5 0.7 fusion.542
  9.2 0.7 fusion.543
  10.1 0.6 slice.1334
  10.9 0.8 select_reduce_fusion
  67.2 8.9 %all_gather.7 = f32[48,32,128]{2,1,0:T(8,128)S(1)} all-gather(f32[12,32,128]{2,1,0:T(8,128)} %param.9), channel_id=1, replica_groups=mesh['members'=2,'sub'=4,'lev'=4] {'lev'}, dimensions={0}, use_global_device_ids=true | all-gather | bytes 983040 | tf_op jit(solution)/shard_map/all_gather | solution.py:97
  80.9 1.3 compare_select_fusion.1
  82.2 8.7 %all_gather.6 = f32[48,32,128]{2,1,0:T(8,128)S(1)} all-gather(f32[12,32,128]{2,1,0:T(8,128)S(1)} %compare_select_fusion.1), channel_id=1, replica_groups=mesh['members'=2,'sub'=4,'lev'=4] {'lev'}, dimensions={0}, use_global_device_ids=true | all-gather | bytes 983040 | tf_op jit(solution)/shard_map/all_gather | solution.py:96
  90.9 26.4 %multiply_subtract_fusion.16 = (f32[32,128]{1,0:T(8,128)S(1)}, f32[32,128]{1,0:T(8,128)S(1)}, f32[32,128]{1,0:T(8,128)S(1)}, f32[32,128]{1,0:T(8,128)S(1)}, f32[...) fusion(f32[]{:T(128)} %bitcast.42, f32[]{:T(128)} %bitcast.43, ...), kind=kLoop, calls=%fused_computation.809 | loop fusion | flops 2846720 | bytes 1966396 | tf_op jit(solution)/shard_map/sub | solution.py:37
  117.4 32.7 %constant_dynamic-update-slice_fusion.95 = (f32[48,32,128]{2,1,0:T(8,128)S(1)}, f32[1,32,128]{2,1,0:T(8,128)S(1)}, f32[1,32,128]{2,1,0:T(8,128)S(1)}, f32[1,32,1...) fusion(f32[48,32,128]{2,1,0:T(8,128)S(1)} %all_gather.7, ...), kind=kLoop, calls=%fused_computation.102 | loop fusion | flops 4435967 | bytes 3899780
  150.0 3.2 constant_dynamic-update-slice_fusion.94
  153.3 3.2 constant_dynamic-update-slice_fusion.93
  156.5 0.7 constant_dynamic-update-slice_fusion.92
  157.2 0.6 constant_dynamic-update-slice_fusion.90
  157.8 0.6 constant_dynamic-update-slice_fusion.88
  158.4 0.7 constant_dynamic-update-slice_fusion.86
  159.2 0.6 constant_dynamic-update-slice_fusion.84
  159.8 0.7 constant_dynamic-update-slice_fusion.82
  160.5 0.6 constant_dynamic-update-slice_fusion.80
  161.2 0.6 constant_dynamic-update-slice_fusion.78
  161.8 0.6 constant_dynamic-update-slice_fusion.76
  162.4 0.6 constant_dynamic-update-slice_fusion.74
  163.1 0.6 constant_dynamic-update-slice_fusion.72
  163.7 0.6 constant_dynamic-update-slice_fusion.70
  164.3 0.6 constant_dynamic-update-slice_fusion.68
  165.0 0.6 constant_dynamic-update-slice_fusion.66
  165.6 0.6 constant_dynamic-update-slice_fusion.64
  166.2 0.6 constant_dynamic-update-slice_fusion.62
  166.8 0.6 constant_dynamic-update-slice_fusion.60
  167.4 0.6 constant_dynamic-update-slice_fusion.58
  168.1 23.5 %multiply_divide_fusion.64 = (f32[1,32,128]{2,1,0:T(8,128)S(1)}, f32[1,32,128]{2,1,0:T(8,128)S(1)}, f32[1,32,128]{2,1,0:T(8,128)S(1)}, f32[1,32,128]{2,1,0:T(8,1...) fusion(f32[1,32,128]{2,1,0:T(8,128)S(1)} %get-tuple-element.133, ...), kind=kLoop, calls=%fused_computation.1174 | loop fusion | flops 1351680 | bytes 1179804 | tf_op jit(solution)/shard_map/div | solution.py:38
  191.6 23.4 %subtract_divide_fusion.40 = (f32[1,32,128]{2,1,0:T(8,128)S(1)}, f32[1,32,128]{2,1,0:T(8,128)S(1)}, f32[1,32,128]{2,1,0:T(8,128)S(1)}, f32[1,32,128]{2,1,0:T(8,1...) fusion(f32[48,32,128]{2,1,0:T(8,128)S(1)} %all_gather.6, ...), kind=kLoop, calls=%fused_computation.1178 | loop fusion | flops 1507328 | bytes 2359452 | tf_op jit(solution)/shard_map/div | solution.py:39
  215.0 8.4 %constant_dynamic-update-slice_fusion.47 = (f32[48,32,128]{2,1,0:T(8,128)S(1)}, f32[1,32,128]{2,1,0:T(8,128)S(1)}, f32[1,32,128]{2,1,0:T(8,128)S(1)}, f32[1,32,1...) fusion(f32[1,32,128]{2,1,0:T(8,128)S(1)} %get-tuple-element.280, ...), kind=kLoop, calls=%fused_computation.54 | loop fusion | flops 1273855 | bytes 1949792
  223.4 1.3 constant_dynamic-update-slice_fusion.46
  225.2 30.8 %constant_dynamic-update-slice_fusion.55 = (f32[48,32,128]{2,1,0:T(8,128)S(1)}, f32[32,128]{1,0:T(8,128)S(1)}, f32[32,128]{1,0:T(8,128)S(1)}, f32[32,128]{1,0:T(...) fusion(f32[48,32,128]{2,1,0:T(8,128)S(1)} %get-tuple-element.36, ...), kind=kLoop, calls=%fused_computation.62 | loop fusion | flops 2617344 | bytes 2015468
  256.0 28.6 %multiply_divide_fusion.48 = (f32[32,128]{1,0:T(8,128)S(1)}, f32[32,128]{1,0:T(8,128)S(1)}, f32[32,128]{1,0:T(8,128)S(1)}, f32[32,128]{1,0:T(8,128)S(1)}, f32[32,128]{1,0:T(8,128)S(1)}, /*index=5*/f32[32,128]{1,0:T(8,128)S(1)}) fusion(f32[32,128]{1,0:T(8,128)S(1)} %get-tuple-element.28, f32[]{:T(128)} %bitcast.49, f32[32,128]{1,0:T(8,128)S(1)} %get-tuple-element.29, ...), kind=kLoop, calls=%fused_computation.1014 | loop fusion | flops 1646592 | bytes 835772 | tf_op jit(solution)/shard_map/div | solution.py:38
  284.6 28.6 %fusion.162 = (f32[32,128]{1,0:T(8,128)S(1)}, f32[32,128]{1,0:T(8,128)S(1)}, f32[32,128]{1,0:T(8,128)S(1)}, f32[32,128]{1,0:T(8,128)S(1)}, f32[32,128]{1,0:T(8,128)S(1)}) fusion(f32[48,32,128]{2,1,0:T(8,128)S(1)} %all_gather.6, f32[]{:T(128)} %bitcast.49, f32[32,128]{1,0:T(8,128)S(1)} %get-tuple-element.29, f32[32,128]{1,0:T(8,128)S(1)} %get-tuple-element.177, ...), kind=kLoop, calls=%fused_computation.362 | loop fusion | flops 2097152 | bytes 1638588 | tf_op jit(solution)/shard_map/div | solution.py:39
  313.2 3.2 constant_dynamic-update-slice_fusion.7
  316.5 3.2 constant_dynamic-update-slice_fusion.54
  319.7 3.2 constant_dynamic-update-slice_fusion.53
  322.9 0.6 constant_dynamic-update-slice_fusion.52
  323.5 0.6 constant_dynamic-update-slice_fusion.50
  324.1 1.9 constant_dynamic-update-slice_fusion.48
  326.1 0.1 multiply_reduce_fusion
  326.2 10.8 %psum.49 = f32[32,128]{1,0:T(8,128)S(1)} all-reduce(f32[32,128]{1,0:T(8,128)S(1)} %get-tuple-element.281), channel_id=1, replica_groups=mesh['members'=2,'sub'=4,'lev'=4] {'lev'}, use_global_device_ids=true, to_apply=%region_1.2 | all-reduce | flops 4096 | bytes 32768 | tf_op jit(solution)/shard_map/psum | solution.py:115
  337.0 0.1 fusion.532
  337.3 3.8 collective-permute-start.5
  341.1 3.8 collective-permute-start.3
  344.9 0.7 constant_dynamic-slice_fusion
  345.6 0.7 multiply_reduce_fusion.4
  346.3 10.2 %all-reduce.2 = (f32[]{:T(128)}, f32[]{:T(128)}) all-reduce(f32[]{:T(128)} %get-tuple-element.8, f32[]{:T(128)} %get-tuple-element.7), channel_id=1, replica_groups=mesh['members'=2,'sub'=4,'lev'=4] {'sub'}, use_global_device_ids=true, to_apply=%region_3.4 | all-reduce | flops 2 | bytes 16 | tf_op jit(solution)/shard_map/psum | solution.py:74
  358.0 0.7 collective-permute-start.6
  358.7 3.1 collective-permute-start.7
  361.8 1.7 collective-permute-done.6
  363.5 0.7 multiply_reduce_fusion.2
  364.2 12.9 %all-reduce.1 = (f32[]{:T(128)}, f32[]{:T(128)}) all-reduce(f32[]{:T(128)} %get-tuple-element.6, f32[]{:T(128)} %get-tuple-element.5), channel_id=1, replica_groups=mesh['members'=2,'sub'=4,'lev'=4] {'sub'}, use_global_device_ids=true, to_apply=%region_8.9 | all-reduce | flops 2 | bytes 16 | tf_op jit(solution)/shard_map/psum | solution.py:74
  381.6 3.8 collective-permute-start.9
  385.4 1.7 collective-permute-done.8
  387.1 0.7 fusion.31
  387.8 12.8 %all-reduce = (f32[]{:T(128)}, f32[]{:T(128)}) all-reduce(f32[]{:T(128)} %get-tuple-element.4, f32[]{:T(128)} %get-tuple-element.3), channel_id=1, replica_groups=mesh['members'=2,'sub'=4,'lev'=4] {'sub'}, use_global_device_ids=true, to_apply=%region_12.13 | all-reduce | flops 2 | bytes 16 | tf_op jit(solution)/shard_map/psum | solution.py:74
  404.4 0.6 multiply_add_fusion
  405.0 1.0 fusion.6
  (111 shorter events, 1.1 us)
Async XLA Ops:
  0.6 9.4 %copy-start = (f32[12,32,128]{2,1,0:T(8,128)S(1)}, f32[12,32,128]{2,1,0:T(8,128)}, u32[]{:S(2)}) copy-start(f32[12,32,128]{2,1,0:T(8,128)} %param.6) | copy-start | bytes 589828
  0.6 9.4 %copy-start.2 = (f32[12,32,128]{2,1,0:T(8,128)S(1)}, f32[12,32,128]{2,1,0:T(8,128)}, u32[]{:S(2)}) copy-start(f32[12,32,128]{2,1,0:T(8,128)} %param.8) | copy-start | bytes 589828
  2.8 5.1 %copy-start.3 = (f32[48]{0:T(128)S(1)}, f32[48]{0:T(128)}, u32[]{:S(2)}) copy-start(f32[48]{0:T(128)} %param.10) | copy-start | bytes 580
  2.8 78.1 %collective-permute-start = (f32[2,12,32,1]{3,2,1,0:T(8,128)}, f32[2,12,32,1]{3,2,1,0:T(8,128)S(1)}, u32[]{:S(2)}, u32[]{:S(2)}) collective-permute-start(f32[2,12,32,1]{3,2,1,0:T(8,128)} %get-tuple-element.283), channel_id=1, source_target_pairs={{4,0},{8,4},{12,8},{0,12},{5,1},{9,5},{13,9},{1,13},{6,2},{10,6},{... | collective-permute-start | bytes 9224 | tf_op jit(solution)/shard_map/ppermute | solution.py:22
  7.8 73.1 %collective-permute-start.1 = (f32[2,12,32,1]{3,2,1,0:T(8,128)S(1)}, f32[2,12,32,1]{3,2,1,0:T(8,128)}, u32[]{:S(2)}, u32[]{:S(2)}) collective-permute-start(f32[2,12,32,1]{3,2,1,0:T(8,128)S(1)} %get-tuple-element.284), channel_id=1, source_target_pairs={{0,4},{4,8},{8,12},{12,0},{1,5},{5,9},{9,13},{13,1},{2,6},{6,10},{... | collective-permute-start | bytes 9224 | tf_op jit(solution)/shard_map/ppermute | solution.py:20
  10.1 0.7 copy-start.4
  67.2 13.7 %copy-start.1 = (f32[12,32,128]{2,1,0:T(8,128)S(1)}, f32[12,32,128]{2,1,0:T(8,128)}, u32[]{:S(2)}) copy-start(f32[12,32,128]{2,1,0:T(8,128)} %param.7) | copy-start | bytes 589828
  324.1 1.9 copy-start.5
  337.2 8.4 %collective-permute-start.4 = (f32[32,1]{1,0:T(8,128)S(1)}, f32[32,1]{1,0:T(8,128)S(1)}, u32[]{:S(2)}, u32[]{:S(2)}) collective-permute-start(f32[32,1]{1,0:T(8,128)S(1)} %get-tuple-element.305), channel_id=1, source_target_pairs={{0,4},{4,8},{8,12},{12,0},{1,5},{5,9},{9,13},{13,1},{2,6},{6,10},{... | collective-permute-start | bytes 392 | tf_op jit(solution)/shard_map/ppermute | solution.py:20
  337.3 8.3 %collective-permute-start.5 = (f32[32,1]{1,0:T(8,128)S(1)}, f32[32,1]{1,0:T(8,128)S(1)}, u32[]{:S(2)}, u32[]{:S(2)}) collective-permute-start(f32[32,1]{1,0:T(8,128)S(1)} %get-tuple-element.306), channel_id=1, source_target_pairs={{4,0},{8,4},{12,8},{0,12},{5,1},{9,5},{13,9},{1,13},{6,2},{10,6},{... | collective-permute-start | bytes 392 | tf_op jit(solution)/shard_map/ppermute | solution.py:22
  341.1 63.9 %collective-permute-start.2 = (f32[12,32,1]{2,1,0:T(8,128)S(1)}, f32[12,32,1]{2,1,0:T(8,128)S(1)}, u32[]{:S(2)}, u32[]{:S(2)}) collective-permute-start(f32[12,32,1]{2,1,0:T(8,128)S(1)} %get-tuple-element.289), channel_id=1, source_target_pairs={{0,4},{4,8},{8,12},{12,0},{1,5},{5,9},{9,13},{13,1},{2,6},{6,10},{... | collective-permute-start | bytes 4616 | tf_op jit(solution)/shard_map/ppermute | solution.py:20
  341.1 63.9 %collective-permute-start.3 = (f32[12,32,1]{2,1,0:T(8,128)S(1)}, f32[12,32,1]{2,1,0:T(8,128)S(1)}, u32[]{:S(2)}, u32[]{:S(2)}) collective-permute-start(f32[12,32,1]{2,1,0:T(8,128)S(1)} %get-tuple-element.290), channel_id=1, source_target_pairs={{4,0},{8,4},{12,8},{0,12},{5,1},{9,5},{13,9},{1,13},{6,2},{10,6},{... | collective-permute-start | bytes 4616 | tf_op jit(solution)/shard_map/ppermute | solution.py:22
  344.9 0.7 copy-start.6
  358.0 5.5 %collective-permute-start.6 = (f32[32,1]{1,0:T(8,128)S(1)}, f32[32,1]{1,0:T(8,128)S(1)}, u32[]{:S(2)}, u32[]{:S(2)}) collective-permute-start(f32[32,1]{1,0:T(8,128)S(1)} %get-tuple-element.299), channel_id=1, source_target_pairs={{0,4},{4,8},{8,12},{12,0},{1,5},{5,9},{9,13},{13,1},{2,6},{6,10},{... | collective-permute-start | bytes 392 | tf_op jit(solution)/shard_map/ppermute | solution.py:20
  358.7 4.8 %collective-permute-start.7 = (f32[32,1]{1,0:T(8,128)S(1)}, f32[32,1]{1,0:T(8,128)S(1)}, u32[]{:S(2)}, u32[]{:S(2)}) collective-permute-start(f32[32,1]{1,0:T(8,128)S(1)} %get-tuple-element.300), channel_id=1, source_target_pairs={{4,0},{8,4},{12,8},{0,12},{5,1},{9,5},{13,9},{1,13},{6,2},{10,6},{... | collective-permute-start | bytes 392 | tf_op jit(solution)/shard_map/ppermute | solution.py:22
  381.6 5.5 %collective-permute-start.8 = (f32[32,1]{1,0:T(8,128)S(1)}, f32[32,1]{1,0:T(8,128)S(1)}, u32[]{:S(2)}, u32[]{:S(2)}) collective-permute-start(f32[32,1]{1,0:T(8,128)S(1)} %get-tuple-element.297), channel_id=1, source_target_pairs={{0,4},{4,8},{8,12},{12,0},{1,5},{5,9},{9,13},{13,1},{2,6},{6,10},{... | collective-permute-start | bytes 392 | tf_op jit(solution)/shard_map/ppermute | solution.py:20
  381.6 5.5 %collective-permute-start.9 = (f32[32,1]{1,0:T(8,128)S(1)}, f32[32,1]{1,0:T(8,128)S(1)}, u32[]{:S(2)}, u32[]{:S(2)}) collective-permute-start(f32[32,1]{1,0:T(8,128)S(1)} %get-tuple-element.298), channel_id=1, source_target_pairs={{4,0},{8,4},{12,8},{0,12},{5,1},{9,5},{13,9},{1,13},{6,2},{10,6},{... | collective-permute-start | bytes 392 | tf_op jit(solution)/shard_map/ppermute | solution.py:22
where the time goes:
time: 411 us; the launch traced here: 406 us
  other arithmetic  242 us (59%)
  between operations  71.2 us (17%)
  blocking collectives  64.3 us (16%)
  starting transfers between devices  20.4 us (5%)
  local copies, waits for them, and re-layouts  4.26 us (1%)
    unnamed x50, other arithmetic  102 us
    div x2, other arithmetic, thomas(): (right_side[k] - lower_band[k] * partial_value[k - 1]) / divisor  52 us
    div x2, other arithmetic, thomas(): ratios.append(upper_band[k] / divisor)  52 us
    psum x3, blocking collectives, paired_sums(): lax.psum((jnp.sum(residual * residual), jnp.sum(residual * image_field)),...  35.9 us
    sub x1, other arithmetic, thomas(): divisor = diagonal[k] - lower_band[k] * ratios[k - 1]  26.4 us
    ppermute x5, starting transfers between devices, with_halo(): lax.ppermute(head, axis, [((i + 1) % count, i) for i in range(count)])  19.6 us
    psum x1, blocking collectives, on_device(): source = lax.psum(jnp.sum(own_thick * mixed_adjoint, axis=0), 'lev')  10.8 us
    all_gather x1, blocking collectives, on_device(): lax.all_gather(cotangent, 'lev', axis=0, tiled=True)  8.94 us
  transfers between devices with their start and end apart: 10, of which 2 were waited for; matrix products, arithmetic and copies ran while one was open for 2% of the time, Pallas kernels for 0%

commit v1 on v0

v1 whole, which is shorter than its diff:
```python
import functools

import jax
import jax.numpy as jnp
from jax import lax
from jax.experimental import pallas as pl
from jax.experimental.pallas import tpu as pltpu
from jax.sharding import PartitionSpec as P

ITERS = 3
ADVECT_STEP = 0.25
MIX_RATE = 2.0
HALF_STEP = 0.5 * ADVECT_STEP

N_BLOCK = 12
N_LAST = 6

VMEM_IN = pl.BlockSpec(memory_space=pltpu.VMEM)
SMEM_IN = pl.BlockSpec(memory_space=pltpu.SMEM)


def in_vmem(*shape):
    return pltpu.VMEM(shape, jnp.float32)


def lanes(rows, width):
    return lax.broadcasted_iota(jnp.int32, (rows, width), 1)


def turn(field, shift, axis):
    size = field.shape[axis]
    shift = shift % size
    return field if shift == 0 else pltpu.roll(field, shift, axis)


def splat(scalar, width):
    return jnp.full((1, width), scalar, jnp.float32)


def conductance(drop, upper_thick, lower_thick, wet):
    spacing = 0.5 * (upper_thick + lower_thick)
    rate = 0.2 / spacing + spacing / (spacing * spacing + drop * drop)
    return jnp.where(wet, MIX_RATE * rate, 0.0)


def pack_kernel(tracer_ref, zonal_ref, east_ref, west_ref):
    own, rows, width = tracer_ref.shape
    lane = lanes(rows, width)
    east = jnp.zeros((rows, width), jnp.float32)
    west = jnp.zeros((rows, width), jnp.float32)
    for k in range(own):
        values = tracer_ref[k]
        east = jnp.where(lane == k, turn(values, k + 1, 1), east)
        west = jnp.where(lane == k, turn(values, k, 1), west)
        west = jnp.where(lane == own + k, turn(zonal_ref[k], own + k, 1), west)
    east_ref[...] = east
    west_ref[...] = west


def local_kernel(
    thick_ref, wet_ref, tracer_ref, zonal_ref, merid_ref, cot_ref, from_west_ref, from_east_ref,
    block_ref, forward_ref, adjoint_ref, top_ref, bottom_ref, u_next_ref, damping_ref,
):
    own, rows, width = tracer_ref.shape
    level_count = thick_ref.shape[0]
    first = lax.axis_index("lev") * own
    lane = lanes(rows, width)
    wet_levels = wet_ref[...]
    from_west = from_west_ref[...]
    from_east = from_east_ref[...]
    forward = []
    for k in range(own):
        values = tracer_ref[k]
        zonal = zonal_ref[k]
        merid = merid_ref[k]
        c_west = jnp.where(lane == 0, turn(from_west, -k, 1), turn(values, 1, 1))
        c_east = jnp.where(lane == width - 1, turn(from_east, width - 1 - k, 1), turn(values, -1, 1))
        u_next = jnp.where(lane == width - 1, turn(from_east, width - 1 - own - k, 1), turn(zonal, -1, 1))
        u_next_ref[k] = u_next
        flux_y = merid * (turn(values, 1, 0) + values)
        change = u_next * (values + c_east) - zonal * (c_west + values) + (turn(flux_y, -1, 0) - flux_y)
        forward.append(jnp.where(wet_levels > first + k, values - HALF_STEP * change, 0.0))

    thick = [splat(thick_ref[first + k], width) for k in range(own)]
    conduct = [None]
    for k in range(1, own):
        conduct.append(
            conductance(forward[k] - forward[k - 1], thick[k - 1], thick[k], wet_levels > first + k)
        )
    pivot = jnp.broadcast_to(thick[0], (rows, width))
    ratio, scale = [None], []
    g_forward = [thick[0] * forward[0]]
    g_adjoint = [cot_ref[0]]
    g_top = [jnp.ones((rows, width), jnp.float32)]
    for k in range(1, own):
        inverse = 1.0 / (pivot + conduct[k])
        scale.append(inverse)
        ratio.append(conduct[k] * inverse)
        pivot = thick[k] + pivot * ratio[k]
        g_forward.append(thick[k] * forward[k] + ratio[k] * g_forward[k - 1])
        g_adjoint.append(cot_ref[k] + ratio[k] * g_adjoint[k - 1])
        g_top.append(ratio[k] * g_top[k - 1])
    scale.append(1.0 / pivot)
    last = own - 1
    y_forward = g_forward[last] * scale[last]
    y_adjoint = g_adjoint[last] * scale[last]
    y_top = g_top[last] * scale[last]
    y_bottom = scale[last]
    block_ref[1] = y_top
    block_ref[2] = y_bottom
    block_ref[4] = y_forward
    block_ref[6] = y_adjoint
    block_ref[7] = forward[0]
    block_ref[8] = forward[last]
    sums = [jnp.zeros((rows, width), jnp.float32)] * 3
    for k in range(last, -1, -1):
        if k < last:
            y_forward = g_forward[k] * scale[k] + ratio[k + 1] * y_forward
            y_adjoint = g_adjoint[k] * scale[k] + ratio[k + 1] * y_adjoint
            y_top = g_top[k] * scale[k] + ratio[k + 1] * y_top
            y_bottom = ratio[k + 1] * y_bottom
        forward_ref[k] = y_forward
        adjoint_ref[k] = y_adjoint
        top_ref[k] = y_top
        bottom_ref[k] = y_bottom
        square = thick[k] * thick[k]
        sums = [s + square * y for s, y in zip(sums, (y_adjoint, y_top, y_bottom))]
    block_ref[0] = y_top
    block_ref[3] = y_forward
    block_ref[5] = y_adjoint
    block_ref[9] = sums[0]
    block_ref[10] = sums[1]
    block_ref[11] = sums[2]

    def add_level(k, total):
        return total + jnp.where(wet_levels > k, thick_ref[k], 0.0)

    depth = lax.fori_loop(0, level_count, add_level, jnp.zeros((rows, width), jnp.float32), unroll=8)
    damping_ref[...] = 0.3 + depth / level_count


def merge_kernel(size, final, own, thick_ref, wet_ref, mine_ref, other_ref, block_ref, flux_ref):
    place = lax.axis_index("lev")
    width = wet_ref.shape[1]
    upper = lax.rem(place // size, 2) == 0
    above = [jnp.where(upper, mine_ref[i], other_ref[i]) for i in range(N_BLOCK)]
    below = [jnp.where(upper, other_ref[i], mine_ref[i]) for i in range(N_BLOCK)]
    start = (place // (2 * size) * 2 + 1) * size * own
    rate = conductance(
        below[7] - above[8],
        splat(thick_ref[start - 1], width),
        splat(thick_ref[start], width),
        wet_ref[...] > start,
    )
    rate = rate / (1.0 + rate * (below[0] + above[2]))
    by_forward = rate * (below[3] - above[4])
    by_adjoint = rate * (below[5] - above[6])
    by_top = -rate * above[1]
    by_bottom = rate * below[1]
    flux_ref[0] = by_forward
    flux_ref[1] = by_adjoint
    flux_ref[2] = by_top
    flux_ref[3] = by_bottom
    spread = above[11] - below[10]
    merged = [
        above[0] + above[1] * by_top,
        -below[1] * by_top,
        below[2] - below[1] * by_bottom,
        above[3] + above[1] * by_forward,
        below[4] - below[1] * by_forward,
        above[5] + above[1] * by_adjoint,
        below[6] - below[1] * by_adjoint,
        above[7],
        below[8],
        above[9] + below[9] + by_adjoint * spread,
        above[10] + by_top * spread,
        below[11] + by_bottom * spread,
    ]
    if final:
        upper_next = lax.rem(place // (2 * size), 2) == 0
        merged = last_fields(upper_next, merged)
    for i, field in enumerate(merged):
        block_ref[i] = field


def last_fields(upper, block):
    return [
        jnp.where(upper, block[2], block[0]),
        jnp.where(upper, block[4], block[3]),
        jnp.where(upper, block[6], block[5]),
        jnp.where(upper, block[8], block[7]),
        block[9],
        jnp.where(upper, block[11], block[10]),
    ]


def pick_kernel(size, block_ref, out_ref):
    upper = lax.rem(lax.axis_index("lev") // size, 2) == 0
    block = [block_ref[i] for i in range(N_BLOCK)]
    for i, field in enumerate(last_fields(upper, block)):
        out_ref[i] = field


def final_kernel(
    sizes, own, thick_ref, wet_ref, mine_ref, other_ref, adjoint_ref, top_ref, bottom_ref, damping_ref, *rest
):
    flux_refs, message_ref, ends_ref, pulled_ref = rest[:-3], rest[-3], rest[-2], rest[-1]
    rows, width = wet_ref.shape
    place = lax.axis_index("lev")
    size = sizes[-1]
    upper = lax.rem(place // size, 2) == 0
    start = (place // (2 * size) * 2 + 1) * size * own
    wet_levels = wet_ref[...]
    rate = conductance(
        mine_ref[3] - other_ref[3],
        splat(thick_ref[start - 1], width),
        splat(thick_ref[start], width),
        wet_levels > start,
    )
    rate = rate / (1.0 + rate * (mine_ref[0] + other_ref[0]))
    in_forward = rate * (other_ref[1] - mine_ref[1])
    in_adjoint = rate * (other_ref[2] - mine_ref[2])
    source = mine_ref[4] + other_ref[4] + in_adjoint * (mine_ref[5] - other_ref[5])
    ends = []
    for into, index in ((in_forward, 0), (in_adjoint, 1)):
        top = jnp.where(upper, 0.0, into)
        bottom = jnp.where(upper, into, 0.0)
        for step in range(len(sizes) - 2, -1, -1):
            flux_ref = flux_refs[step]
            flux = flux_ref[index] + top * flux_ref[2] + bottom * flux_ref[3]
            above = lax.rem(place // sizes[step], 2) == 0
            top, bottom = jnp.where(above, top, -flux), jnp.where(above, flux, bottom)
        ends += [top, bottom]
    for i in range(4):
        ends_ref[i] = ends[i]
    lane = lanes(rows, width)
    first = place * own
    edges = jnp.zeros((rows, width), jnp.float32)
    for k in range(own):
        mixed = adjoint_ref[k] + top_ref[k] * ends[2] + bottom_ref[k] * ends[3]
        pulled = jnp.where(wet_levels > first + k, thick_ref[first + k] * mixed, 0.0)
        pulled_ref[k] = pulled
        edges = jnp.where(lane == k, turn(pulled, k, 1), edges)
        edges = jnp.where(lane == own + k, turn(pulled, own + k + 1, 1), edges)
    message_ref[0] = source
    message_ref[1] = edges
    message_ref[2] = damping_ref[...]


def forward_kernel(forward_ref, top_ref, bottom_ref, ends_ref, out_ref):
    top = ends_ref[0]
    bottom = ends_ref[1]
    for k in range(forward_ref.shape[0]):
        out_ref[k] = forward_ref[k] + top_ref[k] * top + bottom_ref[k] * bottom


def total(field):
    while field.ndim > 2:
        field = jnp.sum(field, axis=0)
    return jnp.sum(jnp.sum(field, axis=0, keepdims=True), axis=1, keepdims=True)


def surface_kernel(
    pulled_ref, zonal_ref, merid_ref, u_next_ref, messages_ref, tracer_adjoint_ref, surface_ref,
    source_scr, damping_scr,
):
    own, rows, width = pulled_ref.shape
    count = messages_ref.shape[0]
    place = lax.axis_index("sub")
    lane = lanes(rows, width)
    west_edges = jnp.zeros((rows, width), jnp.float32)
    east_edges = jnp.zeros((rows, width), jnp.float32)
    for i in range(count):
        owner = jnp.bitwise_xor(place, i)
        source_scr[owner] = messages_ref[i, 0]
        damping_scr[owner] = messages_ref[i, 2]
    west_edges = messages_ref[jnp.bitwise_xor(place, lax.rem(place + count - 1, count)), 1]
    east_edges = messages_ref[jnp.bitwise_xor(place, lax.rem(place + 1, count)), 1]
    for k in range(own):
        pulled = pulled_ref[k]
        merid = merid_ref[k]
        b_west = jnp.where(lane == 0, turn(west_edges, -own - k, 1), turn(pulled, 1, 1))
        b_east = jnp.where(lane == width - 1, turn(east_edges, width - 1 - k, 1), turn(pulled, -1, 1))
        across = zonal_ref[k] * (pulled - b_west) + u_next_ref[k] * (b_east - pulled)
        step = merid * (pulled - turn(pulled, 1, 0))
        across = across + step + turn(step, -1, 0)
        tracer_adjoint_ref[k] = pulled + HALF_STEP * across

    first_lane = lax.broadcasted_iota(jnp.int32, (count, rows, width), 2) == 0
    last_lane = lax.broadcasted_iota(jnp.int32, (count, rows, width), 2) == width - 1
    damping = 4.0 + damping_scr[...]

    def beside(field, shift):
        return jnp.concatenate([field[-shift:], field[:-shift]]) if count > 1 else field

    def image_of(field):
        west = turn(field, 1, 2)
        west = jnp.where(first_lane, beside(west, 1), west)
        east = turn(field, -1, 2)
        east = jnp.where(last_lane, beside(east, -1), east)
        return damping * field - (west + east + turn(field, 1, 1) + turn(field, -1, 1))

    residual = source_scr[...]
    image = image_of(residual)
    norm = total(residual * residual)
    step_size = norm / total(residual * image)
    direction, along = residual, image
    surface = jnp.zeros_like(residual)
    for sweep in range(ITERS):
        surface = surface + step_size * direction
        if sweep + 1 < ITERS:
            residual = residual - step_size * along
            image = image_of(residual)
            norm_next = total(residual * residual)
            product = total(residual * image)
            growth = norm_next / norm
            step_size = norm_next / (product - growth * norm_next / step_size)
            direction = residual + growth * direction
            along = image + growth * along
            norm = norm_next
    source_scr[...] = surface
    surface_ref[...] = source_scr[place]


def on_device(tracer, zonal_flow, meridional_flow, cotangent, thickness, wet_levels):
    own, rows, width = tracer.shape
    lev_count = lax.axis_size("lev")
    sub_count = lax.axis_size("sub")
    edge = in_vmem(rows, width)
    levels = in_vmem(own, rows, width)

    east, west = pl.pallas_call(
        pack_kernel, out_shape=(edge, edge), in_specs=[VMEM_IN] * 2, out_specs=(VMEM_IN,) * 2, name="pack"
    )(tracer, zonal_flow)
    ring = [(i, (i + 1) % sub_count) for i in range(sub_count)]
    from_west = lax.ppermute(east, "sub", ring)
    from_east = lax.ppermute(west, "sub", [(b, a) for a, b in ring])

    block, forward, adjoint, top, bottom, u_next, damping = pl.pallas_call(
        local_kernel,
        out_shape=(in_vmem(N_BLOCK, rows, width), levels, levels, levels, levels, levels, edge),
        in_specs=[SMEM_IN] + [VMEM_IN] * 7,
        out_specs=(VMEM_IN,) * 7,
        name="local",
    )(thickness, wet_levels, tracer, zonal_flow, meridional_flow, cotangent, from_west, from_east)

    sizes = [1]
    while sizes[-1] * 2 < lev_count:
        sizes.append(sizes[-1] * 2)
    fluxes = []
    if len(sizes) == 1:
        block = pl.pallas_call(
            functools.partial(pick_kernel, 1), out_shape=in_vmem(N_LAST, rows, width),
            in_specs=[VMEM_IN], out_specs=VMEM_IN, name="pick",
        )(block)
    for size in sizes:
        other = lax.ppermute(block, "lev", [(i, i ^ size) for i in range(lev_count)])
        if size == sizes[-1]:
            break
        final = size * 2 == sizes[-1]
        block, flux = pl.pallas_call(
            functools.partial(merge_kernel, size, final, own),
            out_shape=(in_vmem(N_LAST if final else N_BLOCK, rows, width), in_vmem(4, rows, width)),
            in_specs=[SMEM_IN] + [VMEM_IN] * 3,
            out_specs=(VMEM_IN,) * 2,
            name="merge",
        )(thickness, wet_levels, block, other)
        fluxes.append(flux)

    message, ends, pulled = pl.pallas_call(
        functools.partial(final_kernel, sizes, own),
        out_shape=(in_vmem(3, rows, width), in_vmem(4, rows, width), levels),
        in_specs=[SMEM_IN] + [VMEM_IN] * (7 + len(fluxes)),
        out_specs=(VMEM_IN,) * 3,
        name="final",
    )(thickness, wet_levels, block, other, adjoint, top, bottom, damping, *fluxes)

    messages = message[None]
    size = 1
    while size < sub_count:
        got = lax.ppermute(messages, "sub", [(i, i ^ size) for i in range(sub_count)])
        messages = jnp.concatenate([messages, got])
        size *= 2

    next_tracer = pl.pallas_call(
        forward_kernel,
        out_shape=jax.ShapeDtypeStruct(tracer.shape, jnp.float32),
        in_specs=[VMEM_IN] * 4,
        out_specs=VMEM_IN,
        name="forward",
    )(forward, top, bottom, ends)

    tracer_adjoint, surface = pl.pallas_call(
        surface_kernel,
        out_shape=(
            jax.ShapeDtypeStruct(tracer.shape, jnp.float32),
            jax.ShapeDtypeStruct((rows, width), jnp.float32),
        ),
        in_specs=[VMEM_IN] * 5,
        out_specs=(VMEM_IN,) * 2,
        scratch_shapes=[pltpu.VMEM((sub_count, rows, width), jnp.float32)] * 2,
        name="surface",
    )(pulled, zonal_flow, meridional_flow, u_next, messages)
    return (next_tracer, tracer_adjoint, surface)


def solution(mesh):
    whole = P(("members", "lev"), None, "sub")
    return jax.shard_map(
        on_device,
        mesh=mesh,
        in_specs=(whole, whole, whole, whole, P(), P(None, "sub")),
        out_specs=(whole, whole, P("members", "sub")),
        check_vma=False,
    )
```

time: 411 us -> 40.3 us (0.10); the launches traced: 406 us -> 40 us
  other arithmetic: 242 us -> 0.69 us
  between operations: 71.2 us -> 0.73 us
  blocking collectives: 64.3 us -> 0 us
  starting transfers between devices: 20.4 us -> 9.58 us
  Pallas kernels: 0 us -> 10.1 us
  waiting for transfers between devices: 3.44 us -> 12.6 us
    div x4 -> x0, other arithmetic: 104 us -> none  [the longest x2 52 us: thomas(): (right_side[k] - lower_band[k] * partial_value[k - 1]) / divisor]
    unnamed x50 -> x0, other arithmetic: 102 us -> none
    psum x4 -> x0, blocking collectives: 46.7 us -> none  [the longest x3 35.9 us: paired_sums(): lax.psum((jnp.sum(residual * residual), jnp.sum(residual * image_field)),...]
    sub x3 -> x0, other arithmetic: 26.5 us -> none  [the longest x1 26.4 us: thomas(): divisor = diagonal[k] - lower_band[k] * ratios[k - 1]]
    all_gather x2 -> x0, blocking collectives: 17.7 us -> none  [the longest x1 8.94 us: on_device(): lax.all_gather(cotangent, 'lev', axis=0, tiled=True)]
    ppermute x10 -> x6, starting transfers between devices: 20.4 us -> 9.58 us  [the longest x1 3.08 us: on_device(): from_west = lax.ppermute(east, 'sub', ring)]
    pallas_call x0 -> x6, Pallas kernels: none -> 10.1 us  [the longest x1 2.61 us: on_device(): pl.pallas_call(surface_kernel, out_shape=(jax.ShapeDtypeStruct(tracer.sha...]
    ppermute x10 -> x6, waiting for transfers between devices: 3.44 us -> 12.6 us  [the longest x2 6.09 us: on_device(): lax.ppermute(messages, 'sub', [(i, i ^ size) for i in range(sub_count)])]
  transfers between devices with their start and end apart: 10 -> 6, of which waited for: 2 -> 6; matrix products, arithmetic and copies ran while one was open for 2% -> 0% of each run, Pallas kernels for 0% -> 5%
where the time goes in v1:
time: 40.3 us; the launch traced here: 40 us
  waiting for transfers between devices  12.6 us (31%)
  Pallas kernels  10.1 us (25%)
  starting transfers between devices  9.58 us (24%)
  local copies, waits for them, and re-layouts  6.31 us (16%)
  between operations  0.73 us (2%)
  other arithmetic  0.69 us (2%)
    unnamed x30, local copies, waits for them, and re-layouts  6.31 us
    ppermute x2, waiting for transfers between devices, on_device(): lax.ppermute(messages, 'sub', [(i, i ^ size) for i in range(sub_count)])  6.09 us
    ppermute x2, waiting for transfers between devices, on_device(): lax.ppermute(block, 'lev', [(i, i ^ size) for i in range(lev_count)])  4.67 us
    ppermute x1, starting transfers between devices, on_device(): from_west = lax.ppermute(east, 'sub', ring)  3.08 us
    ppermute x2, starting transfers between devices, on_device(): lax.ppermute(messages, 'sub', [(i, i ^ size) for i in range(sub_count)])  2.81 us
    pallas_call x1, Pallas kernels, on_device(): pl.pallas_call(surface_kernel, out_shape=(jax.ShapeDtypeStruct(tracer.sha...  2.61 us
    ppermute x1, starting transfers between devices, on_device(): from_east = lax.ppermute(west, 'sub', [(b, a) for a, b in ring])  2.09 us
    pallas_call x1, Pallas kernels, on_device(): pl.pallas_call(local_kernel, out_shape=(in_vmem(N_BLOCK, rows, width), le...  1.89 us
  transfers between devices with their start and end apart: 6, of which 6 were waited for; matrix products, arithmetic and copies ran while one was open for 0% of the time, Pallas kernels for 5%

profile of v1, /device:TPU:0, one launch (start us, length us, event | category | flops | bytes accessed | tf_op | source)
XLA Modules:
  0.0 40.0 jit_solution(15029250090953647604)
XLA Ops:
  0.6 1.2 %pack.1 = (f32[32,128]{1,0:T(8,128)S(1)}, f32[32,128]{1,0:T(8,128)S(1)}) custom-call(f32[12,32,128]{2,1,0:T(8,128)} %tracer_ref.3, f32[12,32,128]{2,1,0:T(8,128)} %zonal_ref.5), custom_call_target="tpu_custom_call" | custom-call | tf_op jit(solution)/shard_map/pack/pallas_call | solution.py:332
  1.9 3.1 %collective-permute-start = (f32[32,128]{1,0:T(8,128)S(1)}, f32[32,128]{1,0:T(8,128)S(1)}, u32[]{:S(2)}, u32[]{:S(2)}) collective-permute-start(f32[32,128]{1,0:T(8,128)S(1)} %get-tuple-element.19), channel_id=1, source_target_pairs={{0,4},{4,8},{8,12},{12,0},{1,5},{5,9},{9,13},{13,1},{2,6},{6,10},{... | collective-permute-start | bytes 49160 | tf_op jit(solution)/shard_map/ppermute | solution.py:336
  4.9 2.1 %collective-permute-start.1 = (f32[32,128]{1,0:T(8,128)S(1)}, f32[32,128]{1,0:T(8,128)S(1)}, u32[]{:S(2)}, u32[]{:S(2)}) collective-permute-start(f32[32,128]{1,0:T(8,128)S(1)} %get-tuple-element.20), channel_id=1, source_target_pairs={{4,0},{8,4},{12,8},{0,12},{5,1},{9,5},{13,9},{1,13},{6,2},{10,6},{... | collective-permute-start | bytes 49160 | tf_op jit(solution)/shard_map/ppermute | solution.py:337
  7.0 1.8 %collective-permute-done.from_west_ref = f32[32,128]{1,0:T(8,128)S(1)} collective-permute-done((f32[32,128]{1,0:T(8,128)S(1)}, f32[32,128]{1,0:T(8,128)S(1)}, u32[]{:S(2)}, u32[]{:S(2)}) %collective-permute-start) | collective-permute-done | bytes 16416 | tf_op jit(solution)/shard_map/ppermute | solution.py:336
  8.8 0.0 copy-start.13
  8.8 0.1 collective-permute-done.1.from_east_ref
  8.9 0.5 %copy-done.13 = f32[32,128]{1,0:T(8,128)} copy-done((f32[32,128]{1,0:T(8,128)}, f32[32,128]{1,0:T(8,128)S(1)}, u32[]{:S(2)}) %copy-start.13) | copy-done | bytes 16408
  9.4 0.0 copy-start.14
  9.4 0.6 %copy-done.14 = f32[32,128]{1,0:T(8,128)} copy-done((f32[32,128]{1,0:T(8,128)}, f32[32,128]{1,0:T(8,128)S(1)}, u32[]{:S(2)}) %copy-start.14) | copy-done | bytes 16408
  10.0 1.9 %local.1 = (f32[12,32,128]{2,1,0:T(8,128)S(1)}, f32[12,32,128]{2,1,0:T(8,128)S(1)}, f32[12,32,128]{2,1,0:T(8,128)S(1)}, f32[12,32,128]{2,1,0:T(8,128)S(1)}, f32[...) custom-call(f32[48]{0:T(128)} %thick_ref.5, s32[32,128]{1,0:T(8,128)} %wet_ref.5, ...), custom_call_target="tpu_custom_call" | custom-call | tf_op jit(solution)/shard_map/local/pallas_call | solution.py:339
  11.9 0.0 copy-start.3
  11.9 0.7 %copy-done.3 = f32[12,32,128]{2,1,0:T(8,128)} copy-done((f32[12,32,128]{2,1,0:T(8,128)}, f32[12,32,128]{2,1,0:T(8,128)S(1)}, u32[]{:S(2)}) %copy-start.3) | copy-done | bytes 196632
  12.6 0.0 copy-start.4
  12.6 0.7 %copy-done.4 = f32[12,32,128]{2,1,0:T(8,128)} copy-done((f32[12,32,128]{2,1,0:T(8,128)}, f32[12,32,128]{2,1,0:T(8,128)S(1)}, u32[]{:S(2)}) %copy-start.4) | copy-done | bytes 196632
  13.3 0.0 copy-start.5
  13.3 0.7 %copy-done.5 = f32[12,32,128]{2,1,0:T(8,128)} copy-done((f32[12,32,128]{2,1,0:T(8,128)}, f32[12,32,128]{2,1,0:T(8,128)S(1)}, u32[]{:S(2)}) %copy-start.5) | copy-done | bytes 196632
  13.9 0.0 copy-start.10
  13.9 0.6 %copy-done.10 = f32[32,128]{1,0:T(8,128)} copy-done((f32[32,128]{1,0:T(8,128)}, f32[32,128]{1,0:T(8,128)S(1)}, u32[]{:S(2)}) %copy-start.10) | copy-done | bytes 16408
  14.5 0.0 copy-start.2
  14.5 0.0 copy-start
  14.5 0.0 copy-start.1
  14.5 0.0 collective-permute-start.2
  14.5 1.4 %collective-permute-done.2.other_ref = f32[12,32,128]{2,1,0:T(8,128)S(1)} collective-permute-done((f32[12,32,128]{2,1,0:T(8,128)S(1)}, f32[12,32,128]{2,1,0:T(8,128)S(1)}, u32[]{:S(2)}, u32[]{:S(2)}) %collective-permute-start.2) | collective-permute-done | bytes 196640 | tf_op jit(solution)/shard_map/ppermute | solution.py:357
  16.0 0.0 copy-done.2
  16.0 0.0 copy-start.11
  16.0 0.7 %copy-done.11 = f32[12,32,128]{2,1,0:T(8,128)} copy-done((f32[12,32,128]{2,1,0:T(8,128)}, f32[12,32,128]{2,1,0:T(8,128)S(1)}, u32[]{:S(2)}) %copy-start.11) | copy-done | bytes 196632
  16.7 1.1 %merge.1 = (f32[6,32,128]{2,1,0:T(8,128)S(1)}, f32[4,32,128]{2,1,0:T(8,128)S(1)}) custom-call(f32[48]{0:T(128)} %thick_ref.5, s32[32,128]{1,0:T(8,128)} %wet_ref.5, f32[12,32,128]{2,1,0:T(8,128)} %copy-done.2, f32[12,32,128]{2,1,0:T(8,128)} %copy-done.11), custom_call_target="tpu_custom_call" | custom-call | tf_op jit(solution)/shard_map/merge/pallas_call | solution.py:361
  17.8 0.0 copy-done
  17.8 0.0 copy-done.1
  17.8 0.0 copy-start.8
  17.8 0.6 %copy-done.8 = f32[4,32,128]{2,1,0:T(8,128)} copy-done((f32[4,32,128]{2,1,0:T(8,128)}, f32[4,32,128]{2,1,0:T(8,128)S(1)}, u32[]{:S(2)}) %copy-start.8) | copy-done | bytes 65560
  18.4 0.0 copy-start.7
  18.4 1.6 %collective-permute-start.3 = (f32[6,32,128]{2,1,0:T(8,128)S(1)}, f32[6,32,128]{2,1,0:T(8,128)S(1)}, u32[]{:S(2)}, u32[]{:S(2)}) collective-permute-start(f32[6,32,128]{2,1,0:T(8,128)S(1)} %get-tuple-element.25.mine_ref), channel_id=1, source_target_pairs={{0,2},{1,3},{2,0},{3,1},{4,6},{5,7},{6,4},{7,5},{8,10},{9,11},{10,... | collective-permute-start | bytes 294920 | tf_op jit(solution)/shard_map/ppermute | solution.py:357
  20.0 3.2 %collective-permute-done.3.other_ref = f32[6,32,128]{2,1,0:T(8,128)S(1)} collective-permute-done((f32[6,32,128]{2,1,0:T(8,128)S(1)}, f32[6,32,128]{2,1,0:T(8,128)S(1)}, u32[]{:S(2)}, u32[]{:S(2)}) %collective-permute-start.3) | collective-permute-done | bytes 98336 | tf_op jit(solution)/shard_map/ppermute | solution.py:357
  23.2 0.0 copy-start.12
  23.3 0.0 copy-done.7
  23.3 0.6 %copy-done.12 = f32[6,32,128]{2,1,0:T(8,128)} copy-done((f32[6,32,128]{2,1,0:T(8,128)}, f32[6,32,128]{2,1,0:T(8,128)S(1)}, u32[]{:S(2)}) %copy-start.12) | copy-done | bytes 98328
  23.9 1.5 %final.1 = (f32[3,32,128]{2,1,0:T(8,128)S(1)}, f32[4,32,128]{2,1,0:T(8,128)S(1)}, f32[12,32,128]{2,1,0:T(8,128)S(1)}) custom-call(f32[48]{0:T(128)} %thick_ref.5, s32[32,128]{1,0:T(8,128)} %wet_ref.5, f32[6,32,128]{2,1,0:T(8,128)} %copy-done.7, f32[6,32,128]{2,1,0:T(8,128)} %copy-done.12, f32[12,32,128]{2,1,0:T(8,128)} %copy-done.3, f32[12,32,128]{2,1,0:T(8,128)} %copy-done, ...), custom_call_target="tpu_custom_call" | custom-call | tf_op jit(solution)/shard_map/final/pallas_call | solution.py:370
  25.4 0.0 copy-start.9
  25.4 0.6 %copy-done.9 = f32[4,32,128]{2,1,0:T(8,128)} copy-done((f32[4,32,128]{2,1,0:T(8,128)}, f32[4,32,128]{2,1,0:T(8,128)S(1)}, u32[]{:S(2)}) %copy-start.9) | copy-done | bytes 65560
  26.0 0.0 copy-start.6
  26.0 0.9 %collective-permute-start.4 = (f32[1,3,32,128]{3,2,1,0:T(8,128)S(1)}, f32[1,3,32,128]{3,2,1,0:T(8,128)S(1)}, u32[]{:S(2)}, u32[]{:S(2)}) collective-permute-start(f32[1,3,32,128]{3,2,1,0:T(8,128)S(1)} %bitcast.1), channel_id=1, source_target_pairs={{0,4},{4,0},{8,12},{12,8},{1,5},{5,1},{9,13},{13,9},{2,6},{6,2},{1... | collective-permute-start | bytes 147464 | tf_op jit(solution)/shard_map/ppermute | solution.py:381
  26.8 3.2 %collective-permute-done.4 = f32[1,3,32,128]{3,2,1,0:T(8,128)S(1)} collective-permute-done((f32[1,3,32,128]{3,2,1,0:T(8,128)S(1)}, f32[1,3,32,128]{3,2,1,0:T(8,128)S(1)}, u32[]{:S(2)}, u32[]{:S(2)}) %collective-permute-start.4) | collective-permute-done | bytes 49184 | tf_op jit(solution)/shard_map/ppermute | solution.py:381
  30.1 1.9 %collective-permute-start.5 = (f32[2,3,32,128]{3,2,1,0:T(8,128)S(1)}, f32[2,3,32,128]{3,2,1,0:T(8,128)S(1)}, u32[]{:S(2)}, u32[]{:S(2)}) collective-permute-start(f32[2,3,32,128]{3,2,1,0:T(8,128)S(1)} %pad_maximum_fusion.1), channel_id=1, source_target_pairs={{0,8},{4,12},{8,0},{12,4},{1,9},{5,13},{9,1},{13,5},{2,10},{6,14},... | collective-permute-start | bytes 294920 | tf_op jit(solution)/shard_map/ppermute | solution.py:381
  32.0 1.8 %forward.1 = f32[12,32,128]{2,1,0:T(8,128)} custom-call(f32[12,32,128]{2,1,0:T(8,128)} %copy-done.5, f32[12,32,128]{2,1,0:T(8,128)} %copy-done, f32[12,32,128]{2,1,0:T(8,128)} %copy-done.1, f32[4,32,128]{2,1,0:T(8,128)} %copy-done.9), custom_call_target="tpu_custom_call" | custom-call | tf_op jit(solution)/shard_map/forward/pallas_call | solution.py:385
  33.9 0.0 copy-done.6
  33.9 2.9 %collective-permute-done.5 = f32[2,3,32,128]{3,2,1,0:T(8,128)S(1)} collective-permute-done((f32[2,3,32,128]{3,2,1,0:T(8,128)S(1)}, f32[2,3,32,128]{3,2,1,0:T(8,128)S(1)}, u32[]{:S(2)}, u32[]{:S(2)}) %collective-permute-start.5) | collective-permute-done | bytes 98336 | tf_op jit(solution)/shard_map/ppermute | solution.py:381
  36.7 0.7 %pad_maximum_fusion.messages_ref = f32[4,3,32,128]{3,2,1,0:T(8,128)} fusion(f32[2,3,32,128]{3,2,1,0:T(8,128)S(1)} %collective-permute-done.5, f32[1,3,32,128]{3,2,1,0:T(8,128)S(1)} %collective-permute-done.4, f32[1,3,32,128]{3,2,1,0:T(8,128)S(1)} %bitcast.3), kind=kLoop, calls=%fused_computation | loop fusion | flops 98304 | bytes 393216 | tf_op jit(solution)/shard_map/concatenate | solution.py:382
  37.4 2.6 %surface.1 = (f32[12,32,128]{2,1,0:T(8,128)}, f32[32,128]{1,0:T(8,128)}) custom-call(f32[12,32,128]{2,1,0:T(8,128)} %copy-done.6, f32[12,32,128]{2,1,0:T(8,128)} %zonal_ref.5, f32[12,32,128]{2,1,0:T(8,128)} %merid_ref.3, f32[12,32,128]{2,1,0:T(8,128)} %copy-done.4, f32[4,3,32,128]{3,2,1,0:T(8,128)} %pad_maximum_fusion.messages_ref), custom_call_target="tpu_custom_call" | custom-call | tf_op jit(solution)/shard_map/surface/pallas_call | solution.py:393
  (1 shorter events, 0.0 us)
Async XLA Ops:
  1.9 6.9 %collective-permute-start = (f32[32,128]{1,0:T(8,128)S(1)}, f32[32,128]{1,0:T(8,128)S(1)}, u32[]{:S(2)}, u32[]{:S(2)}) collective-permute-start(f32[32,128]{1,0:T(8,128)S(1)} %get-tuple-element.19), channel_id=1, source_target_pairs={{0,4},{4,8},{8,12},{12,0},{1,5},{5,9},{9,13},{13,1},{2,6},{6,10},{... | collective-permute-start | bytes 49160 | tf_op jit(solution)/shard_map/ppermute | solution.py:336
  4.9 3.9 %collective-permute-start.1 = (f32[32,128]{1,0:T(8,128)S(1)}, f32[32,128]{1,0:T(8,128)S(1)}, u32[]{:S(2)}, u32[]{:S(2)}) collective-permute-start(f32[32,128]{1,0:T(8,128)S(1)} %get-tuple-element.20), channel_id=1, source_target_pairs={{4,0},{8,4},{12,8},{0,12},{5,1},{9,5},{13,9},{1,13},{6,2},{10,6},{... | collective-permute-start | bytes 49160 | tf_op jit(solution)/shard_map/ppermute | solution.py:337
  8.8 0.6 %copy-start.13 = (f32[32,128]{1,0:T(8,128)}, f32[32,128]{1,0:T(8,128)S(1)}, u32[]{:S(2)}) copy-start(f32[32,128]{1,0:T(8,128)S(1)} %collective-permute-done.from_west_ref) | copy-start | bytes 49156
  9.4 0.6 %copy-start.14 = (f32[32,128]{1,0:T(8,128)}, f32[32,128]{1,0:T(8,128)S(1)}, u32[]{:S(2)}) copy-start(f32[32,128]{1,0:T(8,128)S(1)} %collective-permute-done.1.from_east_ref) | copy-start | bytes 49156
  11.9 0.7 %copy-start.3 = (f32[12,32,128]{2,1,0:T(8,128)}, f32[12,32,128]{2,1,0:T(8,128)S(1)}, u32[]{:S(2)}) copy-start(f32[12,32,128]{2,1,0:T(8,128)S(1)} %get-tuple-element.26.adjoint_ref) | copy-start | bytes 589828
  12.6 0.7 %copy-start.4 = (f32[12,32,128]{2,1,0:T(8,128)}, f32[12,32,128]{2,1,0:T(8,128)S(1)}, u32[]{:S(2)}) copy-start(f32[12,32,128]{2,1,0:T(8,128)S(1)} %get-tuple-element.31.u_next_ref) | copy-start | bytes 589828
  13.3 0.7 %copy-start.5 = (f32[12,32,128]{2,1,0:T(8,128)}, f32[12,32,128]{2,1,0:T(8,128)S(1)}, u32[]{:S(2)}) copy-start(f32[12,32,128]{2,1,0:T(8,128)S(1)} %get-tuple-element.21.forward_ref) | copy-start | bytes 589828
  13.9 0.6 %copy-start.10 = (f32[32,128]{1,0:T(8,128)}, f32[32,128]{1,0:T(8,128)S(1)}, u32[]{:S(2)}) copy-start(f32[32,128]{1,0:T(8,128)S(1)} %get-tuple-element.27.damping_ref) | copy-start | bytes 49156
  14.5 1.5 %copy-start.2 = (f32[12,32,128]{2,1,0:T(8,128)}, f32[12,32,128]{2,1,0:T(8,128)S(1)}, u32[]{:S(2)}) copy-start(f32[12,32,128]{2,1,0:T(8,128)S(1)} %get-tuple-element.24.mine_ref) | copy-start | bytes 589828
  14.5 3.2 %copy-start = (f32[12,32,128]{2,1,0:T(8,128)}, f32[12,32,128]{2,1,0:T(8,128)S(1)}, u32[]{:S(2)}) copy-start(f32[12,32,128]{2,1,0:T(8,128)S(1)} %get-tuple-element.22.top_ref) | copy-start | bytes 589828
  14.5 3.2 %copy-start.1 = (f32[12,32,128]{2,1,0:T(8,128)}, f32[12,32,128]{2,1,0:T(8,128)S(1)}, u32[]{:S(2)}) copy-start(f32[12,32,128]{2,1,0:T(8,128)S(1)} %get-tuple-element.23.bottom_ref) | copy-start | bytes 589828
  14.5 1.4 %collective-permute-start.2 = (f32[12,32,128]{2,1,0:T(8,128)S(1)}, f32[12,32,128]{2,1,0:T(8,128)S(1)}, u32[]{:S(2)}, u32[]{:S(2)}) collective-permute-start(f32[12,32,128]{2,1,0:T(8,128)S(1)} %get-tuple-element.24.mine_ref), channel_id=1, source_target_pairs={{0,1},{1,0},{2,3},{3,2},{4,5},{5,4},{6,7},{7,6},{8,9},{9,8},{10,11... | collective-permute-start | bytes 589832 | tf_op jit(solution)/shard_map/ppermute | solution.py:357
  16.0 0.7 %copy-start.11 = (f32[12,32,128]{2,1,0:T(8,128)}, f32[12,32,128]{2,1,0:T(8,128)S(1)}, u32[]{:S(2)}) copy-start(f32[12,32,128]{2,1,0:T(8,128)S(1)} %collective-permute-done.2.other_ref) | copy-start | bytes 589828
  17.8 0.6 %copy-start.8 = (f32[4,32,128]{2,1,0:T(8,128)}, f32[4,32,128]{2,1,0:T(8,128)S(1)}, u32[]{:S(2)}) copy-start(f32[4,32,128]{2,1,0:T(8,128)S(1)} %get-tuple-element.28.rest_0_) | copy-start | bytes 196612
  18.4 4.8 %copy-start.7 = (f32[6,32,128]{2,1,0:T(8,128)}, f32[6,32,128]{2,1,0:T(8,128)S(1)}, u32[]{:S(2)}) copy-start(f32[6,32,128]{2,1,0:T(8,128)S(1)} %get-tuple-element.25.mine_ref) | copy-start | bytes 294916
  18.4 4.8 %collective-permute-start.3 = (f32[6,32,128]{2,1,0:T(8,128)S(1)}, f32[6,32,128]{2,1,0:T(8,128)S(1)}, u32[]{:S(2)}, u32[]{:S(2)}) collective-permute-start(f32[6,32,128]{2,1,0:T(8,128)S(1)} %get-tuple-element.25.mine_ref), channel_id=1, source_target_pairs={{0,2},{1,3},{2,0},{3,1},{4,6},{5,7},{6,4},{7,5},{8,10},{9,11},{10,... | collective-permute-start | bytes 294920 | tf_op jit(solution)/shard_map/ppermute | solution.py:357
  23.2 0.6 %copy-start.12 = (f32[6,32,128]{2,1,0:T(8,128)}, f32[6,32,128]{2,1,0:T(8,128)S(1)}, u32[]{:S(2)}) copy-start(f32[6,32,128]{2,1,0:T(8,128)S(1)} %collective-permute-done.3.other_ref) | copy-start | bytes 294916
  25.4 0.6 %copy-start.9 = (f32[4,32,128]{2,1,0:T(8,128)}, f32[4,32,128]{2,1,0:T(8,128)S(1)}, u32[]{:S(2)}) copy-start(f32[4,32,128]{2,1,0:T(8,128)S(1)} %get-tuple-element.29.ends_ref) | copy-start | bytes 196612
  26.0 7.9 %copy-start.6 = (f32[12,32,128]{2,1,0:T(8,128)}, f32[12,32,128]{2,1,0:T(8,128)S(1)}, u32[]{:S(2)}) copy-start(f32[12,32,128]{2,1,0:T(8,128)S(1)} %get-tuple-element.30.pulled_ref) | copy-start | bytes 589828
  26.0 4.1 %collective-permute-start.4 = (f32[1,3,32,128]{3,2,1,0:T(8,128)S(1)}, f32[1,3,32,128]{3,2,1,0:T(8,128)S(1)}, u32[]{:S(2)}, u32[]{:S(2)}) collective-permute-start(f32[1,3,32,128]{3,2,1,0:T(8,128)S(1)} %bitcast.1), channel_id=1, source_target_pairs={{0,4},{4,0},{8,12},{12,8},{1,5},{5,1},{9,13},{13,9},{2,6},{6,2},{1... | collective-permute-start | bytes 147464 | tf_op jit(solution)/shard_map/ppermute | solution.py:381
  30.1 6.6 %collective-permute-start.5 = (f32[2,3,32,128]{3,2,1,0:T(8,128)S(1)}, f32[2,3,32,128]{3,2,1,0:T(8,128)S(1)}, u32[]{:S(2)}, u32[]{:S(2)}) collective-permute-start(f32[2,3,32,128]{3,2,1,0:T(8,128)S(1)} %pad_maximum_fusion.1), channel_id=1, source_target_pairs={{0,8},{4,12},{8,0},{12,4},{1,9},{5,13},{9,1},{13,5},{2,10},{6,14},... | collective-permute-start | bytes 294920 | tf_op jit(solution)/shard_map/ppermute | solution.py:381

commit v2 on v1

--- a/solution.py
+++ b/solution.py
@@ -23,6 +23,10 @@
     return pltpu.VMEM(shape, jnp.float32)
 
 
+def near(*arrays):
+    return [pltpu.with_memory_space_constraint(array, pltpu.VMEM) for array in arrays]
+
+
 def lanes(rows, width):
     return lax.broadcasted_iota(jnp.int32, (rows, width), 1)
 
@@ -43,18 +47,47 @@
     return jnp.where(wet, MIX_RATE * rate, 0.0)
 
 
-def pack_kernel(tracer_ref, zonal_ref, east_ref, west_ref):
+def fold(field):
+    rows, width = field.shape
+    groups = rows // 8
+    slot = width // groups
+    lane = lanes(8, width)
+    folded = field[:8]
+    for group in range(1, groups):
+        folded = jnp.where(lane // slot == group, turn(field[8 * group : 8 * group + 8], slot * group, 1), folded)
+    return folded
+
+
+def unfold(folded, rows):
+    width = folded.shape[1]
+    groups = rows // 8
+    return jnp.concatenate([turn(folded, -(width // groups) * group, 1) for group in range(groups)])
+
+
+def pack_kernel(tracer_hbm, zonal_hbm, wet_hbm, tracer_ref, zonal_ref, wet_ref, east_ref, west_ref, sems):
     own, rows, width = tracer_ref.shape
+    copies = [
+        pltpu.make_async_copy(source, target, sems.at[i])
+        for i, (source, target) in enumerate(
+            ((tracer_hbm, tracer_ref), (zonal_hbm, zonal_ref), (wet_hbm, wet_ref))
+        )
+    ]
+    for copy in copies:
+        copy.start()
     lane = lanes(rows, width)
     east = jnp.zeros((rows, width), jnp.float32)
     west = jnp.zeros((rows, width), jnp.float32)
+    copies[0].wait()
     for k in range(own):
         values = tracer_ref[k]
         east = jnp.where(lane == k, turn(values, k + 1, 1), east)
         west = jnp.where(lane == k, turn(values, k, 1), west)
+    east_ref[...] = fold(east)
+    copies[1].wait()
+    for k in range(own):
         west = jnp.where(lane == own + k, turn(zonal_ref[k], own + k, 1), west)
-    east_ref[...] = east
-    west_ref[...] = west
+    west_ref[...] = fold(west)
+    copies[2].wait()
 
 
 def local_kernel(
@@ -66,8 +99,8 @@
     first = lax.axis_index("lev") * own
     lane = lanes(rows, width)
     wet_levels = wet_ref[...]
-    from_west = from_west_ref[...]
-    from_east = from_east_ref[...]
+    from_west = unfold(from_west_ref[...], rows)
+    from_east = unfold(from_east_ref[...], rows)
     forward = []
     for k in range(own):
         values = tracer_ref[k]
@@ -242,9 +275,9 @@
         pulled_ref[k] = pulled
         edges = jnp.where(lane == k, turn(pulled, k, 1), edges)
         edges = jnp.where(lane == own + k, turn(pulled, own + k + 1, 1), edges)
-    message_ref[0] = source
-    message_ref[1] = edges
-    message_ref[2] = damping_ref[...]
+    message_ref[:rows] = source
+    message_ref[rows : rows + 8] = fold(edges)
+    message_ref[rows + 8 :] = damping_ref[...]
 
 
 def forward_kernel(forward_ref, top_ref, bottom_ref, ends_ref, out_ref):
@@ -268,14 +301,14 @@
     count = messages_ref.shape[0]
     place = lax.axis_index("sub")
     lane = lanes(rows, width)
-    west_edges = jnp.zeros((rows, width), jnp.float32)
-    east_edges = jnp.zeros((rows, width), jnp.float32)
     for i in range(count):
         owner = jnp.bitwise_xor(place, i)
-        source_scr[owner] = messages_ref[i, 0]
-        damping_scr[owner] = messages_ref[i, 2]
-    west_edges = messages_ref[jnp.bitwise_xor(place, lax.rem(place + count - 1, count)), 1]
-    east_edges = messages_ref[jnp.bitwise_xor(place, lax.rem(place + 1, count)), 1]
+        source_scr[owner] = messages_ref[i, :rows]
+        damping_scr[owner] = messages_ref[i, rows + 8 :]
+    west_of = jnp.bitwise_xor(place, lax.rem(place + count - 1, count))
+    east_of = jnp.bitwise_xor(place, lax.rem(place + 1, count))
+    west_edges = unfold(messages_ref[west_of, rows : rows + 8], rows)
+    east_edges = unfold(messages_ref[east_of, rows : rows + 8], rows)
     for k in range(own):
         pulled = pulled_ref[k]
         merid = merid_ref[k]
@@ -327,11 +360,17 @@
     lev_count = lax.axis_size("lev")
     sub_count = lax.axis_size("sub")
     edge = in_vmem(rows, width)
+    thickness = pltpu.with_memory_space_constraint(thickness, pltpu.SMEM)
     levels = in_vmem(own, rows, width)
 
-    east, west = pl.pallas_call(
-        pack_kernel, out_shape=(edge, edge), in_specs=[VMEM_IN] * 2, out_specs=(VMEM_IN,) * 2, name="pack"
-    )(tracer, zonal_flow)
+    tracer, zonal_flow, wet_levels, east, west = pl.pallas_call(
+        pack_kernel,
+        out_shape=(levels, levels, pltpu.VMEM((rows, width), jnp.int32), in_vmem(8, width), in_vmem(8, width)),
+        in_specs=[pl.BlockSpec(memory_space=pl.ANY)] * 3,
+        out_specs=(VMEM_IN,) * 5,
+        scratch_shapes=[pltpu.SemaphoreType.DMA((3,))],
+        name="pack",
+    )(tracer, zonal_flow, wet_levels)
     ring = [(i, (i + 1) % sub_count) for i in range(sub_count)]
     from_west = lax.ppermute(east, "sub", ring)
     from_east = lax.ppermute(west, "sub", [(b, a) for a, b in ring])
@@ -342,7 +381,7 @@
         in_specs=[SMEM_IN] + [VMEM_IN] * 7,
         out_specs=(VMEM_IN,) * 7,
         name="local",
-    )(thickness, wet_levels, tracer, zonal_flow, meridional_flow, cotangent, from_west, from_east)
+    )(thickness, *near(wet_levels, tracer, zonal_flow, meridional_flow, cotangent, from_west, from_east))
 
     sizes = [1]
     while sizes[-1] * 2 < lev_count:
@@ -352,7 +391,7 @@
         block = pl.pallas_call(
             functools.partial(pick_kernel, 1), out_shape=in_vmem(N_LAST, rows, width),
             in_specs=[VMEM_IN], out_specs=VMEM_IN, name="pick",
-        )(block)
+        )(*near(block))
     for size in sizes:
         other = lax.ppermute(block, "lev", [(i, i ^ size) for i in range(lev_count)])
         if size == sizes[-1]:
@@ -364,16 +403,16 @@
             in_specs=[SMEM_IN] + [VMEM_IN] * 3,
             out_specs=(VMEM_IN,) * 2,
             name="merge",
-        )(thickness, wet_levels, block, other)
+        )(thickness, *near(wet_levels, block, other))
         fluxes.append(flux)
 
     message, ends, pulled = pl.pallas_call(
         functools.partial(final_kernel, sizes, own),
-        out_shape=(in_vmem(3, rows, width), in_vmem(4, rows, width), levels),
+        out_shape=(in_vmem(2 * rows + 8, width), in_vmem(4, rows, width), levels),
         in_specs=[SMEM_IN] + [VMEM_IN] * (7 + len(fluxes)),
         out_specs=(VMEM_IN,) * 3,
         name="final",
-    )(thickness, wet_levels, block, other, adjoint, top, bottom, damping, *fluxes)
+    )(thickness, *near(wet_levels, block, other, adjoint, top, bottom, damping, *fluxes))
 
     messages = message[None]
     size = 1
@@ -388,7 +427,7 @@
         in_specs=[VMEM_IN] * 4,
         out_specs=VMEM_IN,
         name="forward",
-    )(forward, top, bottom, ends)
+    )(*near(forward, top, bottom, ends))
 
     tracer_adjoint, surface = pl.pallas_call(
         surface_kernel,
@@ -400,7 +439,7 @@
         out_specs=(VMEM_IN,) * 2,
         scratch_shapes=[pltpu.VMEM((sub_count, rows, width), jnp.float32)] * 2,
         name="surface",
-    )(pulled, zonal_flow, meridional_flow, u_next, messages)
+    )(*near(pulled, zonal_flow, meridional_flow, u_next, messages))
     return (next_tracer, tracer_adjoint, surface)
 
 

time: 40.3 us -> 29 us (0.72)
  local copies, waits for them, and re-layouts: 6.31 us -> 0.01 us
  Pallas kernels: 10.1 us -> 6.43 us
  waiting for transfers between devices: 12.6 us -> 10.6 us
  starting transfers between devices: 9.58 us -> 11.1 us
  other arithmetic: 0.69 us -> 0.02 us
    unnamed x30 -> x4, local copies, waits for them, and re-layouts: 6.31 us -> 0.01 us
    ppermute x2, waiting for transfers between devices: 6.09 us -> 4.45 us  [on_device(): lax.ppermute(messages, 'sub', [(i, i ^ size) for i in range(sub_count)])]
    ppermute x2, starting transfers between devices: 2.81 us -> 4.08 us  [on_device(): lax.ppermute(messages, 'sub', [(i, i ^ size) for i in range(sub_count)])]
    pallas_call x1, Pallas kernels: 2.61 us -> 1.34 us  [on_device(): pl.pallas_call(surface_kernel, out_shape=(jax.ShapeDtypeStruct(tracer.sha...]
    pallas_call x1, Pallas kernels: 1.83 us -> 0.71 us  [on_device(): pl.pallas_call(forward_kernel, out_shape=jax.ShapeDtypeStruct(tracer.shap...]
    concatenate x2, other arithmetic: 0.69 us -> 0.02 us  [on_device(): messages = jnp.concatenate([messages, got])]
    pallas_call x1, Pallas kernels: 1.89 us -> 1.33 us  [on_device(): pl.pallas_call(local_kernel, out_shape=(in_vmem(N_BLOCK, rows, width), le...]
    pallas_call x1, Pallas kernels: 1.47 us -> 0.94 us  [on_device(): pl.pallas_call(functools.partial(final_kernel, sizes, own), out_shape=(in...]
  transfers between devices with their start and end apart: 6 -> 6, of which waited for: 6 -> 5; matrix products, arithmetic and copies ran while one was open for 0% -> 0% of each run, Pallas kernels for 5% -> 2%
where the time goes in v2:
time: 29 us; the launch traced here: 28.8 us
  starting transfers between devices  11.1 us (38%)
  waiting for transfers between devices  10.6 us (37%)
  Pallas kernels  6.43 us (22%)
  between operations  0.69 us (2%)
    ppermute x2, waiting for transfers between devices, on_device(): lax.ppermute(block, 'lev', [(i, i ^ size) for i in range(lev_count)])  4.6 us
    ppermute x2, waiting for transfers between devices, on_device(): lax.ppermute(messages, 'sub', [(i, i ^ size) for i in range(sub_count)])  4.45 us
    ppermute x2, starting transfers between devices, on_device(): lax.ppermute(messages, 'sub', [(i, i ^ size) for i in range(sub_count)])  4.08 us
    ppermute x1, starting transfers between devices, on_device(): from_west = lax.ppermute(east, 'sub', ring)  3.08 us
    ppermute x1, starting transfers between devices, on_device(): from_east = lax.ppermute(west, 'sub', [(b, a) for a, b in ring])  2.09 us
    ppermute x2, starting transfers between devices, on_device(): lax.ppermute(block, 'lev', [(i, i ^ size) for i in range(lev_count)])  1.8 us
    ppermute x1, waiting for transfers between devices, on_device(): from_west = lax.ppermute(east, 'sub', ring)  1.56 us
    pallas_call x1, Pallas kernels, on_device(): pl.pallas_call(pack_kernel, out_shape=(levels, levels, pltpu.VMEM((rows,...  1.38 us
  transfers between devices with their start and end apart: 6, of which 5 were waited for; matrix products, arithmetic and copies ran while one was open for 0% of the time, Pallas kernels for 2%

profile of v2, /device:TPU:0, one launch (start us, length us, event | category | flops | bytes accessed | tf_op | source)
XLA Modules:
  0.0 28.8 jit_solution(8502764631674393181)
XLA Ops:
  0.6 0.0 copy-start
  0.6 0.0 copy-start.1
  0.7 1.4 %pack.1 = (f32[12,32,128]{2,1,0:T(8,128)S(1)}, f32[12,32,128]{2,1,0:T(8,128)S(1)}, s32[32,128]{1,0:T(8,128)S(1)}, f32[8,128]{1,0:T(8,128)S(1)}, f32[8,128]{1,0:T(8,128)S(1)}) custom-call(f32[12,32,128]{2,1,0:T(8,128)} %tracer_hbm.1, f32[12,32,128]{2,1,0:T(8,128)} %zonal_hbm.1, s32[32,128]{1,0:T(8,128)} %wet_hbm.1), custom_call_target="tpu_custom_call" | custom-call | tf_op jit(solution)/shard_map/pack/pallas_call | solution.py:366
  2.0 3.1 %collective-permute-start = (f32[8,128]{1,0:T(8,128)S(1)}, f32[8,128]{1,0:T(8,128)S(1)}, u32[]{:S(2)}, u32[]{:S(2)}) collective-permute-start(f32[8,128]{1,0:T(8,128)S(1)} %get-tuple-element.25), channel_id=1, source_target_pairs={{0,4},{4,8},{8,12},{12,0},{1,5},{5,9},{9,13},{13,1},{2,6},{6,10},{... | collective-permute-start | bytes 12296 | tf_op jit(solution)/shard_map/ppermute | solution.py:375
  5.1 2.1 %collective-permute-start.1 = (f32[8,128]{1,0:T(8,128)S(1)}, f32[8,128]{1,0:T(8,128)S(1)}, u32[]{:S(2)}, u32[]{:S(2)}) collective-permute-start(f32[8,128]{1,0:T(8,128)S(1)} %get-tuple-element.26), channel_id=1, source_target_pairs={{4,0},{8,4},{12,8},{0,12},{5,1},{9,5},{13,9},{1,13},{6,2},{10,6},{... | collective-permute-start | bytes 12296 | tf_op jit(solution)/shard_map/ppermute | solution.py:376
  7.2 1.6 %collective-permute-done.from_west_ref = f32[8,128]{1,0:T(8,128)S(1)} collective-permute-done((f32[8,128]{1,0:T(8,128)S(1)}, f32[8,128]{1,0:T(8,128)S(1)}, u32[]{:S(2)}, u32[]{:S(2)}) %collective-permute-start) | collective-permute-done | bytes 4128 | tf_op jit(solution)/shard_map/ppermute | solution.py:375
  8.8 0.0 collective-permute-done.1.from_east_ref
  8.8 0.0 copy-done
  8.8 0.0 copy-done.1
  8.8 1.3 %local.1 = (f32[12,32,128]{2,1,0:T(8,128)S(1)}, f32[12,32,128]{2,1,0:T(8,128)S(1)}, f32[12,32,128]{2,1,0:T(8,128)S(1)}, f32[12,32,128]{2,1,0:T(8,128)S(1)}, f32[...) custom-call(f32[48]{0:T(128)} %thick_ref.5, s32[32,128]{1,0:T(8,128)S(1)} %get-tuple-element.22.wet_ref, ...), custom_call_target="tpu_custom_call" | custom-call | tf_op jit(solution)/shard_map/local/pallas_call | solution.py:378
  10.1 0.1 collective-permute-start.2
  10.2 1.4 %collective-permute-done.2.other_ref = f32[12,32,128]{2,1,0:T(8,128)S(1)} collective-permute-done((f32[12,32,128]{2,1,0:T(8,128)S(1)}, f32[12,32,128]{2,1,0:T(8,128)S(1)}, u32[]{:S(2)}, u32[]{:S(2)}) %collective-permute-start.2) | collective-permute-done | bytes 196640 | tf_op jit(solution)/shard_map/ppermute | solution.py:396
  11.6 0.7 %merge.1 = (f32[6,32,128]{2,1,0:T(8,128)S(1)}, f32[4,32,128]{2,1,0:T(8,128)S(1)}) custom-call(f32[48]{0:T(128)} %thick_ref.5, s32[32,128]{1,0:T(8,128)S(1)} %get-tuple-element.22.wet_ref, f32[12,32,128]{2,1,0:T(8,128)S(1)} %get-tuple-element.30.mine_ref, f32[12,32,128]{2,1,0:T(8,128)S(1)} %collective-permute-done.2.other_ref), custom_call_target="tpu_custom_call" | custom-call | tf_op jit(solution)/shard_map/merge/pallas_call | solution.py:400
  12.4 1.7 %collective-permute-start.3 = (f32[6,32,128]{2,1,0:T(8,128)S(1)}, f32[6,32,128]{2,1,0:T(8,128)S(1)}, u32[]{:S(2)}, u32[]{:S(2)}) collective-permute-start(f32[6,32,128]{2,1,0:T(8,128)S(1)} %get-tuple-element.31.mine_ref), channel_id=1, source_target_pairs={{0,2},{1,3},{2,0},{3,1},{4,6},{5,7},{6,4},{7,5},{8,10},{9,11},{10,... | collective-permute-start | bytes 294920 | tf_op jit(solution)/shard_map/ppermute | solution.py:396
  14.1 3.2 %collective-permute-done.3.other_ref = f32[6,32,128]{2,1,0:T(8,128)S(1)} collective-permute-done((f32[6,32,128]{2,1,0:T(8,128)S(1)}, f32[6,32,128]{2,1,0:T(8,128)S(1)}, u32[]{:S(2)}, u32[]{:S(2)}) %collective-permute-start.3) | collective-permute-done | bytes 98336 | tf_op jit(solution)/shard_map/ppermute | solution.py:396
  17.3 0.9 %final.1 = (f32[72,128]{1,0:T(8,128)S(1)}, f32[4,32,128]{2,1,0:T(8,128)S(1)}, f32[12,32,128]{2,1,0:T(8,128)S(1)}) custom-call(f32[48]{0:T(128)} %thick_ref.5, s32[32,128]{1,0:T(8,128)S(1)} %get-tuple-element.22.wet_ref, f32[6,32,128]{2,1,0:T(8,128)S(1)} %get-tuple-element.31.mine_ref, f32[6,32,128]{2,1,0:T(8,128)S(1)} %collective-permute-done.3.other_ref, ...), custom_call_target="tpu_custom_call" | custom-call | tf_op jit(solution)/shard_map/final/pallas_call | solution.py:409
  18.2 1.5 %collective-permute-start.4 = (f32[1,72,128]{2,1,0:T(8,128)S(1)}, f32[1,72,128]{2,1,0:T(8,128)S(1)}, u32[]{:S(2)}, u32[]{:S(2)}) collective-permute-start(f32[1,72,128]{2,1,0:T(8,128)S(1)} %bitcast.1), channel_id=1, source_target_pairs={{0,4},{4,0},{8,12},{12,8},{1,5},{5,1},{9,13},{13,9},{2,6},{6,2},{1... | collective-permute-start | bytes 110600 | tf_op jit(solution)/shard_map/ppermute | solution.py:420
  19.7 2.4 %collective-permute-done.4 = f32[1,72,128]{2,1,0:T(8,128)S(1)} collective-permute-done((f32[1,72,128]{2,1,0:T(8,128)S(1)}, f32[1,72,128]{2,1,0:T(8,128)S(1)}, u32[]{:S(2)}, u32[]{:S(2)}) %collective-permute-start.4) | collective-permute-done | bytes 36896 | tf_op jit(solution)/shard_map/ppermute | solution.py:420
  22.2 2.5 %collective-permute-start.5 = (f32[2,72,128]{2,1,0:T(8,128)S(1)}, f32[2,72,128]{2,1,0:T(8,128)S(1)}, u32[]{:S(2)}, u32[]{:S(2)}) collective-permute-start(f32[2,72,128]{2,1,0:T(8,128)S(1)} %pad_maximum_fusion.1), channel_id=1, source_target_pairs={{0,8},{4,12},{8,0},{12,4},{1,9},{5,13},{9,1},{13,5},{2,10},{6,14},... | collective-permute-start | bytes 221192 | tf_op jit(solution)/shard_map/ppermute | solution.py:420
  24.7 0.7 %forward.1 = f32[12,32,128]{2,1,0:T(8,128)} custom-call(f32[12,32,128]{2,1,0:T(8,128)S(1)} %get-tuple-element.27.forward_ref, f32[12,32,128]{2,1,0:T(8,128)S(1)} %get-tuple-element.28.top_ref, f32[12,32,128]{2,1,0:T(8,128)S(1)} %get-tuple-element.29.bottom_ref, f32[4,32,128]{2,1,0:T(8,128)S(1)} %get-tuple-element.35.ends_ref), custom_call_target="tpu_custom_call" | custom-call | tf_op jit(solution)/shard_map/forward/pallas_call | solution.py:424
  25.4 2.0 %collective-permute-done.5 = f32[2,72,128]{2,1,0:T(8,128)S(1)} collective-permute-done((f32[2,72,128]{2,1,0:T(8,128)S(1)}, f32[2,72,128]{2,1,0:T(8,128)S(1)}, u32[]{:S(2)}, u32[]{:S(2)}) %collective-permute-start.5) | collective-permute-done | bytes 73760 | tf_op jit(solution)/shard_map/ppermute | solution.py:420
  27.5 1.3 %surface.1 = (f32[12,32,128]{2,1,0:T(8,128)}, f32[32,128]{1,0:T(8,128)}) custom-call(f32[12,32,128]{2,1,0:T(8,128)S(1)} %get-tuple-element.36.pulled_ref, f32[12,32,128]{2,1,0:T(8,128)S(1)} %get-tuple-element.24.zonal_ref, f32[12,32,128]{2,1,0:T(8,128)S(1)} %copy-done, f32[12,32,128]{2,1,0:T(8,128)S(1)} %get-tuple-element.37.u_next_ref, ...), custom_call_target="tpu_custom_call" | custom-call | tf_op jit(solution)/shard_map/surface/pallas_call | solution.py:432
  (2 shorter events, 0.0 us)
Async XLA Ops:
  0.6 8.1 %copy-start = (f32[12,32,128]{2,1,0:T(8,128)S(1)}, f32[12,32,128]{2,1,0:T(8,128)}, u32[]{:S(2)}) copy-start(f32[12,32,128]{2,1,0:T(8,128)} %merid_ref.3) | copy-start | bytes 589828
  0.6 8.1 %copy-start.1 = (f32[12,32,128]{2,1,0:T(8,128)S(1)}, f32[12,32,128]{2,1,0:T(8,128)}, u32[]{:S(2)}) copy-start(f32[12,32,128]{2,1,0:T(8,128)} %cot_ref.1) | copy-start | bytes 589828
  2.0 6.7 %collective-permute-start = (f32[8,128]{1,0:T(8,128)S(1)}, f32[8,128]{1,0:T(8,128)S(1)}, u32[]{:S(2)}, u32[]{:S(2)}) collective-permute-start(f32[8,128]{1,0:T(8,128)S(1)} %get-tuple-element.25), channel_id=1, source_target_pairs={{0,4},{4,8},{8,12},{12,0},{1,5},{5,9},{9,13},{13,1},{2,6},{6,10},{... | collective-permute-start | bytes 12296 | tf_op jit(solution)/shard_map/ppermute | solution.py:375
  5.1 3.7 %collective-permute-start.1 = (f32[8,128]{1,0:T(8,128)S(1)}, f32[8,128]{1,0:T(8,128)S(1)}, u32[]{:S(2)}, u32[]{:S(2)}) collective-permute-start(f32[8,128]{1,0:T(8,128)S(1)} %get-tuple-element.26), channel_id=1, source_target_pairs={{4,0},{8,4},{12,8},{0,12},{5,1},{9,5},{13,9},{1,13},{6,2},{10,6},{... | collective-permute-start | bytes 12296 | tf_op jit(solution)/shard_map/ppermute | solution.py:376
  10.1 1.5 %collective-permute-start.2 = (f32[12,32,128]{2,1,0:T(8,128)S(1)}, f32[12,32,128]{2,1,0:T(8,128)S(1)}, u32[]{:S(2)}, u32[]{:S(2)}) collective-permute-start(f32[12,32,128]{2,1,0:T(8,128)S(1)} %get-tuple-element.30.mine_ref), channel_id=1, source_target_pairs={{0,1},{1,0},{2,3},{3,2},{4,5},{5,4},{6,7},{7,6},{8,9},{9,8},{10,11... | collective-permute-start | bytes 589832 | tf_op jit(solution)/shard_map/ppermute | solution.py:396
  12.4 4.9 %collective-permute-start.3 = (f32[6,32,128]{2,1,0:T(8,128)S(1)}, f32[6,32,128]{2,1,0:T(8,128)S(1)}, u32[]{:S(2)}, u32[]{:S(2)}) collective-permute-start(f32[6,32,128]{2,1,0:T(8,128)S(1)} %get-tuple-element.31.mine_ref), channel_id=1, source_target_pairs={{0,2},{1,3},{2,0},{3,1},{4,6},{5,7},{6,4},{7,5},{8,10},{9,11},{10,... | collective-permute-start | bytes 294920 | tf_op jit(solution)/shard_map/ppermute | solution.py:396
  18.2 4.0 %collective-permute-start.4 = (f32[1,72,128]{2,1,0:T(8,128)S(1)}, f32[1,72,128]{2,1,0:T(8,128)S(1)}, u32[]{:S(2)}, u32[]{:S(2)}) collective-permute-start(f32[1,72,128]{2,1,0:T(8,128)S(1)} %bitcast.1), channel_id=1, source_target_pairs={{0,4},{4,0},{8,12},{12,8},{1,5},{5,1},{9,13},{13,9},{2,6},{6,2},{1... | collective-permute-start | bytes 110600 | tf_op jit(solution)/shard_map/ppermute | solution.py:420
  22.2 5.3 %collective-permute-start.5 = (f32[2,72,128]{2,1,0:T(8,128)S(1)}, f32[2,72,128]{2,1,0:T(8,128)S(1)}, u32[]{:S(2)}, u32[]{:S(2)}) collective-permute-start(f32[2,72,128]{2,1,0:T(8,128)S(1)} %pad_maximum_fusion.1), channel_id=1, source_target_pairs={{0,8},{4,12},{8,0},{12,4},{1,9},{5,13},{9,1},{13,5},{2,10},{6,14},... | collective-permute-start | bytes 221192 | tf_op jit(solution)/shard_map/ppermute | solution.py:420

commit v3 on v2

v3 whole, which is shorter than its diff:
```python
import functools

import jax
import jax.numpy as jnp
from jax import lax
from jax.experimental import pallas as pl
from jax.experimental.pallas import tpu as pltpu
from jax.sharding import PartitionSpec as P

ITERS = 3
ADVECT_STEP = 0.25
MIX_RATE = 2.0
HALF_STEP = 0.5 * ADVECT_STEP

N_BLOCK = 12
N_LAST = 6

VMEM_IN = pl.BlockSpec(memory_space=pltpu.VMEM)
SMEM_IN = pl.BlockSpec(memory_space=pltpu.SMEM)


def in_vmem(*shape):
    return pltpu.VMEM(shape, jnp.float32)


def near(*arrays):
    return [pltpu.with_memory_space_constraint(array, pltpu.VMEM) for array in arrays]


def lanes(rows, width):
    return lax.broadcasted_iota(jnp.int32, (rows, width), 1)


def turn(field, shift, axis):
    size = field.shape[axis]
    shift = shift % size
    return field if shift == 0 else pltpu.roll(field, shift, axis)


def splat(scalar, width):
    return jnp.full((1, width), scalar, jnp.float32)


def conductance(drop, upper_thick, lower_thick, wet):
    spacing = 0.5 * (upper_thick + lower_thick)
    rate = 0.2 / spacing + spacing / (spacing * spacing + drop * drop)
    return jnp.where(wet, MIX_RATE * rate, 0.0)


def parity(width):
    return lax.rem(lanes(8, width), 2)


def fold_edges(levels):
    rows, width = levels[0].shape
    groups = rows // 8
    slot = width // groups
    pair = lanes(8, width) // 2
    folded = jnp.zeros((8, width), levels[0].dtype)
    for k, field in enumerate(levels):
        for group in range(groups):
            place = slot * group + 2 * k
            turned = turn(field[8 * group : 8 * group + 8], place + 1, 1)
            folded = jnp.where(pair == place // 2, turned, folded)
    return folded


def fold_surface(field):
    rows, width = field.shape
    groups = rows // 8
    slot = width // groups
    group_of = lanes(8, width) // slot
    folded = jnp.zeros((8, width), field.dtype)
    for group in range(groups):
        part = field[8 * group : 8 * group + 8]
        ends = jnp.where(
            parity(width) == 0,
            jnp.broadcast_to(part[:, width - 1 :], part.shape),
            jnp.broadcast_to(part[:, :1], part.shape),
        )
        folded = jnp.where(group_of == group, ends, folded)
    return folded


def beside_edges(from_west, from_east):
    return jnp.where(parity(from_west.shape[1]) == 0, turn(from_east, -1, 1), turn(from_west, 1, 1))


def spread_edges(beside, rows, k):
    width = beside.shape[1]
    groups = rows // 8
    slot = width // groups
    return jnp.concatenate([turn(beside, -(slot * group + 2 * k + 1), 1) for group in range(groups)])


def pack_kernel(
    tracer_hbm, zonal_hbm, wet_hbm, tracer_ref, zonal_ref, wet_ref, east_ref, west_ref, zonal_edges_ref, sems
):
    own = tracer_ref.shape[0]
    copies = [
        pltpu.make_async_copy(source, target, sems.at[i])
        for i, (source, target) in enumerate(
            ((tracer_hbm, tracer_ref), (zonal_hbm, zonal_ref), (wet_hbm, wet_ref))
        )
    ]
    for copy in copies:
        copy.start()
    copies[0].wait()
    east = fold_edges([tracer_ref[k] for k in range(own)])
    east_ref[:8] = east
    east_ref[8:] = east
    west_ref[:8] = east
    copies[1].wait()
    zonal_edges = fold_edges([zonal_ref[k] for k in range(own)])
    west_ref[8:] = zonal_edges
    zonal_edges_ref[...] = zonal_edges
    copies[2].wait()


def prepare_kernel(own, thick_ref, wet_ref, rows_ref, damping_ref, weight_ref):
    level_count = thick_ref.shape[0]
    rows, width = wet_ref.shape
    wet_levels = wet_ref[...]
    depth = jnp.zeros((rows, width), jnp.float32)
    for k in range(level_count):
        thick = splat(thick_ref[k], width)
        rows_ref[k : k + 1] = thick
        depth = depth + jnp.where(wet_levels > k, thick, 0.0)
    damping_ref[...] = 0.3 + depth / level_count
    wet_edges = fold_surface(wet_levels)
    offset = lax.rem(lanes(8, width), width // (rows // 8)) // 2
    first = lax.axis_index("lev") * own
    thick = jnp.zeros((8, width), jnp.float32)
    for k in range(own):
        thick = jnp.where(offset == k, thick_ref[first + k], thick)
    weight_ref[...] = jnp.where(wet_edges > offset + first, thick, 0.0)


def local_kernel(
    thick_ref, wet_ref, tracer_ref, zonal_ref, merid_ref, cot_ref, from_west_ref, from_east_ref,
    zonal_edges_ref, block_ref, forward_ref, adjoint_ref, top_ref, bottom_ref, u_next_ref, factor_ref, edges_ref,
):
    own, rows, width = tracer_ref.shape
    first = lax.axis_index("lev") * own
    lane = lanes(rows, width)
    wet_levels = wet_ref[...]
    beside = beside_edges(from_west_ref[:8], from_east_ref[:8])
    beside_zonal = turn(from_east_ref[8:], -1, 1)
    factor_ref[...] = HALF_STEP * jnp.where(parity(width) == 0, beside_zonal, -zonal_edges_ref[...])
    forward = []
    for k in range(own):
        values = tracer_ref[k]
        zonal = zonal_ref[k]
        merid = merid_ref[k]
        edge = spread_edges(beside, rows, k)
        c_west = jnp.where(lane == 0, edge, turn(values, 1, 1))
        c_east = jnp.where(lane == width - 1, edge, turn(values, -1, 1))
        u_next = jnp.where(lane == width - 1, spread_edges(beside_zonal, rows, k), turn(zonal, -1, 1))
        u_next_ref[k] = u_next
        flux_y = merid * (turn(values, 1, 0) + values)
        change = u_next * (values + c_east) - zonal * (c_west + values) + (turn(flux_y, -1, 0) - flux_y)
        forward.append(jnp.where(wet_levels > first + k, values - HALF_STEP * change, 0.0))

    thick = [thick_ref[pl.ds(first + k, 1)] for k in range(own)]
    conduct = [None]
    for k in range(1, own):
        conduct.append(
            conductance(forward[k] - forward[k - 1], thick[k - 1], thick[k], wet_levels > first + k)
        )
    pivot = jnp.broadcast_to(thick[0], (rows, width))
    ratio, scale = [None], []
    g_forward = [thick[0] * forward[0]]
    g_adjoint = [cot_ref[0]]
    g_top = [jnp.ones((rows, width), jnp.float32)]
    for k in range(1, own):
        inverse = 1.0 / (pivot + conduct[k])
        scale.append(inverse)
        ratio.append(conduct[k] * inverse)
        pivot = thick[k] + pivot * ratio[k]
        g_forward.append(thick[k] * forward[k] + ratio[k] * g_forward[k - 1])
        g_adjoint.append(cot_ref[k] + ratio[k] * g_adjoint[k - 1])
        g_top.append(ratio[k] * g_top[k - 1])
    scale.append(1.0 / pivot)

    def put(index, field):
        block_ref[rows * index : rows * (index + 1)] = field

    last = own - 1
    y_forward = g_forward[last] * scale[last]
    y_adjoint = g_adjoint[last] * scale[last]
    y_top = g_top[last] * scale[last]
    y_bottom = scale[last]
    put(1, y_top)
    put(2, y_bottom)
    put(4, y_forward)
    put(6, y_adjoint)
    put(7, forward[0])
    put(8, forward[last])
    sums = [jnp.zeros((rows, width), jnp.float32)] * 3
    for k in range(last, -1, -1):
        if k < last:
            y_forward = g_forward[k] * scale[k] + ratio[k + 1] * y_forward
            y_adjoint = g_adjoint[k] * scale[k] + ratio[k + 1] * y_adjoint
            y_top = g_top[k] * scale[k] + ratio[k + 1] * y_top
            y_bottom = ratio[k + 1] * y_bottom
        forward_ref[k] = y_forward
        adjoint_ref[k] = y_adjoint
        top_ref[k] = y_top
        bottom_ref[k] = y_bottom
        square = thick[k] * thick[k]
        sums = [s + square * y for s, y in zip(sums, (y_adjoint, y_top, y_bottom))]
    put(0, y_top)
    put(3, y_forward)
    put(5, y_adjoint)
    for i in range(3):
        put(9 + i, sums[i])
    for i, ref in enumerate((adjoint_ref, top_ref, bottom_ref)):
        edges_ref[8 * i : 8 * i + 8] = fold_edges([ref[k] for k in range(own)])


def merge_kernel(size, final, own, thick_ref, wet_ref, mine_ref, other_ref, block_ref, flux_ref):
    place = lax.axis_index("lev")
    rows, width = wet_ref.shape
    upper = lax.rem(place // size, 2) == 0
    mine = [mine_ref[rows * i : rows * (i + 1)] for i in range(N_BLOCK)]
    other = [other_ref[rows * i : rows * (i + 1)] for i in range(N_BLOCK)]
    above = [jnp.where(upper, a, b) for a, b in zip(mine, other)]
    below = [jnp.where(upper, b, a) for a, b in zip(mine, other)]
    start = (place // (2 * size) * 2 + 1) * size * own
    rate = conductance(
        below[7] - above[8],
        thick_ref[pl.ds(start - 1, 1)],
        thick_ref[pl.ds(start, 1)],
        wet_ref[...] > start,
    )
    rate = rate / (1.0 + rate * (below[0] + above[2]))
    by_forward = rate * (below[3] - above[4])
    by_adjoint = rate * (below[5] - above[6])
    by_top = -rate * above[1]
    by_bottom = rate * below[1]
    flux_ref[0] = by_forward
    flux_ref[1] = by_adjoint
    flux_ref[2] = by_top
    flux_ref[3] = by_bottom
    spread = above[11] - below[10]
    merged = [
        above[0] + above[1] * by_top,
        -below[1] * by_top,
        below[2] - below[1] * by_bottom,
        above[3] + above[1] * by_forward,
        below[4] - below[1] * by_forward,
        above[5] + above[1] * by_adjoint,
        below[6] - below[1] * by_adjoint,
        above[7],
        below[8],
        above[9] + below[9] + by_adjoint * spread,
        above[10] + by_top * spread,
        below[11] + by_bottom * spread,
    ]
    if final:
        upper_next = lax.rem(place // (2 * size), 2) == 0
        merged = last_fields(upper_next, merged)
    for i, field in enumerate(merged):
        block_ref[rows * i : rows * (i + 1)] = field


def last_fields(upper, block):
    return [
        jnp.where(upper, block[2], block[0]),
        jnp.where(upper, block[4], block[3]),
        jnp.where(upper, block[6], block[5]),
        jnp.where(upper, block[8], block[7]),
        block[9],
        jnp.where(upper, block[11], block[10]),
    ]


def final_kernel(
    sizes, own, thick_ref, wet_ref, weight_ref, mine_ref, other_ref, edges_ref, damping_ref, *rest
):
    flux_refs, message_ref, ends_ref = rest[:-2], rest[-2], rest[-1]
    rows, width = wet_ref.shape
    place = lax.axis_index("lev")
    size = sizes[-1]
    upper = lax.rem(place // size, 2) == 0
    start = (place // (2 * size) * 2 + 1) * size * own
    mine = [mine_ref[rows * i : rows * (i + 1)] for i in range(N_LAST)]
    other = [other_ref[rows * i : rows * (i + 1)] for i in range(N_LAST)]
    rate = conductance(
        mine[3] - other[3],
        thick_ref[pl.ds(start - 1, 1)],
        thick_ref[pl.ds(start, 1)],
        wet_ref[...] > start,
    )
    rate = rate / (1.0 + rate * (mine[0] + other[0]))
    in_forward = rate * (other[1] - mine[1])
    in_adjoint = rate * (other[2] - mine[2])
    message_ref[:rows] = mine[4] + other[4] + in_adjoint * (mine[5] - other[5])
    message_ref[rows + 8 :] = damping_ref[...]
    for into, index in ((in_forward, 0), (in_adjoint, 1)):
        top = jnp.where(upper, 0.0, into)
        bottom = jnp.where(upper, into, 0.0)
        for step in range(len(sizes) - 2, -1, -1):
            flux_ref = flux_refs[step]
            flux = flux_ref[index] + top * flux_ref[2] + bottom * flux_ref[3]
            above = lax.rem(place // sizes[step], 2) == 0
            top, bottom = jnp.where(above, top, -flux), jnp.where(above, flux, bottom)
        ends_ref[2 * index] = top
        ends_ref[2 * index + 1] = bottom

    mixed = edges_ref[:8] + edges_ref[8:16] * fold_surface(top) + edges_ref[16:] * fold_surface(bottom)
    message_ref[rows : rows + 8] = weight_ref[...] * mixed


def rest_kernel(
    thick_ref, wet_ref, ends_ref, forward_ref, adjoint_ref, top_ref, bottom_ref, zonal_ref, merid_ref, u_next_ref,
    next_tracer_ref, inner_ref,
):
    own, rows, width = forward_ref.shape
    first = lax.axis_index("lev") * own
    lane = lanes(rows, width)
    wet_levels = wet_ref[...]
    ends = [ends_ref[i] for i in range(4)]
    for k in range(own):
        next_tracer_ref[k] = forward_ref[k] + top_ref[k] * ends[0] + bottom_ref[k] * ends[1]
        mixed = adjoint_ref[k] + top_ref[k] * ends[2] + bottom_ref[k] * ends[3]
        pulled = jnp.where(wet_levels > first + k, thick_ref[pl.ds(first + k, 1)] * mixed, 0.0)
        b_west = jnp.where(lane == 0, 0.0, turn(pulled, 1, 1))
        b_east = jnp.where(lane == width - 1, 0.0, turn(pulled, -1, 1))
        across = zonal_ref[k] * (pulled - b_west) + u_next_ref[k] * (b_east - pulled)
        step = merid_ref[k] * (pulled - turn(pulled, 1, 0))
        inner_ref[k] = pulled + HALF_STEP * (across + step + turn(step, -1, 0))


def total(field):
    while field.ndim > 2:
        field = jnp.sum(field, axis=0)
    return jnp.sum(jnp.sum(field, axis=0, keepdims=True), axis=1, keepdims=True)


def surface_kernel(
    gathered_ref, inner_ref, factor_ref, tracer_adjoint_ref, surface_ref,
    source_scr, damping_scr, edges_scr,
):
    own, rows, width = inner_ref.shape
    count = gathered_ref.shape[0]
    place = lax.axis_index("sub")
    for i in range(count):
        owner = jnp.bitwise_xor(place, i)
        source_scr[owner] = gathered_ref[i, :rows]
        damping_scr[owner] = gathered_ref[i, rows + 8 :]
        edges_scr[owner] = gathered_ref[i, rows : rows + 8]
    west_edges = edges_scr[lax.rem(place + count - 1, count)]
    east_edges = edges_scr[lax.rem(place + 1, count)]
    beside = factor_ref[...] * beside_edges(west_edges, east_edges)
    lane = lanes(rows, width)
    at_edge = jnp.logical_or(lane == 0, lane == width - 1)
    for k in range(own):
        tracer_adjoint_ref[k] = inner_ref[k] + jnp.where(at_edge, spread_edges(beside, rows, k), 0.0)

    first_lane = lax.broadcasted_iota(jnp.int32, (count, rows, width), 2) == 0
    last_lane = lax.broadcasted_iota(jnp.int32, (count, rows, width), 2) == width - 1
    damping = 4.0 + damping_scr[...]

    def passed(field, shift):
        return jnp.concatenate([field[-shift:], field[:-shift]]) if count > 1 else field

    def image_of(field):
        west = turn(field, 1, 2)
        west = jnp.where(first_lane, passed(west, 1), west)
        east = turn(field, -1, 2)
        east = jnp.where(last_lane, passed(east, -1), east)
        return damping * field - (west + east + turn(field, 1, 1) + turn(field, -1, 1))

    residual = source_scr[...]
    image = image_of(residual)
    norm = total(residual * residual)
    step_size = norm / total(residual * image)
    direction, along = residual, image
    surface = jnp.zeros_like(residual)
    for sweep in range(ITERS):
        surface = surface + step_size * direction
        if sweep + 1 < ITERS:
            residual = residual - step_size * along
            image = image_of(residual)
            norm_next = total(residual * residual)
            product = total(residual * image)
            growth = norm_next / norm
            step_size = norm_next / (product - growth * norm_next / step_size)
            direction = residual + growth * direction
            along = image + growth * along
            norm = norm_next
    source_scr[...] = surface
    surface_ref[...] = source_scr[place]


def on_device(tracer, zonal_flow, meridional_flow, cotangent, thickness, wet_levels):
    own, rows, width = tracer.shape
    lev_count = lax.axis_size("lev")
    sub_count = lax.axis_size("sub")
    edge = in_vmem(rows, width)
    levels = in_vmem(own, rows, width)
    marks = pltpu.VMEM((rows, width), jnp.int32)
    thickness = pltpu.with_memory_space_constraint(thickness, pltpu.SMEM)

    tracer, zonal_flow, wet_levels, east, west, zonal_edges = pl.pallas_call(
        pack_kernel,
        out_shape=(levels, levels, marks, in_vmem(16, width), in_vmem(16, width), in_vmem(8, width)),
        in_specs=[pl.BlockSpec(memory_space=pl.ANY)] * 3,
        out_specs=(VMEM_IN,) * 6,
        scratch_shapes=[pltpu.SemaphoreType.DMA((3,))],
        name="pack",
    )(tracer, zonal_flow, wet_levels)
    ring = [(i, (i + 1) % sub_count) for i in range(sub_count)]
    from_west = lax.ppermute(east, "sub", ring)
    from_east = lax.ppermute(west, "sub", [(b, a) for a, b in ring])
    thickness, damping, weights = pl.pallas_call(
        functools.partial(prepare_kernel, own),
        out_shape=(in_vmem(thickness.shape[0], width), edge, in_vmem(8, width)),
        in_specs=[SMEM_IN, VMEM_IN],
        out_specs=(VMEM_IN,) * 3,
        name="prepare",
    )(thickness, *near(wet_levels))

    block, forward, adjoint, top, bottom, u_next, factor, edges = pl.pallas_call(
        local_kernel,
        out_shape=(in_vmem(N_BLOCK * rows, width), levels, levels, levels, levels, levels, in_vmem(8, width), in_vmem(24, width)),
        in_specs=[VMEM_IN] * 9,
        out_specs=(VMEM_IN,) * 8,
        name="local",
    )(*near(thickness, wet_levels, tracer, zonal_flow, meridional_flow, cotangent, from_west, from_east, zonal_edges))

    sizes = [1]
    while sizes[-1] * 2 < lev_count:
        sizes.append(sizes[-1] * 2)
    fluxes = []
    for size in sizes:
        other = lax.ppermute(block, "lev", [(i, i ^ size) for i in range(lev_count)])
        if size == sizes[-1]:
            break
        final = size * 2 == sizes[-1]
        block, flux = pl.pallas_call(
            functools.partial(merge_kernel, size, final, own),
            out_shape=(in_vmem((N_LAST if final else N_BLOCK) * rows, width), in_vmem(4, rows, width)),
            in_specs=[VMEM_IN] * 4,
            out_specs=(VMEM_IN,) * 2,
            name="merge",
        )(*near(thickness, wet_levels, block, other))
        fluxes.append(flux)

    message, ends = pl.pallas_call(
        functools.partial(final_kernel, sizes, own),
        out_shape=(in_vmem(2 * rows + 8, width), in_vmem(4, rows, width)),
        in_specs=[VMEM_IN] * (7 + len(fluxes)),
        out_specs=(VMEM_IN,) * 2,
        name="final",
    )(*near(thickness, wet_levels, weights, block, other, edges, damping, *fluxes))

    gathered = message[None]
    size = 1
    while size < sub_count:
        got = lax.ppermute(gathered, "sub", [(i, i ^ size) for i in range(sub_count)])
        gathered = jnp.concatenate([gathered, got])
        size *= 2

    next_tracer, inner = pl.pallas_call(
        rest_kernel,
        out_shape=(jax.ShapeDtypeStruct(tracer.shape, jnp.float32), levels),
        in_specs=[VMEM_IN] * 10,
        out_specs=(VMEM_IN,) * 2,
        name="rest",
    )(*near(thickness, wet_levels, ends, forward, adjoint, top, bottom, zonal_flow, meridional_flow, u_next))

    tracer_adjoint, surface = pl.pallas_call(
        surface_kernel,
        out_shape=(
            jax.ShapeDtypeStruct(tracer.shape, jnp.float32),
            jax.ShapeDtypeStruct((rows, width), jnp.float32),
        ),
        in_specs=[VMEM_IN] * 3,
        out_specs=(VMEM_IN,) * 2,
        scratch_shapes=[pltpu.VMEM((sub_count, rows, width), jnp.float32)] * 2
        + [pltpu.VMEM((sub_count, 8, width), jnp.float32)],
        name="surface",
    )(*near(gathered, inner, factor))
    return (next_tracer, tracer_adjoint, surface)


def solution(mesh):
    whole = P(("members", "lev"), None, "sub")
    return jax.shard_map(
        on_device,
        mesh=mesh,
        in_specs=(whole, whole, whole, whole, P(), P(None, "sub")),
        out_specs=(whole, whole, P("members", "sub")),
        check_vma=False,
    )
```

time: 29 us -> 26.8 us (0.924)
  Pallas kernels: 6.43 us -> 5.13 us
  waiting for transfers between devices: 10.6 us -> 9.84 us
    pallas_call x1, Pallas kernels: 0.94 us -> 0.12 us  [on_device(): pl.pallas_call(functools.partial(final_kernel, sizes, own), out_shape=(in...]
    ppermute x1, waiting for transfers between devices: 1.56 us -> 0.87 us  [on_device(): from_west = lax.ppermute(east, 'sub', ring)]
    pallas_call x1, Pallas kernels: 0.73 us -> 0.07 us  [on_device(): pl.pallas_call(functools.partial(merge_kernel, size, final, own), out_sha...]
    pallas_call x3 -> x4, Pallas kernels: 3.41 us -> 3.63 us  [the longest x1 1.24 us: on_device(): pl.pallas_call(pack_kernel, out_shape=(levels, levels, marks, in_vmem(16,...]
  transfers between devices with their start and end apart: 6 -> 6, of which waited for: 5 -> 5; matrix products, arithmetic and copies ran while one was open for 0% -> 0% of each run, Pallas kernels for 2% -> 6%
where the time goes in v3:
time: 26.8 us; the launch traced here: 26.7 us
  starting transfers between devices  11 us (41%)
  waiting for transfers between devices  9.84 us (37%)
  Pallas kernels  5.13 us (19%)
  between operations  0.7 us (3%)
    ppermute x2, waiting for transfers between devices, on_device(): lax.ppermute(block, 'lev', [(i, i ^ size) for i in range(lev_count)])  4.64 us
    ppermute x2, waiting for transfers between devices, on_device(): lax.ppermute(gathered, 'sub', [(i, i ^ size) for i in range(sub_count)])  4.33 us
    ppermute x2, starting transfers between devices, on_device(): lax.ppermute(gathered, 'sub', [(i, i ^ size) for i in range(sub_count)])  4.04 us
    ppermute x1, starting transfers between devices, on_device(): from_west = lax.ppermute(east, 'sub', ring)  3.08 us
    ppermute x1, starting transfers between devices, on_device(): from_east = lax.ppermute(west, 'sub', [(b, a) for a, b in ring])  2.09 us
    ppermute x2, starting transfers between devices, on_device(): lax.ppermute(block, 'lev', [(i, i ^ size) for i in range(lev_count)])  1.76 us
    pallas_call x1, Pallas kernels, on_device(): pl.pallas_call(surface_kernel, out_shape=(jax.ShapeDtypeStruct(tracer.sha...  1.31 us
    pallas_call x1, Pallas kernels, on_device(): pl.pallas_call(pack_kernel, out_shape=(levels, levels, marks, in_vmem(16,...  1.24 us
  transfers between devices with their start and end apart: 6, of which 5 were waited for; matrix products, arithmetic and copies ran while one was open for 0% of the time, Pallas kernels for 6%

profile of v3, /device:TPU:0, one launch (start us, length us, event | category | flops | bytes accessed | tf_op | source)
XLA Modules:
  0.0 26.7 jit_solution(15104706973934699771)
XLA Ops:
  0.6 0.0 copy-start
  0.6 0.0 copy-start.1
  0.7 1.2 %pack.1 = (f32[12,32,128]{2,1,0:T(8,128)S(1)}, f32[12,32,128]{2,1,0:T(8,128)S(1)}, s32[32,128]{1,0:T(8,128)S(1)}, f32[16,128]{1,0:T(8,128)S(1)}, f32[16,128]{1,0:T(8,128)S(1)}, /*index=5*/f32[8,128]{1,0:T(8,128)S(1)}) custom-call(f32[12,32,128]{2,1,0:T(8,128)} %tracer_hbm.1, f32[12,32,128]{2,1,0:T(8,128)} %zonal_hbm.1, s32[32,128]{1,0:T(8,128)} %wet_hbm.1), custom_call_target="tpu_custom_call" | custom-call | tf_op jit(solution)/shard_map/pack/pallas_call | solution.py:406
  1.9 3.1 %collective-permute-start = (f32[16,128]{1,0:T(8,128)S(1)}, f32[16,128]{1,0:T(8,128)S(1)}, u32[]{:S(2)}, u32[]{:S(2)}) collective-permute-start(f32[16,128]{1,0:T(8,128)S(1)} %get-tuple-element.33), channel_id=1, source_target_pairs={{0,4},{4,8},{8,12},{12,0},{1,5},{5,9},{9,13},{13,1},{2,6},{6,10},{... | collective-permute-start | bytes 24584 | tf_op jit(solution)/shard_map/ppermute | solution.py:415
  5.0 2.1 %collective-permute-start.1 = (f32[16,128]{1,0:T(8,128)S(1)}, f32[16,128]{1,0:T(8,128)S(1)}, u32[]{:S(2)}, u32[]{:S(2)}) collective-permute-start(f32[16,128]{1,0:T(8,128)S(1)} %get-tuple-element.34), channel_id=1, source_target_pairs={{4,0},{8,4},{12,8},{0,12},{5,1},{9,5},{13,9},{1,13},{6,2},{10,6},{... | collective-permute-start | bytes 24584 | tf_op jit(solution)/shard_map/ppermute | solution.py:416
  7.1 0.8 %prepare.1 = (f32[48,128]{1,0:T(8,128)S(1)}, f32[32,128]{1,0:T(8,128)S(1)}, f32[8,128]{1,0:T(8,128)S(1)}) custom-call(f32[48]{0:T(128)} %thick_ref.1, s32[32,128]{1,0:T(8,128)S(1)} %get-tuple-element.28.wet_ref), custom_call_target="tpu_custom_call" | custom-call | tf_op jit(solution)/shard_map/prepare/pallas_call | solution.py:417
  7.8 0.9 %collective-permute-done.from_west_ref = f32[16,128]{1,0:T(8,128)S(1)} collective-permute-done((f32[16,128]{1,0:T(8,128)S(1)}, f32[16,128]{1,0:T(8,128)S(1)}, u32[]{:S(2)}, u32[]{:S(2)}) %collective-permute-start) | collective-permute-done | bytes 8224 | tf_op jit(solution)/shard_map/ppermute | solution.py:415
  8.7 0.0 collective-permute-done.1.from_east_ref
  8.7 0.0 copy-done
  8.7 0.0 copy-done.1
  8.7 0.7 %local.1 = (f32[384,128]{1,0:T(8,128)S(1)}, f32[12,32,128]{2,1,0:T(8,128)S(1)}, f32[12,32,128]{2,1,0:T(8,128)S(1)}, f32[12,32,128]{2,1,0:T(8,128)S(1)}, f32[12,3...) custom-call(f32[48,128]{1,0:T(8,128)S(1)} %get-tuple-element.29.thick_ref, ...), custom_call_target="tpu_custom_call" | custom-call | tf_op jit(solution)/shard_map/local/pallas_call | solution.py:425
  9.4 0.1 collective-permute-start.2
  9.5 1.4 %collective-permute-done.2.other_ref = f32[384,128]{1,0:T(8,128)S(1)} collective-permute-done((f32[384,128]{1,0:T(8,128)S(1)}, f32[384,128]{1,0:T(8,128)S(1)}, u32[]{:S(2)}, u32[]{:S(2)}) %collective-permute-start.2) | collective-permute-done | bytes 196640 | tf_op jit(solution)/shard_map/ppermute | solution.py:438
  10.9 0.1 merge.1
  11.0 1.7 %collective-permute-start.3 = (f32[192,128]{1,0:T(8,128)S(1)}, f32[192,128]{1,0:T(8,128)S(1)}, u32[]{:S(2)}, u32[]{:S(2)}) collective-permute-start(f32[192,128]{1,0:T(8,128)S(1)} %get-tuple-element.37.mine_ref), channel_id=1, source_target_pairs={{0,2},{1,3},{2,0},{3,1},{4,6},{5,7},{6,4},{7,5},{8,10},{9,11},{10,... | collective-permute-start | bytes 294920 | tf_op jit(solution)/shard_map/ppermute | solution.py:438
  12.7 3.2 %collective-permute-done.3.other_ref = f32[192,128]{1,0:T(8,128)S(1)} collective-permute-done((f32[192,128]{1,0:T(8,128)S(1)}, f32[192,128]{1,0:T(8,128)S(1)}, u32[]{:S(2)}, u32[]{:S(2)}) %collective-permute-start.3) | collective-permute-done | bytes 98336 | tf_op jit(solution)/shard_map/ppermute | solution.py:438
  15.9 0.1 final.1
  16.1 1.5 %collective-permute-start.4 = (f32[1,72,128]{2,1,0:T(8,128)S(1)}, f32[1,72,128]{2,1,0:T(8,128)S(1)}, u32[]{:S(2)}, u32[]{:S(2)}) collective-permute-start(f32[1,72,128]{2,1,0:T(8,128)S(1)} %bitcast.1), channel_id=1, source_target_pairs={{0,4},{4,0},{8,12},{12,8},{1,5},{5,1},{9,13},{13,9},{2,6},{6,2},{1... | collective-permute-start | bytes 110600 | tf_op jit(solution)/shard_map/ppermute | solution.py:462
  17.6 2.5 %collective-permute-done.4 = f32[1,72,128]{2,1,0:T(8,128)S(1)} collective-permute-done((f32[1,72,128]{2,1,0:T(8,128)S(1)}, f32[1,72,128]{2,1,0:T(8,128)S(1)}, u32[]{:S(2)}, u32[]{:S(2)}) %collective-permute-start.4) | collective-permute-done | bytes 36896 | tf_op jit(solution)/shard_map/ppermute | solution.py:462
  20.1 2.5 %collective-permute-start.5 = (f32[2,72,128]{2,1,0:T(8,128)S(1)}, f32[2,72,128]{2,1,0:T(8,128)S(1)}, u32[]{:S(2)}, u32[]{:S(2)}) collective-permute-start(f32[2,72,128]{2,1,0:T(8,128)S(1)} %pad_maximum_fusion.1), channel_id=1, source_target_pairs={{0,8},{4,12},{8,0},{12,4},{1,9},{5,13},{9,1},{13,5},{2,10},{6,14},... | collective-permute-start | bytes 221192 | tf_op jit(solution)/shard_map/ppermute | solution.py:462
  22.6 0.9 %rest.1 = (f32[12,32,128]{2,1,0:T(8,128)}, f32[12,32,128]{2,1,0:T(8,128)S(1)}) custom-call(f32[48,128]{1,0:T(8,128)S(1)} %get-tuple-element.29.thick_ref, s32[32,128]{1,0:T(8,128)S(1)} %get-tuple-element.28.wet_ref, f32[4,32,128]{2,1,0:T(8,128)S(1)} %get-tuple-element.41.ends_ref, f32[12,32,128]{2,1,0:T(8,128)S(1)} %get-tuple-element.42.forward_ref, ...), custom_call_target="tpu_custom_call" | custom-call | tf_op jit(solution)/shard_map/rest/pallas_call | solution.py:466
  23.5 1.9 %collective-permute-done.5 = f32[2,72,128]{2,1,0:T(8,128)S(1)} collective-permute-done((f32[2,72,128]{2,1,0:T(8,128)S(1)}, f32[2,72,128]{2,1,0:T(8,128)S(1)}, u32[]{:S(2)}, u32[]{:S(2)}) %collective-permute-start.5) | collective-permute-done | bytes 73760 | tf_op jit(solution)/shard_map/ppermute | solution.py:462
  25.4 1.3 %surface.1 = (f32[12,32,128]{2,1,0:T(8,128)}, f32[32,128]{1,0:T(8,128)}) custom-call(f32[4,72,128]{2,1,0:T(8,128)S(1)} %pad_maximum_fusion.gathered_ref, f32[12,32,128]{2,1,0:T(8,128)S(1)} %get-tuple-element.49.inner_ref, f32[8,128]{1,0:T(8,128)S(1)} %get-tuple-element.50.factor_ref), custom_call_target="tpu_custom_call" | custom-call | tf_op jit(solution)/shard_map/surface/pallas_call | solution.py:474
  (2 shorter events, 0.0 us)
Async XLA Ops:
  0.6 8.1 %copy-start = (f32[12,32,128]{2,1,0:T(8,128)S(1)}, f32[12,32,128]{2,1,0:T(8,128)}, u32[]{:S(2)}) copy-start(f32[12,32,128]{2,1,0:T(8,128)} %merid_ref.3) | copy-start | bytes 589828
  0.6 8.1 %copy-start.1 = (f32[12,32,128]{2,1,0:T(8,128)S(1)}, f32[12,32,128]{2,1,0:T(8,128)}, u32[]{:S(2)}) copy-start(f32[12,32,128]{2,1,0:T(8,128)} %cot_ref.1) | copy-start | bytes 589828
  1.9 6.8 %collective-permute-start = (f32[16,128]{1,0:T(8,128)S(1)}, f32[16,128]{1,0:T(8,128)S(1)}, u32[]{:S(2)}, u32[]{:S(2)}) collective-permute-start(f32[16,128]{1,0:T(8,128)S(1)} %get-tuple-element.33), channel_id=1, source_target_pairs={{0,4},{4,8},{8,12},{12,0},{1,5},{5,9},{9,13},{13,1},{2,6},{6,10},{... | collective-permute-start | bytes 24584 | tf_op jit(solution)/shard_map/ppermute | solution.py:415
  5.0 3.7 %collective-permute-start.1 = (f32[16,128]{1,0:T(8,128)S(1)}, f32[16,128]{1,0:T(8,128)S(1)}, u32[]{:S(2)}, u32[]{:S(2)}) collective-permute-start(f32[16,128]{1,0:T(8,128)S(1)} %get-tuple-element.34), channel_id=1, source_target_pairs={{4,0},{8,4},{12,8},{0,12},{5,1},{9,5},{13,9},{1,13},{6,2},{10,6},{... | collective-permute-start | bytes 24584 | tf_op jit(solution)/shard_map/ppermute | solution.py:416
  9.4 1.5 %collective-permute-start.2 = (f32[384,128]{1,0:T(8,128)S(1)}, f32[384,128]{1,0:T(8,128)S(1)}, u32[]{:S(2)}, u32[]{:S(2)}) collective-permute-start(f32[384,128]{1,0:T(8,128)S(1)} %get-tuple-element.36.mine_ref), channel_id=1, source_target_pairs={{0,1},{1,0},{2,3},{3,2},{4,5},{5,4},{6,7},{7,6},{8,9},{9,8},{10,11... | collective-permute-start | bytes 589832 | tf_op jit(solution)/shard_map/ppermute | solution.py:438
  11.0 4.9 %collective-permute-start.3 = (f32[192,128]{1,0:T(8,128)S(1)}, f32[192,128]{1,0:T(8,128)S(1)}, u32[]{:S(2)}, u32[]{:S(2)}) collective-permute-start(f32[192,128]{1,0:T(8,128)S(1)} %get-tuple-element.37.mine_ref), channel_id=1, source_target_pairs={{0,2},{1,3},{2,0},{3,1},{4,6},{5,7},{6,4},{7,5},{8,10},{9,11},{10,... | collective-permute-start | bytes 294920 | tf_op jit(solution)/shard_map/ppermute | solution.py:438
  16.1 4.0 %collective-permute-start.4 = (f32[1,72,128]{2,1,0:T(8,128)S(1)}, f32[1,72,128]{2,1,0:T(8,128)S(1)}, u32[]{:S(2)}, u32[]{:S(2)}) collective-permute-start(f32[1,72,128]{2,1,0:T(8,128)S(1)} %bitcast.1), channel_id=1, source_target_pairs={{0,4},{4,0},{8,12},{12,8},{1,5},{5,1},{9,13},{13,9},{2,6},{6,2},{1... | collective-permute-start | bytes 110600 | tf_op jit(solution)/shard_map/ppermute | solution.py:462
  20.1 5.3 %collective-permute-start.5 = (f32[2,72,128]{2,1,0:T(8,128)S(1)}, f32[2,72,128]{2,1,0:T(8,128)S(1)}, u32[]{:S(2)}, u32[]{:S(2)}) collective-permute-start(f32[2,72,128]{2,1,0:T(8,128)S(1)} %pad_maximum_fusion.1), channel_id=1, source_target_pairs={{0,8},{4,12},{8,0},{12,4},{1,9},{5,13},{9,1},{13,5},{2,10},{6,14},... | collective-permute-start | bytes 221192 | tf_op jit(solution)/shard_map/ppermute | solution.py:462

commit v4 on v3

--- a/solution.py
+++ b/solution.py
@@ -94,7 +94,7 @@
 
 
 def pack_kernel(
-    tracer_hbm, zonal_hbm, wet_hbm, tracer_ref, zonal_ref, wet_ref, east_ref, west_ref, zonal_edges_ref, sems
+    tracer_hbm, zonal_hbm, wet_hbm, tracer_ref, zonal_ref, wet_ref, east_ref, west_ref, edges_ref, sems
 ):
     own = tracer_ref.shape[0]
     copies = [
@@ -107,17 +107,17 @@
         copy.start()
     copies[0].wait()
     east = fold_edges([tracer_ref[k] for k in range(own)])
-    east_ref[:8] = east
-    east_ref[8:] = east
-    west_ref[:8] = east
     copies[1].wait()
-    zonal_edges = fold_edges([zonal_ref[k] for k in range(own)])
-    west_ref[8:] = zonal_edges
-    zonal_edges_ref[...] = zonal_edges
+    zonal = fold_edges([zonal_ref[k] for k in range(own)])
+    for ref in (east_ref, west_ref, edges_ref):
+        ref[:8] = east
+        ref[8:] = zonal
     copies[2].wait()
 
 
-def prepare_kernel(own, thick_ref, wet_ref, rows_ref, damping_ref, weight_ref):
+def prepare_kernel(
+    own, thick_ref, wet_ref, tracer_ref, zonal_ref, merid_ref, rows_ref, damping_ref, weight_ref, inside_ref
+):
     level_count = thick_ref.shape[0]
     rows, width = wet_ref.shape
     wet_levels = wet_ref[...]
@@ -134,32 +134,35 @@
     for k in range(own):
         thick = jnp.where(offset == k, thick_ref[first + k], thick)
     weight_ref[...] = jnp.where(wet_edges > offset + first, thick, 0.0)
-
-
-def local_kernel(
-    thick_ref, wet_ref, tracer_ref, zonal_ref, merid_ref, cot_ref, from_west_ref, from_east_ref,
-    zonal_edges_ref, block_ref, forward_ref, adjoint_ref, top_ref, bottom_ref, u_next_ref, factor_ref, edges_ref,
-):
-    own, rows, width = tracer_ref.shape
-    first = lax.axis_index("lev") * own
     lane = lanes(rows, width)
-    wet_levels = wet_ref[...]
-    beside = beside_edges(from_west_ref[:8], from_east_ref[:8])
-    beside_zonal = turn(from_east_ref[8:], -1, 1)
-    factor_ref[...] = HALF_STEP * jnp.where(parity(width) == 0, beside_zonal, -zonal_edges_ref[...])
-    forward = []
     for k in range(own):
         values = tracer_ref[k]
         zonal = zonal_ref[k]
-        merid = merid_ref[k]
-        edge = spread_edges(beside, rows, k)
-        c_west = jnp.where(lane == 0, edge, turn(values, 1, 1))
-        c_east = jnp.where(lane == width - 1, edge, turn(values, -1, 1))
-        u_next = jnp.where(lane == width - 1, spread_edges(beside_zonal, rows, k), turn(zonal, -1, 1))
-        u_next_ref[k] = u_next
-        flux_y = merid * (turn(values, 1, 0) + values)
-        change = u_next * (values + c_east) - zonal * (c_west + values) + (turn(flux_y, -1, 0) - flux_y)
-        forward.append(jnp.where(wet_levels > first + k, values - HALF_STEP * change, 0.0))
+        c_west = jnp.where(lane == 0, 0.0, turn(values, 1, 1))
+        u_next = jnp.where(lane == width - 1, 0.0, turn(zonal, -1, 1))
+        flux_y = merid_ref[k] * (turn(values, 1, 0) + values)
+        change = u_next * (values + turn(values, -1, 1)) - zonal * (c_west + values) + (turn(flux_y, -1, 0) - flux_y)
+        inside_ref[k] = jnp.where(wet_levels > first + k, values - HALF_STEP * change, 0.0)
+
+
+def local_kernel(
+    thick_ref, wet_ref, weight_ref, inside_ref, cot_ref, edges_ref, from_west_ref, from_east_ref,
+    block_ref, forward_ref, adjoint_ref, top_ref, bottom_ref, factor_ref,
+):
+    own, rows, width = cot_ref.shape
+    first = lax.axis_index("lev") * own
+    lane = lanes(rows, width)
+    at_edge = jnp.logical_or(lane == 0, lane == width - 1)
+    even = parity(width) == 0
+    wet_levels = wet_ref[...]
+    factor = HALF_STEP * jnp.where(even, turn(from_east_ref[8:], -1, 1), -edges_ref[8:])
+    factor_ref[...] = factor
+    beside = beside_edges(from_west_ref[:8], from_east_ref[:8])
+    beside = -factor * jnp.where(even, edges_ref[:8] + beside, beside)
+    beside = jnp.where(weight_ref[...] > 0.0, beside, 0.0)
+    forward = []
+    for k in range(own):
+        forward.append(inside_ref[k] + jnp.where(at_edge, spread_edges(beside, rows, k), 0.0))
 
     thick = [thick_ref[pl.ds(first + k, 1)] for k in range(own)]
     conduct = [None]
@@ -214,8 +217,11 @@
     put(5, y_adjoint)
     for i in range(3):
         put(9 + i, sums[i])
+
+
+def edges_kernel(adjoint_ref, top_ref, bottom_ref, edges_ref):
     for i, ref in enumerate((adjoint_ref, top_ref, bottom_ref)):
-        edges_ref[8 * i : 8 * i + 8] = fold_edges([ref[k] for k in range(own)])
+        edges_ref[8 * i : 8 * i + 8] = fold_edges([ref[k] for k in range(ref.shape[0])])
 
 
 def merge_kernel(size, final, own, thick_ref, wet_ref, mine_ref, other_ref, block_ref, flux_ref):
@@ -313,7 +319,7 @@
 
 
 def rest_kernel(
-    thick_ref, wet_ref, ends_ref, forward_ref, adjoint_ref, top_ref, bottom_ref, zonal_ref, merid_ref, u_next_ref,
+    thick_ref, wet_ref, ends_ref, forward_ref, adjoint_ref, top_ref, bottom_ref, zonal_ref, merid_ref, factor_ref,
     next_tracer_ref, inner_ref,
 ):
     own, rows, width = forward_ref.shape
@@ -321,21 +327,28 @@
     lane = lanes(rows, width)
     wet_levels = wet_ref[...]
     ends = [ends_ref[i] for i in range(4)]
+    factor = factor_ref[...]
     for k in range(own):
         next_tracer_ref[k] = forward_ref[k] + top_ref[k] * ends[0] + bottom_ref[k] * ends[1]
         mixed = adjoint_ref[k] + top_ref[k] * ends[2] + bottom_ref[k] * ends[3]
         pulled = jnp.where(wet_levels > first + k, thick_ref[pl.ds(first + k, 1)] * mixed, 0.0)
         b_west = jnp.where(lane == 0, 0.0, turn(pulled, 1, 1))
         b_east = jnp.where(lane == width - 1, 0.0, turn(pulled, -1, 1))
-        across = zonal_ref[k] * (pulled - b_west) + u_next_ref[k] * (b_east - pulled)
-        step = merid_ref[k] * (pulled - turn(pulled, 1, 0))
-        inner_ref[k] = pulled + HALF_STEP * (across + step + turn(step, -1, 0))
+        zonal = HALF_STEP * zonal_ref[k]
+        u_next = jnp.where(lane == width - 1, spread_edges(factor, rows, k), turn(zonal, -1, 1))
+        across = zonal * (pulled - b_west) + u_next * (b_east - pulled)
+        step = HALF_STEP * merid_ref[k] * (pulled - turn(pulled, 1, 0))
+        inner_ref[k] = pulled + across + step + turn(step, -1, 0)
 
 
 def total(field):
     while field.ndim > 2:
         field = jnp.sum(field, axis=0)
     return jnp.sum(jnp.sum(field, axis=0, keepdims=True), axis=1, keepdims=True)
+
+
+def away_order(count):
+    return [0, 1, 3, 2] if count == 4 else list(range(count))
 
 
 def surface_kernel(
@@ -345,8 +358,8 @@
     own, rows, width = inner_ref.shape
     count = gathered_ref.shape[0]
     place = lax.axis_index("sub")
-    for i in range(count):
-        owner = jnp.bitwise_xor(place, i)
+    for i, away in enumerate(away_order(count)):
+        owner = jnp.bitwise_xor(place, away)
         source_scr[owner] = gathered_ref[i, :rows]
         damping_scr[owner] = gathered_ref[i, rows + 8 :]
         edges_scr[owner] = gathered_ref[i, rows : rows + 8]
@@ -403,9 +416,9 @@
     marks = pltpu.VMEM((rows, width), jnp.int32)
     thickness = pltpu.with_memory_space_constraint(thickness, pltpu.SMEM)
 
-    tracer, zonal_flow, wet_levels, east, west, zonal_edges = pl.pallas_call(
+    tracer, zonal_flow, wet_levels, east, west, edges = pl.pallas_call(
         pack_kernel,
-        out_shape=(levels, levels, marks, in_vmem(16, width), in_vmem(16, width), in_vmem(8, width)),
+        out_shape=(levels, levels, marks, in_vmem(16, width), in_vmem(16, width), in_vmem(16, width)),
         in_specs=[pl.BlockSpec(memory_space=pl.ANY)] * 3,
         out_specs=(VMEM_IN,) * 6,
         scratch_shapes=[pltpu.SemaphoreType.DMA((3,))],
@@ -414,21 +427,24 @@
     ring = [(i, (i + 1) % sub_count) for i in range(sub_count)]
     from_west = lax.ppermute(east, "sub", ring)
     from_east = lax.ppermute(west, "sub", [(b, a) for a, b in ring])
-    thickness, damping, weights = pl.pallas_call(
+    thickness, damping, weights, inside = pl.pallas_call(
         functools.partial(prepare_kernel, own),
-        out_shape=(in_vmem(thickness.shape[0], width), edge, in_vmem(8, width)),
-        in_specs=[SMEM_IN, VMEM_IN],
-        out_specs=(VMEM_IN,) * 3,
+        out_shape=(in_vmem(thickness.shape[0], width), edge, in_vmem(8, width), levels),
+        in_specs=[SMEM_IN] + [VMEM_IN] * 4,
+        out_specs=(VMEM_IN,) * 4,
         name="prepare",
-    )(thickness, *near(wet_levels))
-
-    block, forward, adjoint, top, bottom, u_next, factor, edges = pl.pallas_call(
+    )(thickness, *near(wet_levels, tracer, zonal_flow, meridional_flow))
+
+    block, forward, adjoint, top, bottom, factor = pl.pallas_call(
         local_kernel,
-        out_shape=(in_vmem(N_BLOCK * rows, width), levels, levels, levels, levels, levels, in_vmem(8, width), in_vmem(24, width)),
-        in_specs=[VMEM_IN] * 9,
-        out_specs=(VMEM_IN,) * 8,
+        out_shape=(in_vmem(N_BLOCK * rows, width), levels, levels, levels, levels, in_vmem(8, width)),
+        in_specs=[VMEM_IN] * 8,
+        out_specs=(VMEM_IN,) * 6,
         name="local",
-    )(*near(thickness, wet_levels, tracer, zonal_flow, meridional_flow, cotangent, from_west, from_east, zonal_edges))
+    )(*near(thickness, wet_levels, weights, inside, cotangent, edges, from_west, from_east))
+    edges = pl.pallas_call(
+        edges_kernel, out_shape=in_vmem(24, width), in_specs=[VMEM_IN] * 3, out_specs=VMEM_IN, name="edges"
+    )(*near(adjoint, top, bottom))
 
     sizes = [1]
     while sizes[-1] * 2 < lev_count:
@@ -456,12 +472,18 @@
         name="final",
     )(*near(thickness, wet_levels, weights, block, other, edges, damping, *fluxes))
 
-    gathered = message[None]
-    size = 1
-    while size < sub_count:
-        got = lax.ppermute(gathered, "sub", [(i, i ^ size) for i in range(sub_count)])
-        gathered = jnp.concatenate([gathered, got])
-        size *= 2
+    aways = away_order(sub_count)
+    if sub_count <= 4:
+        gathered = jnp.stack(
+            [message]
+            + [lax.ppermute(message, "sub", [(i, i ^ away) for i in range(sub_count)]) for away in aways[1:]]
+        )
+    else:
+        gathered = message[None]
+        while gathered.shape[0] < sub_count:
+            size = gathered.shape[0]
+            got = lax.ppermute(gathered, "sub", [(i, i ^ size) for i in range(sub_count)])
+            gathered = jnp.concatenate([gathered, got])
 
     next_tracer, inner = pl.pallas_call(
         rest_kernel,
@@ -469,7 +491,7 @@
         in_specs=[VMEM_IN] * 10,
         out_specs=(VMEM_IN,) * 2,
         name="rest",
-    )(*near(thickness, wet_levels, ends, forward, adjoint, top, bottom, zonal_flow, meridional_flow, u_next))
+    )(*near(thickness, wet_levels, ends, forward, adjoint, top, bottom, zonal_flow, meridional_flow, factor))
 
     tracer_adjoint, surface = pl.pallas_call(
         surface_kernel,

time: 26.8 us -> 25.5 us (0.951)
  waiting for transfers between devices: 9.84 us -> 7.95 us
  starting transfers between devices: 11 us -> 11.4 us
    ppermute x2 -> x3, waiting for transfers between devices: 4.33 us -> 2.95 us  [on_device(): lax.ppermute(message, 'sub', [(i, i ^ away) for i in range(sub_count)])]
    ppermute x2 -> x3, starting transfers between devices: 4.04 us -> 4.43 us  [on_device(): lax.ppermute(message, 'sub', [(i, i ^ away) for i in range(sub_count)])]
    ppermute x1, waiting for transfers between devices: 0.87 us -> 0.57 us  [on_device(): from_west = lax.ppermute(east, 'sub', ring)]
    pallas_call x1, Pallas kernels: 0.78 us -> 1.07 us  [on_device(): pl.pallas_call(functools.partial(prepare_kernel, own), out_shape=(in_vmem...]
    pallas_call x1, Pallas kernels: 0.7 us -> 0.41 us  [on_device(): pl.pallas_call(local_kernel, out_shape=(in_vmem(N_BLOCK * rows, width), l...]
  transfers between devices with their start and end apart: 6 -> 7, of which waited for: 5 -> 4; matrix products, arithmetic and copies ran while one was open for 0% -> 0% of each run, Pallas kernels for 6% -> 9%
where the time goes in v4:
time: 25.5 us; the launch traced here: 25.4 us
  starting transfers between devices  11.4 us (45%)
  waiting for transfers between devices  7.95 us (31%)
  Pallas kernels  5.36 us (21%)
  between operations  0.69 us (3%)
    ppermute x2, waiting for transfers between devices, on_device(): lax.ppermute(block, 'lev', [(i, i ^ size) for i in range(lev_count)])  4.43 us
    ppermute x3, starting transfers between devices, on_device(): lax.ppermute(message, 'sub', [(i, i ^ away) for i in range(sub_count)])  4.43 us
    ppermute x1, starting transfers between devices, on_device(): from_west = lax.ppermute(east, 'sub', ring)  3.08 us
    ppermute x3, waiting for transfers between devices, on_device(): lax.ppermute(message, 'sub', [(i, i ^ away) for i in range(sub_count)])  2.95 us
    ppermute x1, starting transfers between devices, on_device(): from_east = lax.ppermute(west, 'sub', [(b, a) for a, b in ring])  2.09 us
    ppermute x2, starting transfers between devices, on_device(): lax.ppermute(block, 'lev', [(i, i ^ size) for i in range(lev_count)])  1.76 us
    pallas_call x1, Pallas kernels, on_device(): pl.pallas_call(surface_kernel, out_shape=(jax.ShapeDtypeStruct(tracer.sha...  1.31 us
    pallas_call x1, Pallas kernels, on_device(): pl.pallas_call(pack_kernel, out_shape=(levels, levels, marks, in_vmem(16,...  1.23 us
  transfers between devices with their start and end apart: 7, of which 4 were waited for; matrix products, arithmetic and copies ran while one was open for 0% of the time, Pallas kernels for 9%

profile of v4, /device:TPU:0, one launch (start us, length us, event | category | flops | bytes accessed | tf_op | source)
XLA Modules:
  0.0 25.4 jit_solution(3821663158768911817)
XLA Ops:
  0.6 0.0 copy-start
  0.6 1.2 %pack.1 = (f32[12,32,128]{2,1,0:T(8,128)S(1)}, f32[12,32,128]{2,1,0:T(8,128)S(1)}, s32[32,128]{1,0:T(8,128)S(1)}, f32[16,128]{1,0:T(8,128)S(1)}, f32[16,128]{1,0:T(8,128)S(1)}, /*index=5*/f32[16,128]{1,0:T(8,128)S(1)}) custom-call(f32[12,32,128]{2,1,0:T(8,128)} %tracer_hbm.1, f32[12,32,128]{2,1,0:T(8,128)} %zonal_hbm.1, s32[32,128]{1,0:T(8,128)} %wet_hbm.1), custom_call_target="tpu_custom_call" | custom-call | tf_op jit(solution)/shard_map/pack/pallas_call | solution.py:419
  1.9 3.1 %collective-permute-start = (f32[16,128]{1,0:T(8,128)S(1)}, f32[16,128]{1,0:T(8,128)S(1)}, u32[]{:S(2)}, u32[]{:S(2)}) collective-permute-start(f32[16,128]{1,0:T(8,128)S(1)} %get-tuple-element.34), channel_id=1, source_target_pairs={{0,4},{4,8},{8,12},{12,0},{1,5},{5,9},{9,13},{13,1},{2,6},{6,10},{... | collective-permute-start | bytes 24584 | tf_op jit(solution)/shard_map/ppermute | solution.py:428
  5.0 2.1 %collective-permute-start.1 = (f32[16,128]{1,0:T(8,128)S(1)}, f32[16,128]{1,0:T(8,128)S(1)}, u32[]{:S(2)}, u32[]{:S(2)}) collective-permute-start(f32[16,128]{1,0:T(8,128)S(1)} %get-tuple-element.35), channel_id=1, source_target_pairs={{4,0},{8,4},{12,8},{0,12},{5,1},{9,5},{13,9},{1,13},{6,2},{10,6},{... | collective-permute-start | bytes 24584 | tf_op jit(solution)/shard_map/ppermute | solution.py:429
  7.0 0.0 copy-done
  7.1 0.0 copy-start.1
  7.1 1.1 %prepare.1 = (f32[48,128]{1,0:T(8,128)S(1)}, f32[32,128]{1,0:T(8,128)S(1)}, f32[8,128]{1,0:T(8,128)S(1)}, f32[12,32,128]{2,1,0:T(8,128)S(1)}) custom-call(f32[48]{0:T(128)} %thick_ref.1, s32[32,128]{1,0:T(8,128)S(1)} %get-tuple-element.27.wet_ref, f32[12,32,128]{2,1,0:T(8,128)S(1)} %get-tuple-element.28.tracer_ref, ...), custom_call_target="tpu_custom_call" | custom-call | tf_op jit(solution)/shard_map/prepare/pallas_call | solution.py:430
  8.1 0.6 %collective-permute-done.from_west_ref = f32[16,128]{1,0:T(8,128)S(1)} collective-permute-done((f32[16,128]{1,0:T(8,128)S(1)}, f32[16,128]{1,0:T(8,128)S(1)}, u32[]{:S(2)}, u32[]{:S(2)}) %collective-permute-start) | collective-permute-done | bytes 8224 | tf_op jit(solution)/shard_map/ppermute | solution.py:428
  8.7 0.0 collective-permute-done.1.from_east_ref
  8.7 0.0 copy-done.1
  8.7 0.4 %local.1 = (f32[384,128]{1,0:T(8,128)S(1)}, f32[12,32,128]{2,1,0:T(8,128)S(1)}, f32[12,32,128]{2,1,0:T(8,128)S(1)}, f32[12,32,128]{2,1,0:T(8,128)S(1)}, f32[12,3...) custom-call(f32[48,128]{1,0:T(8,128)S(1)} %get-tuple-element.30.thick_ref, s32[32,128]{1,0:T(8,128)S(1)} %get-tuple-element.27.wet_ref, ...), custom_call_target="tpu_custom_call" | custom-call | tf_op jit(solution)/shard_map/local/pallas_call | solution.py:438
  9.1 0.1 collective-permute-start.2
  9.2 1.4 %collective-permute-done.2.other_ref = f32[384,128]{1,0:T(8,128)S(1)} collective-permute-done((f32[384,128]{1,0:T(8,128)S(1)}, f32[384,128]{1,0:T(8,128)S(1)}, u32[]{:S(2)}, u32[]{:S(2)}) %collective-permute-start.2) | collective-permute-done | bytes 196640 | tf_op jit(solution)/shard_map/ppermute | solution.py:454
  10.6 0.1 merge.1
  10.7 1.7 %collective-permute-start.3 = (f32[192,128]{1,0:T(8,128)S(1)}, f32[192,128]{1,0:T(8,128)S(1)}, u32[]{:S(2)}, u32[]{:S(2)}) collective-permute-start(f32[192,128]{1,0:T(8,128)S(1)} %get-tuple-element.37.mine_ref), channel_id=1, source_target_pairs={{0,2},{1,3},{2,0},{3,1},{4,6},{5,7},{6,4},{7,5},{8,10},{9,11},{10,... | collective-permute-start | bytes 294920 | tf_op jit(solution)/shard_map/ppermute | solution.py:454
  12.4 0.2 edges.1.edges_ref
  12.6 3.0 %collective-permute-done.3.other_ref = f32[192,128]{1,0:T(8,128)S(1)} collective-permute-done((f32[192,128]{1,0:T(8,128)S(1)}, f32[192,128]{1,0:T(8,128)S(1)}, u32[]{:S(2)}, u32[]{:S(2)}) %collective-permute-start.3) | collective-permute-done | bytes 98336 | tf_op jit(solution)/shard_map/ppermute | solution.py:454
  15.6 0.1 final.1
  15.7 2.6 %collective-permute-start.6 = (f32[72,128]{1,0:T(8,128)S(1)}, f32[72,128]{1,0:T(8,128)S(1)}, u32[]{:S(2)}, u32[]{:S(2)}) collective-permute-start(f32[72,128]{1,0:T(8,128)S(1)} %get-tuple-element.47), channel_id=1, source_target_pairs={{0,8},{4,12},{8,0},{12,4},{1,9},{5,13},{9,1},{13,5},{2,10},{6,14},... | collective-permute-start | bytes 110600 | tf_op jit(solution)/shard_map/ppermute | solution.py:479
  18.3 1.4 %collective-permute-start.5 = (f32[72,128]{1,0:T(8,128)S(1)}, f32[72,128]{1,0:T(8,128)S(1)}, u32[]{:S(2)}, u32[]{:S(2)}) collective-permute-start(f32[72,128]{1,0:T(8,128)S(1)} %get-tuple-element.47), channel_id=1, source_target_pairs={{0,12},{4,8},{8,4},{12,0},{1,13},{5,9},{9,5},{13,1},{2,14},{6,10},... | collective-permute-start | bytes 110600 | tf_op jit(solution)/shard_map/ppermute | solution.py:479
  19.7 0.5 %collective-permute-start.4 = (f32[72,128]{1,0:T(8,128)S(1)}, f32[72,128]{1,0:T(8,128)S(1)}, u32[]{:S(2)}, u32[]{:S(2)}) collective-permute-start(f32[72,128]{1,0:T(8,128)S(1)} %get-tuple-element.47), channel_id=1, source_target_pairs={{0,4},{4,0},{8,12},{12,8},{1,5},{5,1},{9,13},{13,9},{2,6},{6,2},{1... | collective-permute-start | bytes 110600 | tf_op jit(solution)/shard_map/ppermute | solution.py:479
  20.2 0.9 %rest.1 = (f32[12,32,128]{2,1,0:T(8,128)}, f32[12,32,128]{2,1,0:T(8,128)S(1)}) custom-call(f32[48,128]{1,0:T(8,128)S(1)} %get-tuple-element.30.thick_ref, s32[32,128]{1,0:T(8,128)S(1)} %get-tuple-element.27.wet_ref, f32[4,32,128]{2,1,0:T(8,128)S(1)} %get-tuple-element.43.ends_ref, f32[12,32,128]{2,1,0:T(8,128)S(1)} %get-tuple-element.44.forward_ref, ...), custom_call_target="tpu_custom_call" | custom-call | tf_op jit(solution)/shard_map/rest/pallas_call | solution.py:488
  21.1 0.0 collective-permute-done.6
  21.1 2.9 %collective-permute-done.5 = f32[72,128]{1,0:T(8,128)S(1)} collective-permute-done((f32[72,128]{1,0:T(8,128)S(1)}, f32[72,128]{1,0:T(8,128)S(1)}, u32[]{:S(2)}, u32[]{:S(2)}) %collective-permute-start.5) | collective-permute-done | bytes 36896 | tf_op jit(solution)/shard_map/ppermute | solution.py:479
  24.1 0.0 collective-permute-done.4
  24.1 1.3 %surface.1 = (f32[12,32,128]{2,1,0:T(8,128)}, f32[32,128]{1,0:T(8,128)}) custom-call(f32[4,72,128]{2,1,0:T(8,128)S(1)} %pad_maximum_fusion.gathered_ref, f32[12,32,128]{2,1,0:T(8,128)S(1)} %get-tuple-element.48.inner_ref, f32[8,128]{1,0:T(8,128)S(1)} %get-tuple-element.45.factor_ref), custom_call_target="tpu_custom_call" | custom-call | tf_op jit(solution)/shard_map/surface/pallas_call | solution.py:496
  (1 shorter events, 0.0 us)
Async XLA Ops:
  0.6 6.4 %copy-start = (f32[12,32,128]{2,1,0:T(8,128)S(1)}, f32[12,32,128]{2,1,0:T(8,128)}, u32[]{:S(2)}) copy-start(f32[12,32,128]{2,1,0:T(8,128)} %merid_ref.3) | copy-start | bytes 589828
  1.9 6.8 %collective-permute-start = (f32[16,128]{1,0:T(8,128)S(1)}, f32[16,128]{1,0:T(8,128)S(1)}, u32[]{:S(2)}, u32[]{:S(2)}) collective-permute-start(f32[16,128]{1,0:T(8,128)S(1)} %get-tuple-element.34), channel_id=1, source_target_pairs={{0,4},{4,8},{8,12},{12,0},{1,5},{5,9},{9,13},{13,1},{2,6},{6,10},{... | collective-permute-start | bytes 24584 | tf_op jit(solution)/shard_map/ppermute | solution.py:428
  5.0 3.7 %collective-permute-start.1 = (f32[16,128]{1,0:T(8,128)S(1)}, f32[16,128]{1,0:T(8,128)S(1)}, u32[]{:S(2)}, u32[]{:S(2)}) collective-permute-start(f32[16,128]{1,0:T(8,128)S(1)} %get-tuple-element.35), channel_id=1, source_target_pairs={{4,0},{8,4},{12,8},{0,12},{5,1},{9,5},{13,9},{1,13},{6,2},{10,6},{... | collective-permute-start | bytes 24584 | tf_op jit(solution)/shard_map/ppermute | solution.py:429
  7.1 1.7 %copy-start.1 = (f32[12,32,128]{2,1,0:T(8,128)S(1)}, f32[12,32,128]{2,1,0:T(8,128)}, u32[]{:S(2)}) copy-start(f32[12,32,128]{2,1,0:T(8,128)} %cot_ref.1) | copy-start | bytes 589828
  9.1 1.5 %collective-permute-start.2 = (f32[384,128]{1,0:T(8,128)S(1)}, f32[384,128]{1,0:T(8,128)S(1)}, u32[]{:S(2)}, u32[]{:S(2)}) collective-permute-start(f32[384,128]{1,0:T(8,128)S(1)} %get-tuple-element.36.mine_ref), channel_id=1, source_target_pairs={{0,1},{1,0},{2,3},{3,2},{4,5},{5,4},{6,7},{7,6},{8,9},{9,8},{10,11... | collective-permute-start | bytes 589832 | tf_op jit(solution)/shard_map/ppermute | solution.py:454
  10.7 4.9 %collective-permute-start.3 = (f32[192,128]{1,0:T(8,128)S(1)}, f32[192,128]{1,0:T(8,128)S(1)}, u32[]{:S(2)}, u32[]{:S(2)}) collective-permute-start(f32[192,128]{1,0:T(8,128)S(1)} %get-tuple-element.37.mine_ref), channel_id=1, source_target_pairs={{0,2},{1,3},{2,0},{3,1},{4,6},{5,7},{6,4},{7,5},{8,10},{9,11},{10,... | collective-permute-start | bytes 294920 | tf_op jit(solution)/shard_map/ppermute | solution.py:454
  15.7 5.4 %collective-permute-start.6 = (f32[72,128]{1,0:T(8,128)S(1)}, f32[72,128]{1,0:T(8,128)S(1)}, u32[]{:S(2)}, u32[]{:S(2)}) collective-permute-start(f32[72,128]{1,0:T(8,128)S(1)} %get-tuple-element.47), channel_id=1, source_target_pairs={{0,8},{4,12},{8,0},{12,4},{1,9},{5,13},{9,1},{13,5},{2,10},{6,14},... | collective-permute-start | bytes 110600 | tf_op jit(solution)/shard_map/ppermute | solution.py:479
  18.3 5.8 %collective-permute-start.5 = (f32[72,128]{1,0:T(8,128)S(1)}, f32[72,128]{1,0:T(8,128)S(1)}, u32[]{:S(2)}, u32[]{:S(2)}) collective-permute-start(f32[72,128]{1,0:T(8,128)S(1)} %get-tuple-element.47), channel_id=1, source_target_pairs={{0,12},{4,8},{8,4},{12,0},{1,13},{5,9},{9,5},{13,1},{2,14},{6,10},... | collective-permute-start | bytes 110600 | tf_op jit(solution)/shard_map/ppermute | solution.py:479
  19.7 4.4 %collective-permute-start.4 = (f32[72,128]{1,0:T(8,128)S(1)}, f32[72,128]{1,0:T(8,128)S(1)}, u32[]{:S(2)}, u32[]{:S(2)}) collective-permute-start(f32[72,128]{1,0:T(8,128)S(1)} %get-tuple-element.47), channel_id=1, source_target_pairs={{0,4},{4,0},{8,12},{12,8},{1,5},{5,1},{9,13},{13,9},{2,6},{6,2},{1... | collective-permute-start | bytes 110600 | tf_op jit(solution)/shard_map/ppermute | solution.py:479

commit v5 on v4

--- a/solution.py
+++ b/solution.py
@@ -129,11 +129,14 @@
     damping_ref[...] = 0.3 + depth / level_count
     wet_edges = fold_surface(wet_levels)
     offset = lax.rem(lanes(8, width), width // (rows // 8)) // 2
-    first = lax.axis_index("lev") * own
-    thick = jnp.zeros((8, width), jnp.float32)
-    for k in range(own):
-        thick = jnp.where(offset == k, thick_ref[first + k], thick)
-    weight_ref[...] = jnp.where(wet_edges > offset + first, thick, 0.0)
+    place = lax.axis_index("lev")
+    for i in range(2):
+        first = (place // 2 * 2 + i) * own
+        thick = jnp.zeros((8, width), jnp.float32)
+        for k in range(own):
+            thick = jnp.where(offset == k, thick_ref[first + k], thick)
+        weight_ref[8 * i : 8 * i + 8] = jnp.where(wet_edges > offset + first, thick, 0.0)
+    first = place * own
     lane = lanes(rows, width)
     for k in range(own):
         values = tracer_ref[k]
@@ -159,7 +162,8 @@
     factor_ref[...] = factor
     beside = beside_edges(from_west_ref[:8], from_east_ref[:8])
     beside = -factor * jnp.where(even, edges_ref[:8] + beside, beside)
-    beside = jnp.where(weight_ref[...] > 0.0, beside, 0.0)
+    weight = jnp.where(lax.rem(lax.axis_index("lev"), 2) == 0, weight_ref[:8], weight_ref[8:])
+    beside = jnp.where(weight > 0.0, beside, 0.0)
     forward = []
     for k in range(own):
         forward.append(inside_ref[k] + jnp.where(at_edge, spread_edges(beside, rows, k), 0.0))
@@ -282,7 +286,7 @@
 
 
 def final_kernel(
-    sizes, own, thick_ref, wet_ref, weight_ref, mine_ref, other_ref, edges_ref, damping_ref, *rest
+    sizes, own, thick_ref, wet_ref, weight_ref, mine_ref, other_ref, edges_ref, other_edges_ref, damping_ref, *rest
 ):
     flux_refs, message_ref, ends_ref = rest[:-2], rest[-2], rest[-1]
     rows, width = wet_ref.shape
@@ -302,20 +306,26 @@
     in_forward = rate * (other[1] - mine[1])
     in_adjoint = rate * (other[2] - mine[2])
     message_ref[:rows] = mine[4] + other[4] + in_adjoint * (mine[5] - other[5])
-    message_ref[rows + 8 :] = damping_ref[...]
+    message_ref[rows + 16 :] = damping_ref[...]
+    even = lax.rem(place, 2) == 0
+    pair = []
     for into, index in ((in_forward, 0), (in_adjoint, 1)):
         top = jnp.where(upper, 0.0, into)
         bottom = jnp.where(upper, into, 0.0)
         for step in range(len(sizes) - 2, -1, -1):
             flux_ref = flux_refs[step]
             flux = flux_ref[index] + top * flux_ref[2] + bottom * flux_ref[3]
+            if step == 0:
+                pair = [(top, flux), (-flux, bottom)]
             above = lax.rem(place // sizes[step], 2) == 0
             top, bottom = jnp.where(above, top, -flux), jnp.where(above, flux, bottom)
         ends_ref[2 * index] = top
         ends_ref[2 * index + 1] = bottom
-
-    mixed = edges_ref[:8] + edges_ref[8:16] * fold_surface(top) + edges_ref[16:] * fold_surface(bottom)
-    message_ref[rows : rows + 8] = weight_ref[...] * mixed
+    for i, (top, bottom) in enumerate(pair):
+        is_mine = even if i == 0 else jnp.logical_not(even)
+        edges = jnp.where(is_mine, edges_ref[...], other_edges_ref[...])
+        mixed = edges[:8] + edges[8:16] * fold_surface(top) + edges[16:] * fold_surface(bottom)
+        message_ref[rows + 8 * i : rows + 8 * i + 8] = weight_ref[8 * i : 8 * i + 8] * mixed
 
 
 def rest_kernel(
@@ -347,8 +357,21 @@
     return jnp.sum(jnp.sum(field, axis=0, keepdims=True), axis=1, keepdims=True)
 
 
-def away_order(count):
-    return [0, 1, 3, 2] if count == 4 else list(range(count))
+def routes(count):
+    if count == 4:
+        return [[2, 3, 1, 0], [3, 2, 0, 1], [1, 0, 3, 2]]
+    return [[i ^ away for i in range(count)] for away in range(1, count)]
+
+
+def crossed(route, lev_count):
+    return [(s * lev_count + l, t * lev_count + (l ^ 1)) for s, t in enumerate(route) for l in range(lev_count)]
+
+
+def owner_of(route, place):
+    owner = 0
+    for source, target in enumerate(route):
+        owner = jnp.where(place == target, source, owner)
+    return owner
 
 
 def surface_kernel(
@@ -358,11 +381,13 @@
     own, rows, width = inner_ref.shape
     count = gathered_ref.shape[0]
     place = lax.axis_index("sub")
-    for i, away in enumerate(away_order(count)):
-        owner = jnp.bitwise_xor(place, away)
+    even = lax.rem(lax.axis_index("lev"), 2) == 0
+    ways = [list(range(count))] + routes(count)[:: -1 if count == 4 else 1]
+    for i, route in enumerate(ways):
+        owner = owner_of(route, place)
         source_scr[owner] = gathered_ref[i, :rows]
-        damping_scr[owner] = gathered_ref[i, rows + 8 :]
-        edges_scr[owner] = gathered_ref[i, rows : rows + 8]
+        damping_scr[owner] = gathered_ref[i, rows + 16 :]
+        edges_scr[owner] = jnp.where(even, gathered_ref[i, rows : rows + 8], gathered_ref[i, rows + 8 : rows + 16])
     west_edges = edges_scr[lax.rem(place + count - 1, count)]
     east_edges = edges_scr[lax.rem(place + 1, count)]
     beside = factor_ref[...] * beside_edges(west_edges, east_edges)
@@ -429,7 +454,7 @@
     from_east = lax.ppermute(west, "sub", [(b, a) for a, b in ring])
     thickness, damping, weights, inside = pl.pallas_call(
         functools.partial(prepare_kernel, own),
-        out_shape=(in_vmem(thickness.shape[0], width), edge, in_vmem(8, width), levels),
+        out_shape=(in_vmem(thickness.shape[0], width), edge, in_vmem(16, width), levels),
         in_specs=[SMEM_IN] + [VMEM_IN] * 4,
         out_specs=(VMEM_IN,) * 4,
         name="prepare",
@@ -445,13 +470,14 @@
     edges = pl.pallas_call(
         edges_kernel, out_shape=in_vmem(24, width), in_specs=[VMEM_IN] * 3, out_specs=VMEM_IN, name="edges"
     )(*near(adjoint, top, bottom))
+    other_edges = lax.ppermute(edges, "lev", [(i, i ^ 1) for i in range(lev_count)])
 
     sizes = [1]
     while sizes[-1] * 2 < lev_count:
         sizes.append(sizes[-1] * 2)
     fluxes = []
     for size in sizes:
-        other = lax.ppermute(block, "lev", [(i, i ^ size) for i in range(lev_count)])
+        other = lax.ppermute(block, "lev", [(i, i ^ (2 * size - 1)) for i in range(lev_count)])
         if size == sizes[-1]:
             break
         final = size * 2 == sizes[-1]
@@ -466,17 +492,15 @@
 
     message, ends = pl.pallas_call(
         functools.partial(final_kernel, sizes, own),
-        out_shape=(in_vmem(2 * rows + 8, width), in_vmem(4, rows, width)),
-        in_specs=[VMEM_IN] * (7 + len(fluxes)),
+        out_shape=(in_vmem(2 * rows + 16, width), in_vmem(4, rows, width)),
+        in_specs=[VMEM_IN] * (8 + len(fluxes)),
         out_specs=(VMEM_IN,) * 2,
         name="final",
-    )(*near(thickness, wet_levels, weights, block, other, edges, damping, *fluxes))
-
-    aways = away_order(sub_count)
-    if sub_count <= 4:
+    )(*near(thickness, wet_levels, weights, block, other, edges, other_edges, damping, *fluxes))
+
+    if sub_count == 4:
         gathered = jnp.stack(
-            [message]
-            + [lax.ppermute(message, "sub", [(i, i ^ away) for i in range(sub_count)]) for away in aways[1:]]
+            [message] + [lax.ppermute(message, ("sub", "lev"), crossed(way, lev_count)) for way in routes(sub_count)[::-1]]
         )
     else:
         gathered = message[None]

time: 25.5 us -> 25 us (0.980)
  waiting for transfers between devices: 7.95 us -> 7.49 us
    ppermute x5 -> x6, waiting for transfers between devices: 7.38 us -> 6.92 us  [the longest x2 3.35 us: on_device(): lax.ppermute(block, 'lev', [(i, i ^ 2 * size - 1) for i in range(lev_coun...]
    ppermute x5 -> x6, starting transfers between devices: 6.19 us -> 6.08 us  [the longest x3 4.14 us: on_device(): lax.ppermute(message, ('sub', 'lev'), crossed(way, lev_count))]
  transfers between devices with their start and end apart: 7 -> 8, of which waited for: 4 -> 7; matrix products, arithmetic and copies ran while one was open for 0% -> 0% of each run, Pallas kernels for 9% -> 9%
where the time goes in v5:
time: 25 us; the launch traced here: 24.8 us
  starting transfers between devices  11.2 us (45%)
  waiting for transfers between devices  7.49 us (30%)
  Pallas kernels  5.38 us (22%)
  between operations  0.69 us (3%)
    ppermute x3, starting transfers between devices, on_device(): lax.ppermute(message, ('sub', 'lev'), crossed(way, lev_count))  4.14 us
    ppermute x2, waiting for transfers between devices, on_device(): lax.ppermute(block, 'lev', [(i, i ^ 2 * size - 1) for i in range(lev_coun...  3.35 us
    ppermute x1, starting transfers between devices, on_device(): from_west = lax.ppermute(east, 'sub', ring)  3.08 us
    ppermute x3, waiting for transfers between devices, on_device(): lax.ppermute(message, ('sub', 'lev'), crossed(way, lev_count))  2.73 us
    ppermute x1, starting transfers between devices, on_device(): from_east = lax.ppermute(west, 'sub', [(b, a) for a, b in ring])  2.09 us
    ppermute x2, starting transfers between devices, on_device(): lax.ppermute(block, 'lev', [(i, i ^ 2 * size - 1) for i in range(lev_coun...  1.5 us
    pallas_call x1, Pallas kernels, on_device(): pl.pallas_call(surface_kernel, out_shape=(jax.ShapeDtypeStruct(tracer.sha...  1.31 us
    pallas_call x1, Pallas kernels, on_device(): pl.pallas_call(pack_kernel, out_shape=(levels, levels, marks, in_vmem(16,...  1.23 us
  transfers between devices with their start and end apart: 8, of which 7 were waited for; matrix products, arithmetic and copies ran while one was open for 0% of the time, Pallas kernels for 9%

profile of v5, /device:TPU:0, one launch (start us, length us, event | category | flops | bytes accessed | tf_op | source)
XLA Modules:
  0.0 24.8 jit_solution(14403670588531715814)
XLA Ops:
  0.6 0.0 copy-start
  0.6 1.2 %pack.1 = (f32[12,32,128]{2,1,0:T(8,128)S(1)}, f32[12,32,128]{2,1,0:T(8,128)S(1)}, s32[32,128]{1,0:T(8,128)S(1)}, f32[16,128]{1,0:T(8,128)S(1)}, f32[16,128]{1,0:T(8,128)S(1)}, /*index=5*/f32[16,128]{1,0:T(8,128)S(1)}) custom-call(f32[12,32,128]{2,1,0:T(8,128)} %tracer_hbm.1, f32[12,32,128]{2,1,0:T(8,128)} %zonal_hbm.1, s32[32,128]{1,0:T(8,128)} %wet_hbm.1), custom_call_target="tpu_custom_call" | custom-call | tf_op jit(solution)/shard_map/pack/pallas_call | solution.py:444
  1.9 3.1 %collective-permute-start = (f32[16,128]{1,0:T(8,128)S(1)}, f32[16,128]{1,0:T(8,128)S(1)}, u32[]{:S(2)}, u32[]{:S(2)}) collective-permute-start(f32[16,128]{1,0:T(8,128)S(1)} %get-tuple-element.34), channel_id=1, source_target_pairs={{0,4},{4,8},{8,12},{12,0},{1,5},{5,9},{9,13},{13,1},{2,6},{6,10},{... | collective-permute-start | bytes 24584 | tf_op jit(solution)/shard_map/ppermute | solution.py:453
  5.0 2.1 %collective-permute-start.1 = (f32[16,128]{1,0:T(8,128)S(1)}, f32[16,128]{1,0:T(8,128)S(1)}, u32[]{:S(2)}, u32[]{:S(2)}) collective-permute-start(f32[16,128]{1,0:T(8,128)S(1)} %get-tuple-element.35), channel_id=1, source_target_pairs={{4,0},{8,4},{12,8},{0,12},{5,1},{9,5},{13,9},{1,13},{6,2},{10,6},{... | collective-permute-start | bytes 24584 | tf_op jit(solution)/shard_map/ppermute | solution.py:454
  7.0 0.0 copy-done
  7.1 0.0 copy-start.1
  7.1 1.1 %prepare.1 = (f32[48,128]{1,0:T(8,128)S(1)}, f32[32,128]{1,0:T(8,128)S(1)}, f32[16,128]{1,0:T(8,128)S(1)}, f32[12,32,128]{2,1,0:T(8,128)S(1)}) custom-call(f32[48]{0:T(128)} %thick_ref.1, s32[32,128]{1,0:T(8,128)S(1)} %get-tuple-element.27.wet_ref, f32[12,32,128]{2,1,0:T(8,128)S(1)} %get-tuple-element.28.tracer_ref, ...), custom_call_target="tpu_custom_call" | custom-call | tf_op jit(solution)/shard_map/prepare/pallas_call | solution.py:455
  8.1 0.6 %collective-permute-done.from_west_ref = f32[16,128]{1,0:T(8,128)S(1)} collective-permute-done((f32[16,128]{1,0:T(8,128)S(1)}, f32[16,128]{1,0:T(8,128)S(1)}, u32[]{:S(2)}, u32[]{:S(2)}) %collective-permute-start) | collective-permute-done | bytes 8224 | tf_op jit(solution)/shard_map/ppermute | solution.py:453
  8.7 0.0 collective-permute-done.1.from_east_ref
  8.7 0.0 copy-done.1
  8.7 0.4 %local.1 = (f32[384,128]{1,0:T(8,128)S(1)}, f32[12,32,128]{2,1,0:T(8,128)S(1)}, f32[12,32,128]{2,1,0:T(8,128)S(1)}, f32[12,32,128]{2,1,0:T(8,128)S(1)}, f32[12,3...) custom-call(f32[48,128]{1,0:T(8,128)S(1)} %get-tuple-element.30.thick_ref, s32[32,128]{1,0:T(8,128)S(1)} %get-tuple-element.27.wet_ref, ...), custom_call_target="tpu_custom_call" | custom-call | tf_op jit(solution)/shard_map/local/pallas_call | solution.py:463
  9.1 0.1 collective-permute-start.2
  9.2 1.4 %collective-permute-done.2.other_ref = f32[384,128]{1,0:T(8,128)S(1)} collective-permute-done((f32[384,128]{1,0:T(8,128)S(1)}, f32[384,128]{1,0:T(8,128)S(1)}, u32[]{:S(2)}, u32[]{:S(2)}) %collective-permute-start.2) | collective-permute-done | bytes 196640 | tf_op jit(solution)/shard_map/ppermute | solution.py:480
  10.6 0.1 merge.1
  10.7 1.4 %collective-permute-start.3 = (f32[192,128]{1,0:T(8,128)S(1)}, f32[192,128]{1,0:T(8,128)S(1)}, u32[]{:S(2)}, u32[]{:S(2)}) collective-permute-start(f32[192,128]{1,0:T(8,128)S(1)} %get-tuple-element.37.mine_ref), channel_id=1, source_target_pairs={{0,3},{1,2},{2,1},{3,0},{4,7},{5,6},{6,5},{7,4},{8,11},{9,10},{10,... | collective-permute-start | bytes 294920 | tf_op jit(solution)/shard_map/ppermute | solution.py:480
  12.1 0.2 edges.1.edges_ref
  12.3 0.4 %collective-permute-start.4 = (f32[24,128]{1,0:T(8,128)S(1)}, f32[24,128]{1,0:T(8,128)S(1)}, u32[]{:S(2)}, u32[]{:S(2)}) collective-permute-start(f32[24,128]{1,0:T(8,128)S(1)} %edges.1.edges_ref), channel_id=1, source_target_pairs={{0,1},{1,0},{2,3},{3,2},{4,5},{5,4},{6,7},{7,6},{8,9},{9,8},{10,11... | collective-permute-start | bytes 36872 | tf_op jit(solution)/shard_map/ppermute | solution.py:473
  12.8 0.8 %collective-permute-done.4.other_edges_ref = f32[24,128]{1,0:T(8,128)S(1)} collective-permute-done((f32[24,128]{1,0:T(8,128)S(1)}, f32[24,128]{1,0:T(8,128)S(1)}, u32[]{:S(2)}, u32[]{:S(2)}) %collective-permute-start.4) | collective-permute-done | bytes 12320 | tf_op jit(solution)/shard_map/ppermute | solution.py:473
  13.6 1.9 %collective-permute-done.3.other_ref = f32[192,128]{1,0:T(8,128)S(1)} collective-permute-done((f32[192,128]{1,0:T(8,128)S(1)}, f32[192,128]{1,0:T(8,128)S(1)}, u32[]{:S(2)}, u32[]{:S(2)}) %collective-permute-start.3) | collective-permute-done | bytes 98336 | tf_op jit(solution)/shard_map/ppermute | solution.py:480
  15.5 0.1 final.1
  15.7 2.3 %collective-permute-start.7 = (f32[80,128]{1,0:T(8,128)S(1)}, f32[80,128]{1,0:T(8,128)S(1)}, u32[]{:S(2)}, u32[]{:S(2)}) collective-permute-start(f32[80,128]{1,0:T(8,128)S(1)} %get-tuple-element.47), channel_id=1, source_target_pairs={{0,9},{1,8},{2,11},{3,10},{4,13},{5,12},{6,15},{7,14},{8,5},{9,4},... | collective-permute-start | bytes 122888 | tf_op jit(solution)/shard_map/ppermute | solution.py:503
  18.0 1.4 %collective-permute-start.6 = (f32[80,128]{1,0:T(8,128)S(1)}, f32[80,128]{1,0:T(8,128)S(1)}, u32[]{:S(2)}, u32[]{:S(2)}) collective-permute-start(f32[80,128]{1,0:T(8,128)S(1)} %get-tuple-element.47), channel_id=1, source_target_pairs={{0,13},{1,12},{2,15},{3,14},{4,9},{5,8},{6,11},{7,10},{8,1},{9,0},... | collective-permute-start | bytes 122888 | tf_op jit(solution)/shard_map/ppermute | solution.py:503
  19.3 0.5 %collective-permute-start.5 = (f32[80,128]{1,0:T(8,128)S(1)}, f32[80,128]{1,0:T(8,128)S(1)}, u32[]{:S(2)}, u32[]{:S(2)}) collective-permute-start(f32[80,128]{1,0:T(8,128)S(1)} %get-tuple-element.47), channel_id=1, source_target_pairs={{0,5},{1,4},{2,7},{3,6},{4,1},{5,0},{6,3},{7,2},{8,13},{9,12},{10,... | collective-permute-start | bytes 122888 | tf_op jit(solution)/shard_map/ppermute | solution.py:503
  19.8 0.9 %rest.1 = (f32[12,32,128]{2,1,0:T(8,128)}, f32[12,32,128]{2,1,0:T(8,128)S(1)}) custom-call(f32[48,128]{1,0:T(8,128)S(1)} %get-tuple-element.30.thick_ref, s32[32,128]{1,0:T(8,128)S(1)} %get-tuple-element.27.wet_ref, f32[4,32,128]{2,1,0:T(8,128)S(1)} %get-tuple-element.43.ends_ref, f32[12,32,128]{2,1,0:T(8,128)S(1)} %get-tuple-element.44.forward_ref, ...), custom_call_target="tpu_custom_call" | custom-call | tf_op jit(solution)/shard_map/rest/pallas_call | solution.py:512
  20.8 0.2 collective-permute-done.7
  21.0 1.4 %collective-permute-done.6 = f32[80,128]{1,0:T(8,128)S(1)} collective-permute-done((f32[80,128]{1,0:T(8,128)S(1)}, f32[80,128]{1,0:T(8,128)S(1)}, u32[]{:S(2)}, u32[]{:S(2)}) %collective-permute-start.6) | collective-permute-done | bytes 40992 | tf_op jit(solution)/shard_map/ppermute | solution.py:503
  22.3 1.2 %collective-permute-done.5 = f32[80,128]{1,0:T(8,128)S(1)} collective-permute-done((f32[80,128]{1,0:T(8,128)S(1)}, f32[80,128]{1,0:T(8,128)S(1)}, u32[]{:S(2)}, u32[]{:S(2)}) %collective-permute-start.5) | collective-permute-done | bytes 40992 | tf_op jit(solution)/shard_map/ppermute | solution.py:503
  23.5 1.3 %surface.1 = (f32[12,32,128]{2,1,0:T(8,128)}, f32[32,128]{1,0:T(8,128)}) custom-call(f32[4,80,128]{2,1,0:T(8,128)S(1)} %pad_maximum_fusion.gathered_ref, f32[12,32,128]{2,1,0:T(8,128)S(1)} %get-tuple-element.48.inner_ref, f32[8,128]{1,0:T(8,128)S(1)} %get-tuple-element.45.factor_ref), custom_call_target="tpu_custom_call" | custom-call | tf_op jit(solution)/shard_map/surface/pallas_call | solution.py:520
  (1 shorter events, 0.0 us)
Async XLA Ops:
  0.6 6.4 %copy-start = (f32[12,32,128]{2,1,0:T(8,128)S(1)}, f32[12,32,128]{2,1,0:T(8,128)}, u32[]{:S(2)}) copy-start(f32[12,32,128]{2,1,0:T(8,128)} %merid_ref.3) | copy-start | bytes 589828
  1.9 6.8 %collective-permute-start = (f32[16,128]{1,0:T(8,128)S(1)}, f32[16,128]{1,0:T(8,128)S(1)}, u32[]{:S(2)}, u32[]{:S(2)}) collective-permute-start(f32[16,128]{1,0:T(8,128)S(1)} %get-tuple-element.34), channel_id=1, source_target_pairs={{0,4},{4,8},{8,12},{12,0},{1,5},{5,9},{9,13},{13,1},{2,6},{6,10},{... | collective-permute-start | bytes 24584 | tf_op jit(solution)/shard_map/ppermute | solution.py:453
  5.0 3.7 %collective-permute-start.1 = (f32[16,128]{1,0:T(8,128)S(1)}, f32[16,128]{1,0:T(8,128)S(1)}, u32[]{:S(2)}, u32[]{:S(2)}) collective-permute-start(f32[16,128]{1,0:T(8,128)S(1)} %get-tuple-element.35), channel_id=1, source_target_pairs={{4,0},{8,4},{12,8},{0,12},{5,1},{9,5},{13,9},{1,13},{6,2},{10,6},{... | collective-permute-start | bytes 24584 | tf_op jit(solution)/shard_map/ppermute | solution.py:454
  7.1 1.7 %copy-start.1 = (f32[12,32,128]{2,1,0:T(8,128)S(1)}, f32[12,32,128]{2,1,0:T(8,128)}, u32[]{:S(2)}) copy-start(f32[12,32,128]{2,1,0:T(8,128)} %cot_ref.1) | copy-start | bytes 589828
  9.1 1.5 %collective-permute-start.2 = (f32[384,128]{1,0:T(8,128)S(1)}, f32[384,128]{1,0:T(8,128)S(1)}, u32[]{:S(2)}, u32[]{:S(2)}) collective-permute-start(f32[384,128]{1,0:T(8,128)S(1)} %get-tuple-element.36.mine_ref), channel_id=1, source_target_pairs={{0,1},{1,0},{2,3},{3,2},{4,5},{5,4},{6,7},{7,6},{8,9},{9,8},{10,11... | collective-permute-start | bytes 589832 | tf_op jit(solution)/shard_map/ppermute | solution.py:480
  10.7 4.8 %collective-permute-start.3 = (f32[192,128]{1,0:T(8,128)S(1)}, f32[192,128]{1,0:T(8,128)S(1)}, u32[]{:S(2)}, u32[]{:S(2)}) collective-permute-start(f32[192,128]{1,0:T(8,128)S(1)} %get-tuple-element.37.mine_ref), channel_id=1, source_target_pairs={{0,3},{1,2},{2,1},{3,0},{4,7},{5,6},{6,5},{7,4},{8,11},{9,10},{10,... | collective-permute-start | bytes 294920 | tf_op jit(solution)/shard_map/ppermute | solution.py:480
  12.3 1.3 %collective-permute-start.4 = (f32[24,128]{1,0:T(8,128)S(1)}, f32[24,128]{1,0:T(8,128)S(1)}, u32[]{:S(2)}, u32[]{:S(2)}) collective-permute-start(f32[24,128]{1,0:T(8,128)S(1)} %edges.1.edges_ref), channel_id=1, source_target_pairs={{0,1},{1,0},{2,3},{3,2},{4,5},{5,4},{6,7},{7,6},{8,9},{9,8},{10,11... | collective-permute-start | bytes 36872 | tf_op jit(solution)/shard_map/ppermute | solution.py:473
  15.7 5.3 %collective-permute-start.7 = (f32[80,128]{1,0:T(8,128)S(1)}, f32[80,128]{1,0:T(8,128)S(1)}, u32[]{:S(2)}, u32[]{:S(2)}) collective-permute-start(f32[80,128]{1,0:T(8,128)S(1)} %get-tuple-element.47), channel_id=1, source_target_pairs={{0,9},{1,8},{2,11},{3,10},{4,13},{5,12},{6,15},{7,14},{8,5},{9,4},... | collective-permute-start | bytes 122888 | tf_op jit(solution)/shard_map/ppermute | solution.py:503
  18.0 4.3 %collective-permute-start.6 = (f32[80,128]{1,0:T(8,128)S(1)}, f32[80,128]{1,0:T(8,128)S(1)}, u32[]{:S(2)}, u32[]{:S(2)}) collective-permute-start(f32[80,128]{1,0:T(8,128)S(1)} %get-tuple-element.47), channel_id=1, source_target_pairs={{0,13},{1,12},{2,15},{3,14},{4,9},{5,8},{6,11},{7,10},{8,1},{9,0},... | collective-permute-start | bytes 122888 | tf_op jit(solution)/shard_map/ppermute | solution.py:503
  19.3 4.1 %collective-permute-start.5 = (f32[80,128]{1,0:T(8,128)S(1)}, f32[80,128]{1,0:T(8,128)S(1)}, u32[]{:S(2)}, u32[]{:S(2)}) collective-permute-start(f32[80,128]{1,0:T(8,128)S(1)} %get-tuple-element.47), channel_id=1, source_target_pairs={{0,5},{1,4},{2,7},{3,6},{4,1},{5,0},{6,3},{7,2},{8,13},{9,12},{10,... | collective-permute-start | bytes 122888 | tf_op jit(solution)/shard_map/ppermute | solution.py:503

commit v6 on v5

--- a/solution.py
+++ b/solution.py
@@ -109,10 +109,19 @@
     east = fold_edges([tracer_ref[k] for k in range(own)])
     copies[1].wait()
     zonal = fold_edges([zonal_ref[k] for k in range(own)])
+    copies[2].wait()
     for ref in (east_ref, west_ref, edges_ref):
         ref[:8] = east
-        ref[8:] = zonal
-    copies[2].wait()
+        ref[8:16] = zonal
+        ref[16:] = wet_ref[...].astype(jnp.float32)
+
+
+def damping_of(wet_levels, thick_ref):
+    level_count = thick_ref.shape[0]
+    depth = jnp.zeros(wet_levels.shape, jnp.float32)
+    for k in range(level_count):
+        depth = depth + jnp.where(wet_levels > k, thick_ref[k : k + 1], 0.0)
+    return 0.3 + depth / level_count
 
 
 def prepare_kernel(
@@ -121,12 +130,9 @@
     level_count = thick_ref.shape[0]
     rows, width = wet_ref.shape
     wet_levels = wet_ref[...]
-    depth = jnp.zeros((rows, width), jnp.float32)
     for k in range(level_count):
-        thick = splat(thick_ref[k], width)
-        rows_ref[k : k + 1] = thick
-        depth = depth + jnp.where(wet_levels > k, thick, 0.0)
-    damping_ref[...] = 0.3 + depth / level_count
+        rows_ref[k : k + 1] = splat(thick_ref[k], width)
+    damping_ref[...] = damping_of(wet_levels, rows_ref)
     wet_edges = fold_surface(wet_levels)
     offset = lax.rem(lanes(8, width), width // (rows // 8)) // 2
     place = lax.axis_index("lev")
@@ -158,7 +164,7 @@
     at_edge = jnp.logical_or(lane == 0, lane == width - 1)
     even = parity(width) == 0
     wet_levels = wet_ref[...]
-    factor = HALF_STEP * jnp.where(even, turn(from_east_ref[8:], -1, 1), -edges_ref[8:])
+    factor = HALF_STEP * jnp.where(even, turn(from_east_ref[8:16], -1, 1), -edges_ref[8:16])
     factor_ref[...] = factor
     beside = beside_edges(from_west_ref[:8], from_east_ref[:8])
     beside = -factor * jnp.where(even, edges_ref[:8] + beside, beside)
@@ -286,7 +292,7 @@
 
 
 def final_kernel(
-    sizes, own, thick_ref, wet_ref, weight_ref, mine_ref, other_ref, edges_ref, other_edges_ref, damping_ref, *rest
+    sizes, own, thick_ref, wet_ref, weight_ref, mine_ref, other_ref, edges_ref, damping_ref, *rest
 ):
     flux_refs, message_ref, ends_ref = rest[:-2], rest[-2], rest[-1]
     rows, width = wet_ref.shape
@@ -306,7 +312,8 @@
     in_forward = rate * (other[1] - mine[1])
     in_adjoint = rate * (other[2] - mine[2])
     message_ref[:rows] = mine[4] + other[4] + in_adjoint * (mine[5] - other[5])
-    message_ref[rows + 16 :] = damping_ref[...]
+    if message_ref.shape[0] > rows + 8:
+        message_ref[rows + 8 :] = damping_ref[...]
     even = lax.rem(place, 2) == 0
     pair = []
     for into, index in ((in_forward, 0), (in_adjoint, 1)):
@@ -321,16 +328,17 @@
             top, bottom = jnp.where(above, top, -flux), jnp.where(above, flux, bottom)
         ends_ref[2 * index] = top
         ends_ref[2 * index + 1] = bottom
-    for i, (top, bottom) in enumerate(pair):
-        is_mine = even if i == 0 else jnp.logical_not(even)
-        edges = jnp.where(is_mine, edges_ref[...], other_edges_ref[...])
-        mixed = edges[:8] + edges[8:16] * fold_surface(top) + edges[16:] * fold_surface(bottom)
-        message_ref[rows + 8 * i : rows + 8 * i + 8] = weight_ref[8 * i : 8 * i + 8] * mixed
+    (top_above, bottom_above), (top_below, bottom_below) = pair
+    top = jnp.where(even, top_below, top_above)
+    bottom = jnp.where(even, bottom_below, bottom_above)
+    mixed = edges_ref[:8] + edges_ref[8:16] * fold_surface(top) + edges_ref[16:] * fold_surface(bottom)
+    weight = jnp.where(even, weight_ref[8:], weight_ref[:8])
+    message_ref[rows : rows + 8] = weight * mixed
 
 
 def rest_kernel(
     thick_ref, wet_ref, ends_ref, forward_ref, adjoint_ref, top_ref, bottom_ref, zonal_ref, merid_ref, factor_ref,
-    next_tracer_ref, inner_ref,
+    from_west_ref, from_east_ref, next_tracer_ref, inner_ref, beside_ref,
 ):
     own, rows, width = forward_ref.shape
     first = lax.axis_index("lev") * own
@@ -338,6 +346,8 @@
     wet_levels = wet_ref[...]
     ends = [ends_ref[i] for i in range(4)]
     factor = factor_ref[...]
+    beside_ref[0] = damping_of(from_west_ref[16:], thick_ref)
+    beside_ref[1] = damping_of(from_east_ref[16:], thick_ref)
     for k in range(own):
         next_tracer_ref[k] = forward_ref[k] + top_ref[k] * ends[0] + bottom_ref[k] * ends[1]
         mixed = adjoint_ref[k] + top_ref[k] * ends[2] + bottom_ref[k] * ends[3]
@@ -359,7 +369,7 @@
 
 def routes(count):
     if count == 4:
-        return [[2, 3, 1, 0], [3, 2, 0, 1], [1, 0, 3, 2]]
+        return [[1, 3, 0, 2], [3, 2, 1, 0], [2, 0, 3, 1]]
     return [[i ^ away for i in range(count)] for away in range(1, count)]
 
 
@@ -375,19 +385,22 @@
 
 
 def surface_kernel(
-    gathered_ref, inner_ref, factor_ref, tracer_adjoint_ref, surface_ref,
+    gathered_ref, damping_ref, beside_ref, far_ref, inner_ref, factor_ref, tracer_adjoint_ref, surface_ref,
     source_scr, damping_scr, edges_scr,
 ):
     own, rows, width = inner_ref.shape
     count = gathered_ref.shape[0]
     place = lax.axis_index("sub")
-    even = lax.rem(lax.axis_index("lev"), 2) == 0
-    ways = [list(range(count))] + routes(count)[:: -1 if count == 4 else 1]
+    ways = [list(range(count))] + routes(count)[::-1]
     for i, route in enumerate(ways):
         owner = owner_of(route, place)
         source_scr[owner] = gathered_ref[i, :rows]
-        damping_scr[owner] = gathered_ref[i, rows + 16 :]
-        edges_scr[owner] = jnp.where(even, gathered_ref[i, rows : rows + 8], gathered_ref[i, rows + 8 : rows + 16])
+        if gathered_ref.shape[1] > rows + 8:
+            damping_scr[owner] = gathered_ref[i, rows + 8 :]
+        edges_scr[owner] = gathered_ref[i, rows : rows + 8]
+    if gathered_ref.shape[1] == rows + 8:
+        for away, field in ((0, damping_ref[...]), (3, beside_ref[0]), (1, beside_ref[1]), (2, far_ref[...])):
+            damping_scr[lax.rem(place + away, count)] = field
     west_edges = edges_scr[lax.rem(place + count - 1, count)]
     east_edges = edges_scr[lax.rem(place + 1, count)]
     beside = factor_ref[...] * beside_edges(west_edges, east_edges)
@@ -438,12 +451,13 @@
     sub_count = lax.axis_size("sub")
     edge = in_vmem(rows, width)
     levels = in_vmem(own, rows, width)
+    message_rows = in_vmem(16 + rows, width)
     marks = pltpu.VMEM((rows, width), jnp.int32)
     thickness = pltpu.with_memory_space_constraint(thickness, pltpu.SMEM)
 
     tracer, zonal_flow, wet_levels, east, west, edges = pl.pallas_call(
         pack_kernel,
-        out_shape=(levels, levels, marks, in_vmem(16, width), in_vmem(16, width), in_vmem(16, width)),
+        out_shape=(levels, levels, marks, message_rows, message_rows, message_rows),
         in_specs=[pl.BlockSpec(memory_space=pl.ANY)] * 3,
         out_specs=(VMEM_IN,) * 6,
         scratch_shapes=[pltpu.SemaphoreType.DMA((3,))],
@@ -480,6 +494,8 @@
         other = lax.ppermute(block, "lev", [(i, i ^ (2 * size - 1)) for i in range(lev_count)])
         if size == sizes[-1]:
             break
+        if size == 1:
+            other, other_edges = lax.optimization_barrier((other, other_edges))
         final = size * 2 == sizes[-1]
         block, flux = pl.pallas_call(
             functools.partial(merge_kernel, size, final, own),
@@ -490,32 +506,41 @@
         )(*near(thickness, wet_levels, block, other))
         fluxes.append(flux)
 
+    lean = sub_count == 4
+    far = damping
+    if lean:
+        _, far = lax.optimization_barrier((edges, damping))
+        far = lax.ppermute(far, ("sub", "lev"), crossed([i ^ 2 for i in range(sub_count)], lev_count))
     message, ends = pl.pallas_call(
         functools.partial(final_kernel, sizes, own),
-        out_shape=(in_vmem(2 * rows + 16, width), in_vmem(4, rows, width)),
-        in_specs=[VMEM_IN] * (8 + len(fluxes)),
+        out_shape=(in_vmem((rows if lean else 2 * rows) + 8, width), in_vmem(4, rows, width)),
+        in_specs=[VMEM_IN] * (7 + len(fluxes)),
         out_specs=(VMEM_IN,) * 2,
         name="final",
-    )(*near(thickness, wet_levels, weights, block, other, edges, other_edges, damping, *fluxes))
-
-    if sub_count == 4:
-        gathered = jnp.stack(
-            [message] + [lax.ppermute(message, ("sub", "lev"), crossed(way, lev_count)) for way in routes(sub_count)[::-1]]
-        )
-    else:
-        gathered = message[None]
-        while gathered.shape[0] < sub_count:
-            size = gathered.shape[0]
-            got = lax.ppermute(gathered, "sub", [(i, i ^ size) for i in range(sub_count)])
-            gathered = jnp.concatenate([gathered, got])
-
-    next_tracer, inner = pl.pallas_call(
+    )(*near(thickness, wet_levels, weights, block, other, other_edges, damping, *fluxes))
+
+    ways = routes(sub_count)[::-1]
+    last = message
+    if lean:
+        last, far = lax.optimization_barrier((message, far))
+    gathered = jnp.stack(
+        [message]
+        + [
+            lax.ppermute(message if i else last, ("sub", "lev"), crossed(way, lev_count))
+            for i, way in enumerate(ways)
+        ]
+    )
+
+    next_tracer, inner, beside = pl.pallas_call(
         rest_kernel,
-        out_shape=(jax.ShapeDtypeStruct(tracer.shape, jnp.float32), levels),
-        in_specs=[VMEM_IN] * 10,
-        out_specs=(VMEM_IN,) * 2,
+        out_shape=(jax.ShapeDtypeStruct(tracer.shape, jnp.float32), levels, in_vmem(2, rows, width)),
+        in_specs=[VMEM_IN] * 12,
+        out_specs=(VMEM_IN,) * 3,
         name="rest",
-    )(*near(thickness, wet_levels, ends, forward, adjoint, top, bottom, zonal_flow, meridional_flow, factor))
+    )(
+        *near(thickness, wet_levels, ends, forward, adjoint, top, bottom, zonal_flow, meridional_flow, factor),
+        *near(from_west, from_east),
+    )
 
     tracer_adjoint, surface = pl.pallas_call(
         surface_kernel,
@@ -523,12 +548,12 @@
             jax.ShapeDtypeStruct(tracer.shape, jnp.float32),
             jax.ShapeDtypeStruct((rows, width), jnp.float32),
         ),
-        in_specs=[VMEM_IN] * 3,
+        in_specs=[VMEM_IN] * 6,
         out_specs=(VMEM_IN,) * 2,
         scratch_shapes=[pltpu.VMEM((sub_count, rows, width), jnp.float32)] * 2
         + [pltpu.VMEM((sub_count, 8, width), jnp.float32)],
         name="surface",
-    )(*near(gathered, inner, factor))
+    )(*near(gathered, damping, beside, far, inner, factor))
     return (next_tracer, tracer_adjoint, surface)
 
 

time: 25 us -> 24.4 us (0.976)
  waiting for transfers between devices: 7.49 us -> 3.33 us
  starting transfers between devices: 11.2 us -> 14.7 us
    ppermute x3 -> x4, starting transfers between devices: 4.14 us -> 7.4 us  [the longest x3 5.31 us: on_device(): lax.ppermute(message if i else last, ('sub', 'lev'), crossed(way, lev_cou...]
    ppermute x3 -> x4, waiting for transfers between devices: 2.73 us -> 0.48 us  [the longest x3 0.48 us: on_device(): lax.ppermute(message if i else last, ('sub', 'lev'), crossed(way, lev_cou...]
    ppermute x2, waiting for transfers between devices: 3.35 us -> 1.1 us  [on_device(): lax.ppermute(block, 'lev', [(i, i ^ 2 * size - 1) for i in range(lev_coun...]
  transfers between devices with their start and end apart: 8 -> 9, of which waited for: 7 -> 5; matrix products, arithmetic and copies ran while one was open for 0% -> 0% of each run, Pallas kernels for 9% -> 10%
where the time goes in v6:
time: 24.4 us; the launch traced here: 24.3 us
  starting transfers between devices  14.7 us (60%)
  Pallas kernels  5.54 us (23%)
  waiting for transfers between devices  3.33 us (14%)
  between operations  0.69 us (3%)
    ppermute x3, starting transfers between devices, on_device(): lax.ppermute(message if i else last, ('sub', 'lev'), crossed(way, lev_cou...  5.31 us
    ppermute x1, starting transfers between devices, on_device(): from_west = lax.ppermute(east, 'sub', ring)  3.08 us
    ppermute x1, starting transfers between devices, on_device(): lax.ppermute(far, ('sub', 'lev'), crossed([i ^ 2 for i in range(sub_count...  2.09 us
    ppermute x1, starting transfers between devices, on_device(): from_east = lax.ppermute(west, 'sub', [(b, a) for a, b in ring])  2.09 us
    ppermute x2, starting transfers between devices, on_device(): lax.ppermute(block, 'lev', [(i, i ^ 2 * size - 1) for i in range(lev_coun...  1.58 us
    pallas_call x1, Pallas kernels, on_device(): pl.pallas_call(surface_kernel, out_shape=(jax.ShapeDtypeStruct(tracer.sha...  1.3 us
    pallas_call x1, Pallas kernels, on_device(): pl.pallas_call(pack_kernel, out_shape=(levels, levels, marks, message_row...  1.24 us
    ppermute x2, waiting for transfers between devices, on_device(): lax.ppermute(block, 'lev', [(i, i ^ 2 * size - 1) for i in range(lev_coun...  1.1 us
  transfers between devices with their start and end apart: 9, of which 5 were waited for; matrix products, arithmetic and copies ran while one was open for 0% of the time, Pallas kernels for 10%

profile of v6, /device:TPU:0, one launch (start us, length us, event | category | flops | bytes accessed | tf_op | source)
XLA Modules:
  0.0 24.3 jit_solution(7738146654915712983)
XLA Ops:
  0.6 0.0 copy-start
  0.6 1.2 %pack.1 = (f32[12,32,128]{2,1,0:T(8,128)S(1)}, f32[12,32,128]{2,1,0:T(8,128)S(1)}, s32[32,128]{1,0:T(8,128)S(1)}, f32[48,128]{1,0:T(8,128)S(1)}, f32[48,128]{1,0:T(8,128)S(1)}, /*index=5*/f32[48,128]{1,0:T(8,128)S(1)}) custom-call(f32[12,32,128]{2,1,0:T(8,128)} %tracer_hbm.1, f32[12,32,128]{2,1,0:T(8,128)} %zonal_hbm.1, s32[32,128]{1,0:T(8,128)} %wet_hbm.1), custom_call_target="tpu_custom_call" | custom-call | tf_op jit(solution)/shard_map/pack/pallas_call | solution.py:458
  1.9 3.1 %collective-permute-start = (f32[48,128]{1,0:T(8,128)S(1)}, f32[48,128]{1,0:T(8,128)S(1)}, u32[]{:S(2)}, u32[]{:S(2)}) collective-permute-start(f32[48,128]{1,0:T(8,128)S(1)} %get-tuple-element.40), channel_id=1, source_target_pairs={{0,4},{4,8},{8,12},{12,0},{1,5},{5,9},{9,13},{13,1},{2,6},{6,10},{... | collective-permute-start | bytes 73736 | tf_op jit(solution)/shard_map/ppermute | solution.py:467
  5.0 2.1 %collective-permute-start.1 = (f32[48,128]{1,0:T(8,128)S(1)}, f32[48,128]{1,0:T(8,128)S(1)}, u32[]{:S(2)}, u32[]{:S(2)}) collective-permute-start(f32[48,128]{1,0:T(8,128)S(1)} %get-tuple-element.41), channel_id=1, source_target_pairs={{4,0},{8,4},{12,8},{0,12},{5,1},{9,5},{13,9},{1,13},{6,2},{10,6},{... | collective-permute-start | bytes 73736 | tf_op jit(solution)/shard_map/ppermute | solution.py:468
  7.1 0.0 copy-done
  7.1 0.0 copy-start.1
  7.1 1.1 %prepare.1 = (f32[48,128]{1,0:T(8,128)S(1)}, f32[32,128]{1,0:T(8,128)S(1)}, f32[16,128]{1,0:T(8,128)S(1)}, f32[12,32,128]{2,1,0:T(8,128)S(1)}) custom-call(f32[48]{0:T(128)} %thick_ref.1, s32[32,128]{1,0:T(8,128)S(1)} %get-tuple-element.33.wet_ref, f32[12,32,128]{2,1,0:T(8,128)S(1)} %get-tuple-element.34.tracer_ref, ...), custom_call_target="tpu_custom_call" | custom-call | tf_op jit(solution)/shard_map/prepare/pallas_call | solution.py:469
  8.1 0.8 %collective-permute-done.from_west_ref = f32[48,128]{1,0:T(8,128)S(1)} collective-permute-done((f32[48,128]{1,0:T(8,128)S(1)}, f32[48,128]{1,0:T(8,128)S(1)}, u32[]{:S(2)}, u32[]{:S(2)}) %collective-permute-start) | collective-permute-done | bytes 24608 | tf_op jit(solution)/shard_map/ppermute | solution.py:467
  8.9 0.2 collective-permute-done.1.from_east_ref
  9.1 0.0 copy-done.1
  9.1 0.4 %local.1 = (f32[384,128]{1,0:T(8,128)S(1)}, f32[12,32,128]{2,1,0:T(8,128)S(1)}, f32[12,32,128]{2,1,0:T(8,128)S(1)}, f32[12,32,128]{2,1,0:T(8,128)S(1)}, f32[12,3...) custom-call(f32[48,128]{1,0:T(8,128)S(1)} %get-tuple-element.36.thick_ref, s32[32,128]{1,0:T(8,128)S(1)} %get-tuple-element.33.wet_ref, ...), custom_call_target="tpu_custom_call" | custom-call | tf_op jit(solution)/shard_map/local/pallas_call | solution.py:477
  9.5 0.1 collective-permute-start.2
  9.6 0.2 edges.1
  9.8 0.6 %collective-permute-start.3 = (f32[24,128]{1,0:T(8,128)S(1)}, f32[24,128]{1,0:T(8,128)S(1)}, u32[]{:S(2)}, u32[]{:S(2)}) collective-permute-start(f32[24,128]{1,0:T(8,128)S(1)} %edges.1), channel_id=1, source_target_pairs={{0,1},{1,0},{2,3},{3,2},{4,5},{5,4},{6,7},{7,6},{8,9},{9,8},{10,11... | collective-permute-start | bytes 36872 | tf_op jit(solution)/shard_map/ppermute | solution.py:487
  10.3 0.8 %collective-permute-done.3.edges_ref = f32[24,128]{1,0:T(8,128)S(1)} collective-permute-done((f32[24,128]{1,0:T(8,128)S(1)}, f32[24,128]{1,0:T(8,128)S(1)}, u32[]{:S(2)}, u32[]{:S(2)}) %collective-permute-start.3) | collective-permute-done | bytes 12320 | tf_op jit(solution)/shard_map/ppermute | solution.py:487
  11.2 0.0 collective-permute-done.2.other_ref
  11.2 0.1 merge.1
  11.2 1.5 %collective-permute-start.4 = (f32[192,128]{1,0:T(8,128)S(1)}, f32[192,128]{1,0:T(8,128)S(1)}, u32[]{:S(2)}, u32[]{:S(2)}) collective-permute-start(f32[192,128]{1,0:T(8,128)S(1)} %get-tuple-element.47.mine_ref), channel_id=1, source_target_pairs={{0,3},{1,2},{2,1},{3,0},{4,7},{5,6},{6,5},{7,4},{8,11},{9,10},{10,... | collective-permute-start | bytes 294920 | tf_op jit(solution)/shard_map/ppermute | solution.py:494
  12.8 2.1 %collective-permute-start.5 = (f32[32,128]{1,0:T(8,128)S(1)}, f32[32,128]{1,0:T(8,128)S(1)}, u32[]{:S(2)}, u32[]{:S(2)}) collective-permute-start(f32[32,128]{1,0:T(8,128)S(1)} %get-tuple-element.56.damping_ref), channel_id=1, source_target_pairs={{0,9},{1,8},{2,11},{3,10},{4,13},{5,12},{6,15},{7,14},{8,1},{9,0},... | collective-permute-start | bytes 49160 | tf_op jit(solution)/shard_map/ppermute | solution.py:513
  14.9 1.1 %collective-permute-done.4.other_ref = f32[192,128]{1,0:T(8,128)S(1)} collective-permute-done((f32[192,128]{1,0:T(8,128)S(1)}, f32[192,128]{1,0:T(8,128)S(1)}, u32[]{:S(2)}, u32[]{:S(2)}) %collective-permute-start.4) | collective-permute-done | bytes 98336 | tf_op jit(solution)/shard_map/ppermute | solution.py:494
  16.0 0.1 final.1
  16.1 1.2 %collective-permute-start.8 = (f32[40,128]{1,0:T(8,128)S(1)}, f32[40,128]{1,0:T(8,128)S(1)}, u32[]{:S(2)}, u32[]{:S(2)}) collective-permute-start(f32[40,128]{1,0:T(8,128)S(1)} %get-tuple-element.57), channel_id=1, source_target_pairs={{0,5},{1,4},{2,7},{3,6},{4,13},{5,12},{6,15},{7,14},{8,1},{9,0},{1... | collective-permute-start | bytes 61448 | tf_op jit(solution)/shard_map/ppermute | solution.py:529
  17.3 2.4 %collective-permute-start.7 = (f32[40,128]{1,0:T(8,128)S(1)}, f32[40,128]{1,0:T(8,128)S(1)}, u32[]{:S(2)}, u32[]{:S(2)}) collective-permute-start(f32[40,128]{1,0:T(8,128)S(1)} %get-tuple-element.57), channel_id=1, source_target_pairs={{0,13},{1,12},{2,15},{3,14},{4,9},{5,8},{6,11},{7,10},{8,5},{9,4},... | collective-permute-start | bytes 61448 | tf_op jit(solution)/shard_map/ppermute | solution.py:529
  19.7 0.0 collective-permute-done.5.far_ref
  19.7 1.7 %collective-permute-start.6 = (f32[40,128]{1,0:T(8,128)S(1)}, f32[40,128]{1,0:T(8,128)S(1)}, u32[]{:S(2)}, u32[]{:S(2)}) collective-permute-start(f32[40,128]{1,0:T(8,128)S(1)} %get-tuple-element.57), channel_id=1, source_target_pairs={{0,9},{1,8},{2,11},{3,10},{4,1},{5,0},{6,3},{7,2},{8,13},{9,12},{1... | collective-permute-start | bytes 61448 | tf_op jit(solution)/shard_map/ppermute | solution.py:529
  21.4 1.1 %rest.1 = (f32[12,32,128]{2,1,0:T(8,128)}, f32[12,32,128]{2,1,0:T(8,128)S(1)}, f32[2,32,128]{2,1,0:T(8,128)S(1)}) custom-call(f32[48,128]{1,0:T(8,128)S(1)} %get-tuple-element.36.thick_ref, s32[32,128]{1,0:T(8,128)S(1)} %get-tuple-element.33.wet_ref, f32[4,32,128]{2,1,0:T(8,128)S(1)} %get-tuple-element.51.ends_ref, ...), custom_call_target="tpu_custom_call" | custom-call | tf_op jit(solution)/shard_map/rest/pallas_call | solution.py:534
  22.5 0.0 collective-permute-done.8
  22.5 0.0 collective-permute-done.7
  22.5 0.5 %collective-permute-done.6 = f32[40,128]{1,0:T(8,128)S(1)} collective-permute-done((f32[40,128]{1,0:T(8,128)S(1)}, f32[40,128]{1,0:T(8,128)S(1)}, u32[]{:S(2)}, u32[]{:S(2)}) %collective-permute-start.6) | collective-permute-done | bytes 20512 | tf_op jit(solution)/shard_map/ppermute | solution.py:529
  23.0 1.3 %surface.1 = (f32[12,32,128]{2,1,0:T(8,128)}, f32[32,128]{1,0:T(8,128)}) custom-call(f32[4,40,128]{2,1,0:T(8,128)S(1)} %pad_maximum_fusion.gathered_ref, f32[32,128]{1,0:T(8,128)S(1)} %get-tuple-element.56.damping_ref, f32[2,32,128]{2,1,0:T(8,128)S(1)} %get-tuple-element.58.beside_ref, f32[32,128]{1,0:T(8,128)S(1)} %collective-permute-done.5.far_ref, ...), custom_call_target="tpu_custom_call" | custom-call | tf_op jit(solution)/shard_map/surface/pallas_call | solution.py:545
  (1 shorter events, 0.0 us)
Async XLA Ops:
  0.6 6.4 %copy-start = (f32[12,32,128]{2,1,0:T(8,128)S(1)}, f32[12,32,128]{2,1,0:T(8,128)}, u32[]{:S(2)}) copy-start(f32[12,32,128]{2,1,0:T(8,128)} %merid_ref.3) | copy-start | bytes 589828
  1.9 7.0 %collective-permute-start = (f32[48,128]{1,0:T(8,128)S(1)}, f32[48,128]{1,0:T(8,128)S(1)}, u32[]{:S(2)}, u32[]{:S(2)}) collective-permute-start(f32[48,128]{1,0:T(8,128)S(1)} %get-tuple-element.40), channel_id=1, source_target_pairs={{0,4},{4,8},{8,12},{12,0},{1,5},{5,9},{9,13},{13,1},{2,6},{6,10},{... | collective-permute-start | bytes 73736 | tf_op jit(solution)/shard_map/ppermute | solution.py:467
  5.0 4.1 %collective-permute-start.1 = (f32[48,128]{1,0:T(8,128)S(1)}, f32[48,128]{1,0:T(8,128)S(1)}, u32[]{:S(2)}, u32[]{:S(2)}) collective-permute-start(f32[48,128]{1,0:T(8,128)S(1)} %get-tuple-element.41), channel_id=1, source_target_pairs={{4,0},{8,4},{12,8},{0,12},{5,1},{9,5},{13,9},{1,13},{6,2},{10,6},{... | collective-permute-start | bytes 73736 | tf_op jit(solution)/shard_map/ppermute | solution.py:468
  7.1 2.0 %copy-start.1 = (f32[12,32,128]{2,1,0:T(8,128)S(1)}, f32[12,32,128]{2,1,0:T(8,128)}, u32[]{:S(2)}) copy-start(f32[12,32,128]{2,1,0:T(8,128)} %cot_ref.1) | copy-start | bytes 589828
  9.5 1.7 %collective-permute-start.2 = (f32[384,128]{1,0:T(8,128)S(1)}, f32[384,128]{1,0:T(8,128)S(1)}, u32[]{:S(2)}, u32[]{:S(2)}) collective-permute-start(f32[384,128]{1,0:T(8,128)S(1)} %get-tuple-element.42.mine_ref), channel_id=1, source_target_pairs={{0,1},{1,0},{2,3},{3,2},{4,5},{5,4},{6,7},{7,6},{8,9},{9,8},{10,11... | collective-permute-start | bytes 589832 | tf_op jit(solution)/shard_map/ppermute | solution.py:494
  9.8 1.4 %collective-permute-start.3 = (f32[24,128]{1,0:T(8,128)S(1)}, f32[24,128]{1,0:T(8,128)S(1)}, u32[]{:S(2)}, u32[]{:S(2)}) collective-permute-start(f32[24,128]{1,0:T(8,128)S(1)} %edges.1), channel_id=1, source_target_pairs={{0,1},{1,0},{2,3},{3,2},{4,5},{5,4},{6,7},{7,6},{8,9},{9,8},{10,11... | collective-permute-start | bytes 36872 | tf_op jit(solution)/shard_map/ppermute | solution.py:487
  11.2 4.7 %collective-permute-start.4 = (f32[192,128]{1,0:T(8,128)S(1)}, f32[192,128]{1,0:T(8,128)S(1)}, u32[]{:S(2)}, u32[]{:S(2)}) collective-permute-start(f32[192,128]{1,0:T(8,128)S(1)} %get-tuple-element.47.mine_ref), channel_id=1, source_target_pairs={{0,3},{1,2},{2,1},{3,0},{4,7},{5,6},{6,5},{7,4},{8,11},{9,10},{10,... | collective-permute-start | bytes 294920 | tf_op jit(solution)/shard_map/ppermute | solution.py:494
  12.8 7.0 %collective-permute-start.5 = (f32[32,128]{1,0:T(8,128)S(1)}, f32[32,128]{1,0:T(8,128)S(1)}, u32[]{:S(2)}, u32[]{:S(2)}) collective-permute-start(f32[32,128]{1,0:T(8,128)S(1)} %get-tuple-element.56.damping_ref), channel_id=1, source_target_pairs={{0,9},{1,8},{2,11},{3,10},{4,13},{5,12},{6,15},{7,14},{8,1},{9,0},... | collective-permute-start | bytes 49160 | tf_op jit(solution)/shard_map/ppermute | solution.py:513
  16.1 6.4 %collective-permute-start.8 = (f32[40,128]{1,0:T(8,128)S(1)}, f32[40,128]{1,0:T(8,128)S(1)}, u32[]{:S(2)}, u32[]{:S(2)}) collective-permute-start(f32[40,128]{1,0:T(8,128)S(1)} %get-tuple-element.57), channel_id=1, source_target_pairs={{0,5},{1,4},{2,7},{3,6},{4,13},{5,12},{6,15},{7,14},{8,1},{9,0},{1... | collective-permute-start | bytes 61448 | tf_op jit(solution)/shard_map/ppermute | solution.py:529
  17.3 5.2 %collective-permute-start.7 = (f32[40,128]{1,0:T(8,128)S(1)}, f32[40,128]{1,0:T(8,128)S(1)}, u32[]{:S(2)}, u32[]{:S(2)}) collective-permute-start(f32[40,128]{1,0:T(8,128)S(1)} %get-tuple-element.57), channel_id=1, source_target_pairs={{0,13},{1,12},{2,15},{3,14},{4,9},{5,8},{6,11},{7,10},{8,5},{9,4},... | collective-permute-start | bytes 61448 | tf_op jit(solution)/shard_map/ppermute | solution.py:529
  19.7 3.3 %collective-permute-start.6 = (f32[40,128]{1,0:T(8,128)S(1)}, f32[40,128]{1,0:T(8,128)S(1)}, u32[]{:S(2)}, u32[]{:S(2)}) collective-permute-start(f32[40,128]{1,0:T(8,128)S(1)} %get-tuple-element.57), channel_id=1, source_target_pairs={{0,9},{1,8},{2,11},{3,10},{4,1},{5,0},{6,3},{7,2},{8,13},{9,12},{1... | collective-permute-start | bytes 61448 | tf_op jit(solution)/shard_map/ppermute | solution.py:529

commit v7 on v6

--- a/solution.py
+++ b/solution.py
@@ -113,7 +113,7 @@
     for ref in (east_ref, west_ref, edges_ref):
         ref[:8] = east
         ref[8:16] = zonal
-        ref[16:] = wet_ref[...].astype(jnp.float32)
+    east_ref[16:] = wet_ref[...].astype(jnp.float32)
 
 
 def damping_of(wet_levels, thick_ref):
@@ -229,9 +229,11 @@
         put(9 + i, sums[i])
 
 
-def edges_kernel(adjoint_ref, top_ref, bottom_ref, edges_ref):
+def edges_kernel(adjoint_ref, top_ref, bottom_ref, wet_ref, from_west_ref, edges_ref, wet_pair_ref):
     for i, ref in enumerate((adjoint_ref, top_ref, bottom_ref)):
         edges_ref[8 * i : 8 * i + 8] = fold_edges([ref[k] for k in range(ref.shape[0])])
+    wet_pair_ref[0] = wet_ref[...].astype(jnp.float32)
+    wet_pair_ref[1] = from_west_ref[16:]
 
 
 def merge_kernel(size, final, own, thick_ref, wet_ref, mine_ref, other_ref, block_ref, flux_ref):
@@ -338,7 +340,7 @@
 
 def rest_kernel(
     thick_ref, wet_ref, ends_ref, forward_ref, adjoint_ref, top_ref, bottom_ref, zonal_ref, merid_ref, factor_ref,
-    from_west_ref, from_east_ref, next_tracer_ref, inner_ref, beside_ref,
+    wet_pair_ref, far_ref, next_tracer_ref, inner_ref, dampings_ref,
 ):
     own, rows, width = forward_ref.shape
     first = lax.axis_index("lev") * own
@@ -346,8 +348,8 @@
     wet_levels = wet_ref[...]
     ends = [ends_ref[i] for i in range(4)]
     factor = factor_ref[...]
-    beside_ref[0] = damping_of(from_west_ref[16:], thick_ref)
-    beside_ref[1] = damping_of(from_east_ref[16:], thick_ref)
+    for i, wet_levels_there in enumerate((wet_pair_ref[1], far_ref[1], far_ref[0])):
+        dampings_ref[i] = damping_of(wet_levels_there, thick_ref)
     for k in range(own):
         next_tracer_ref[k] = forward_ref[k] + top_ref[k] * ends[0] + bottom_ref[k] * ends[1]
         mixed = adjoint_ref[k] + top_ref[k] * ends[2] + bottom_ref[k] * ends[3]
@@ -385,7 +387,7 @@
 
 
 def surface_kernel(
-    gathered_ref, damping_ref, beside_ref, far_ref, inner_ref, factor_ref, tracer_adjoint_ref, surface_ref,
+    gathered_ref, damping_ref, dampings_ref, inner_ref, factor_ref, tracer_adjoint_ref, surface_ref,
     source_scr, damping_scr, edges_scr,
 ):
     own, rows, width = inner_ref.shape
@@ -399,7 +401,7 @@
             damping_scr[owner] = gathered_ref[i, rows + 8 :]
         edges_scr[owner] = gathered_ref[i, rows : rows + 8]
     if gathered_ref.shape[1] == rows + 8:
-        for away, field in ((0, damping_ref[...]), (3, beside_ref[0]), (1, beside_ref[1]), (2, far_ref[...])):
+        for away, field in ((0, damping_ref[...]), (3, dampings_ref[0]), (1, dampings_ref[1]), (2, dampings_ref[2])):
             damping_scr[lax.rem(place + away, count)] = field
     west_edges = edges_scr[lax.rem(place + count - 1, count)]
     east_edges = edges_scr[lax.rem(place + 1, count)]
@@ -451,13 +453,12 @@
     sub_count = lax.axis_size("sub")
     edge = in_vmem(rows, width)
     levels = in_vmem(own, rows, width)
-    message_rows = in_vmem(16 + rows, width)
     marks = pltpu.VMEM((rows, width), jnp.int32)
     thickness = pltpu.with_memory_space_constraint(thickness, pltpu.SMEM)
 
     tracer, zonal_flow, wet_levels, east, west, edges = pl.pallas_call(
         pack_kernel,
-        out_shape=(levels, levels, marks, message_rows, message_rows, message_rows),
+        out_shape=(levels, levels, marks, in_vmem(16 + rows, width), in_vmem(16, width), in_vmem(16, width)),
         in_specs=[pl.BlockSpec(memory_space=pl.ANY)] * 3,
         out_specs=(VMEM_IN,) * 6,
         scratch_shapes=[pltpu.SemaphoreType.DMA((3,))],
@@ -481,9 +482,13 @@
         out_specs=(VMEM_IN,) * 6,
         name="local",
     )(*near(thickness, wet_levels, weights, inside, cotangent, edges, from_west, from_east))
-    edges = pl.pallas_call(
-        edges_kernel, out_shape=in_vmem(24, width), in_specs=[VMEM_IN] * 3, out_specs=VMEM_IN, name="edges"
-    )(*near(adjoint, top, bottom))
+    edges, wet_pair = pl.pallas_call(
+        edges_kernel,
+        out_shape=(in_vmem(24, width), in_vmem(2, rows, width)),
+        in_specs=[VMEM_IN] * 5,
+        out_specs=(VMEM_IN,) * 2,
+        name="edges",
+    )(*near(adjoint, top, bottom, wet_levels, from_west))
     other_edges = lax.ppermute(edges, "lev", [(i, i ^ 1) for i in range(lev_count)])
 
     sizes = [1]
@@ -507,9 +512,9 @@
         fluxes.append(flux)
 
     lean = sub_count == 4
-    far = damping
+    far = wet_pair
     if lean:
-        _, far = lax.optimization_barrier((edges, damping))
+        _, far = lax.optimization_barrier((edges, far))
         far = lax.ppermute(far, ("sub", "lev"), crossed([i ^ 2 for i in range(sub_count)], lev_count))
     message, ends = pl.pallas_call(
         functools.partial(final_kernel, sizes, own),
@@ -531,15 +536,15 @@
         ]
     )
 
-    next_tracer, inner, beside = pl.pallas_call(
+    next_tracer, inner, dampings = pl.pallas_call(
         rest_kernel,
-        out_shape=(jax.ShapeDtypeStruct(tracer.shape, jnp.float32), levels, in_vmem(2, rows, width)),
+        out_shape=(jax.ShapeDtypeStruct(tracer.shape, jnp.float32), levels, in_vmem(3, rows, width)),
         in_specs=[VMEM_IN] * 12,
         out_specs=(VMEM_IN,) * 3,
         name="rest",
     )(
         *near(thickness, wet_levels, ends, forward, adjoint, top, bottom, zonal_flow, meridional_flow, factor),
-        *near(from_west, from_east),
+        *near(wet_pair, far),
     )
 
     tracer_adjoint, surface = pl.pallas_call(
@@ -548,12 +553,12 @@
             jax.ShapeDtypeStruct(tracer.shape, jnp.float32),
             jax.ShapeDtypeStruct((rows, width), jnp.float32),
         ),
-        in_specs=[VMEM_IN] * 6,
+        in_specs=[VMEM_IN] * 5,
         out_specs=(VMEM_IN,) * 2,
         scratch_shapes=[pltpu.VMEM((sub_count, rows, width), jnp.float32)] * 2
         + [pltpu.VMEM((sub_count, 8, width), jnp.float32)],
         name="surface",
-    )(*near(gathered, damping, beside, far, inner, factor))
+    )(*near(gathered, damping, dampings, inner, factor))
     return (next_tracer, tracer_adjoint, surface)
 
 

time: 24.4 us -> 24.3 us (level)
  waiting for transfers between devices: 3.33 us -> 3.07 us
    ppermute x1, waiting for transfers between devices: 0.76 us -> 0.25 us  [on_device(): from_west = lax.ppermute(east, 'sub', ring)]
    ppermute x1, waiting for transfers between devices: 0.15 us -> 0.49 us  [on_device(): from_east = lax.ppermute(west, 'sub', [(b, a) for a, b in ring])]
  transfers between devices with their start and end apart: 9 -> 9, of which waited for: 5 -> 5; matrix products, arithmetic and copies ran while one was open for 0% -> 0% of each run, Pallas kernels for 10% -> 11%
where the time goes in v7:
time: 24.3 us; the launch traced here: 24.1 us
  starting transfers between devices  14.7 us (60%)
  Pallas kernels  5.61 us (23%)
  waiting for transfers between devices  3.07 us (13%)
  between operations  0.69 us (3%)
    ppermute x3, starting transfers between devices, on_device(): lax.ppermute(message if i else last, ('sub', 'lev'), crossed(way, lev_cou...  5.31 us
    ppermute x1, starting transfers between devices, on_device(): from_west = lax.ppermute(east, 'sub', ring)  3.08 us
    ppermute x1, starting transfers between devices, on_device(): from_east = lax.ppermute(west, 'sub', [(b, a) for a, b in ring])  2.09 us
    ppermute x1, starting transfers between devices, on_device(): lax.ppermute(far, ('sub', 'lev'), crossed([i ^ 2 for i in range(sub_count...  1.97 us
    ppermute x2, starting transfers between devices, on_device(): lax.ppermute(block, 'lev', [(i, i ^ 2 * size - 1) for i in range(lev_coun...  1.71 us
    pallas_call x1, Pallas kernels, on_device(): pl.pallas_call(surface_kernel, out_shape=(jax.ShapeDtypeStruct(tracer.sha...  1.3 us
    pallas_call x1, Pallas kernels, on_device(): pl.pallas_call(pack_kernel, out_shape=(levels, levels, marks, in_vmem(16...  1.23 us
    pallas_call x1, Pallas kernels, on_device(): pl.pallas_call(rest_kernel, out_shape=(jax.ShapeDtypeStruct(tracer.shape,...  1.18 us
  transfers between devices with their start and end apart: 9, of which 5 were waited for; matrix products, arithmetic and copies ran while one was open for 0% of the time, Pallas kernels for 11%

profile of v7, /device:TPU:0, one launch (start us, length us, event | category | flops | bytes accessed | tf_op | source)
XLA Modules:
  0.0 24.1 jit_solution(16887829022059714803)
XLA Ops:
  0.6 0.0 copy-start
  0.6 1.2 %pack.1 = (f32[12,32,128]{2,1,0:T(8,128)S(1)}, f32[12,32,128]{2,1,0:T(8,128)S(1)}, s32[32,128]{1,0:T(8,128)S(1)}, f32[48,128]{1,0:T(8,128)S(1)}, f32[16,128]{1,0:T(8,128)S(1)}, /*index=5*/f32[16,128]{1,0:T(8,128)S(1)}) custom-call(f32[12,32,128]{2,1,0:T(8,128)} %tracer_hbm.1, f32[12,32,128]{2,1,0:T(8,128)} %zonal_hbm.1, s32[32,128]{1,0:T(8,128)} %wet_hbm.1), custom_call_target="tpu_custom_call" | custom-call | tf_op jit(solution)/shard_map/pack/pallas_call | solution.py:459
  1.9 3.1 %collective-permute-start = (f32[48,128]{1,0:T(8,128)S(1)}, f32[48,128]{1,0:T(8,128)S(1)}, u32[]{:S(2)}, u32[]{:S(2)}) collective-permute-start(f32[48,128]{1,0:T(8,128)S(1)} %get-tuple-element.42), channel_id=1, source_target_pairs={{0,4},{4,8},{8,12},{12,0},{1,5},{5,9},{9,13},{13,1},{2,6},{6,10},{... | collective-permute-start | bytes 73736 | tf_op jit(solution)/shard_map/ppermute | solution.py:468
  5.0 2.1 %collective-permute-start.1 = (f32[16,128]{1,0:T(8,128)S(1)}, f32[16,128]{1,0:T(8,128)S(1)}, u32[]{:S(2)}, u32[]{:S(2)}) collective-permute-start(f32[16,128]{1,0:T(8,128)S(1)} %get-tuple-element.43), channel_id=1, source_target_pairs={{4,0},{8,4},{12,8},{0,12},{5,1},{9,5},{13,9},{1,13},{6,2},{10,6},{... | collective-permute-start | bytes 24584 | tf_op jit(solution)/shard_map/ppermute | solution.py:469
  7.0 0.0 copy-done
  7.1 0.0 copy-start.1
  7.1 1.1 %prepare.1 = (f32[48,128]{1,0:T(8,128)S(1)}, f32[32,128]{1,0:T(8,128)S(1)}, f32[16,128]{1,0:T(8,128)S(1)}, f32[12,32,128]{2,1,0:T(8,128)S(1)}) custom-call(f32[48]{0:T(128)} %thick_ref.1, s32[32,128]{1,0:T(8,128)S(1)} %get-tuple-element.35.wet_ref, f32[12,32,128]{2,1,0:T(8,128)S(1)} %get-tuple-element.36.tracer_ref, ...), custom_call_target="tpu_custom_call" | custom-call | tf_op jit(solution)/shard_map/prepare/pallas_call | solution.py:470
  8.1 0.5 %collective-permute-done.1.from_east_ref = f32[16,128]{1,0:T(8,128)S(1)} collective-permute-done((f32[16,128]{1,0:T(8,128)S(1)}, f32[16,128]{1,0:T(8,128)S(1)}, u32[]{:S(2)}, u32[]{:S(2)}) %collective-permute-start.1) | collective-permute-done | bytes 8224 | tf_op jit(solution)/shard_map/ppermute | solution.py:469
  8.6 0.3 %collective-permute-done.from_west_ref = f32[48,128]{1,0:T(8,128)S(1)} collective-permute-done((f32[48,128]{1,0:T(8,128)S(1)}, f32[48,128]{1,0:T(8,128)S(1)}, u32[]{:S(2)}, u32[]{:S(2)}) %collective-permute-start) | collective-permute-done | bytes 24608 | tf_op jit(solution)/shard_map/ppermute | solution.py:468
  8.9 0.0 copy-done.1
  8.9 0.4 %local.1 = (f32[384,128]{1,0:T(8,128)S(1)}, f32[12,32,128]{2,1,0:T(8,128)S(1)}, f32[12,32,128]{2,1,0:T(8,128)S(1)}, f32[12,32,128]{2,1,0:T(8,128)S(1)}, f32[12,3...) custom-call(f32[48,128]{1,0:T(8,128)S(1)} %get-tuple-element.38.thick_ref, s32[32,128]{1,0:T(8,128)S(1)} %get-tuple-element.35.wet_ref, ...), custom_call_target="tpu_custom_call" | custom-call | tf_op jit(solution)/shard_map/local/pallas_call | solution.py:478
  9.3 0.1 collective-permute-start.2
  9.4 0.2 edges.1
  9.6 0.6 %collective-permute-start.3 = (f32[24,128]{1,0:T(8,128)S(1)}, f32[24,128]{1,0:T(8,128)S(1)}, u32[]{:S(2)}, u32[]{:S(2)}) collective-permute-start(f32[24,128]{1,0:T(8,128)S(1)} %get-tuple-element.48), channel_id=1, source_target_pairs={{0,1},{1,0},{2,3},{3,2},{4,5},{5,4},{6,7},{7,6},{8,9},{9,8},{10,11... | collective-permute-start | bytes 36872 | tf_op jit(solution)/shard_map/ppermute | solution.py:492
  10.2 0.8 %collective-permute-done.3.edges_ref = f32[24,128]{1,0:T(8,128)S(1)} collective-permute-done((f32[24,128]{1,0:T(8,128)S(1)}, f32[24,128]{1,0:T(8,128)S(1)}, u32[]{:S(2)}, u32[]{:S(2)}) %collective-permute-start.3) | collective-permute-done | bytes 12320 | tf_op jit(solution)/shard_map/ppermute | solution.py:492
  11.0 0.0 collective-permute-done.2.other_ref
  11.0 0.1 merge.1
  11.1 1.6 %collective-permute-start.4 = (f32[192,128]{1,0:T(8,128)S(1)}, f32[192,128]{1,0:T(8,128)S(1)}, u32[]{:S(2)}, u32[]{:S(2)}) collective-permute-start(f32[192,128]{1,0:T(8,128)S(1)} %get-tuple-element.50.mine_ref), channel_id=1, source_target_pairs={{0,3},{1,2},{2,1},{3,0},{4,7},{5,6},{6,5},{7,4},{8,11},{9,10},{10,... | collective-permute-start | bytes 294920 | tf_op jit(solution)/shard_map/ppermute | solution.py:499
  12.7 2.0 %collective-permute-start.5 = (f32[2,32,128]{2,1,0:T(8,128)S(1)}, f32[2,32,128]{2,1,0:T(8,128)S(1)}, u32[]{:S(2)}, u32[]{:S(2)}) collective-permute-start(f32[2,32,128]{2,1,0:T(8,128)S(1)} %get-tuple-element.57.wet_pair_ref), channel_id=1, source_target_pairs={{0,9},{1,8},{2,11},{3,10},{4,13},{5,12},{6,15},{7,14},{8,1},{9,0},... | collective-permute-start | bytes 98312 | tf_op jit(solution)/shard_map/ppermute | solution.py:518
  14.7 1.1 %collective-permute-done.4.other_ref = f32[192,128]{1,0:T(8,128)S(1)} collective-permute-done((f32[192,128]{1,0:T(8,128)S(1)}, f32[192,128]{1,0:T(8,128)S(1)}, u32[]{:S(2)}, u32[]{:S(2)}) %collective-permute-start.4) | collective-permute-done | bytes 98336 | tf_op jit(solution)/shard_map/ppermute | solution.py:499
  15.8 0.1 final.1
  15.9 1.2 %collective-permute-start.8 = (f32[40,128]{1,0:T(8,128)S(1)}, f32[40,128]{1,0:T(8,128)S(1)}, u32[]{:S(2)}, u32[]{:S(2)}) collective-permute-start(f32[40,128]{1,0:T(8,128)S(1)} %get-tuple-element.61), channel_id=1, source_target_pairs={{0,5},{1,4},{2,7},{3,6},{4,13},{5,12},{6,15},{7,14},{8,1},{9,0},{1... | collective-permute-start | bytes 61448 | tf_op jit(solution)/shard_map/ppermute | solution.py:534
  17.2 2.4 %collective-permute-start.7 = (f32[40,128]{1,0:T(8,128)S(1)}, f32[40,128]{1,0:T(8,128)S(1)}, u32[]{:S(2)}, u32[]{:S(2)}) collective-permute-start(f32[40,128]{1,0:T(8,128)S(1)} %get-tuple-element.61), channel_id=1, source_target_pairs={{0,13},{1,12},{2,15},{3,14},{4,9},{5,8},{6,11},{7,10},{8,5},{9,4},... | collective-permute-start | bytes 61448 | tf_op jit(solution)/shard_map/ppermute | solution.py:534
  19.5 0.0 collective-permute-done.5.far_ref
  19.5 1.7 %collective-permute-start.6 = (f32[40,128]{1,0:T(8,128)S(1)}, f32[40,128]{1,0:T(8,128)S(1)}, u32[]{:S(2)}, u32[]{:S(2)}) collective-permute-start(f32[40,128]{1,0:T(8,128)S(1)} %get-tuple-element.61), channel_id=1, source_target_pairs={{0,9},{1,8},{2,11},{3,10},{4,1},{5,0},{6,3},{7,2},{8,13},{9,12},{1... | collective-permute-start | bytes 61448 | tf_op jit(solution)/shard_map/ppermute | solution.py:534
  21.2 1.2 %rest.1 = (f32[12,32,128]{2,1,0:T(8,128)}, f32[12,32,128]{2,1,0:T(8,128)S(1)}, f32[3,32,128]{2,1,0:T(8,128)S(1)}) custom-call(f32[48,128]{1,0:T(8,128)S(1)} %get-tuple-element.38.thick_ref, s32[32,128]{1,0:T(8,128)S(1)} %get-tuple-element.35.wet_ref, f32[4,32,128]{2,1,0:T(8,128)S(1)} %get-tuple-element.54.ends_ref, ...), custom_call_target="tpu_custom_call" | custom-call | tf_op jit(solution)/shard_map/rest/pallas_call | solution.py:539
  22.4 0.0 collective-permute-done.8
  22.4 0.0 collective-permute-done.7
  22.4 0.4 %collective-permute-done.6 = f32[40,128]{1,0:T(8,128)S(1)} collective-permute-done((f32[40,128]{1,0:T(8,128)S(1)}, f32[40,128]{1,0:T(8,128)S(1)}, u32[]{:S(2)}, u32[]{:S(2)}) %collective-permute-start.6) | collective-permute-done | bytes 20512 | tf_op jit(solution)/shard_map/ppermute | solution.py:534
  22.8 1.3 %surface.1 = (f32[12,32,128]{2,1,0:T(8,128)}, f32[32,128]{1,0:T(8,128)}) custom-call(f32[4,40,128]{2,1,0:T(8,128)S(1)} %pad_maximum_fusion.gathered_ref, f32[32,128]{1,0:T(8,128)S(1)} %get-tuple-element.52.damping_ref, f32[3,32,128]{2,1,0:T(8,128)S(1)} %get-tuple-element.62.dampings_ref, f32[12,32,128]{2,1,0:T(8,128)S(1)} %get-tuple-element.63.inner_ref, ...), custom_call_target="tpu_custom_call" | custom-call | tf_op jit(solution)/shard_map/surface/pallas_call | solution.py:550
  (1 shorter events, 0.0 us)
Async XLA Ops:
  0.6 6.4 %copy-start = (f32[12,32,128]{2,1,0:T(8,128)S(1)}, f32[12,32,128]{2,1,0:T(8,128)}, u32[]{:S(2)}) copy-start(f32[12,32,128]{2,1,0:T(8,128)} %merid_ref.3) | copy-start | bytes 589828
  1.9 7.0 %collective-permute-start = (f32[48,128]{1,0:T(8,128)S(1)}, f32[48,128]{1,0:T(8,128)S(1)}, u32[]{:S(2)}, u32[]{:S(2)}) collective-permute-start(f32[48,128]{1,0:T(8,128)S(1)} %get-tuple-element.42), channel_id=1, source_target_pairs={{0,4},{4,8},{8,12},{12,0},{1,5},{5,9},{9,13},{13,1},{2,6},{6,10},{... | collective-permute-start | bytes 73736 | tf_op jit(solution)/shard_map/ppermute | solution.py:468
  5.0 3.7 %collective-permute-start.1 = (f32[16,128]{1,0:T(8,128)S(1)}, f32[16,128]{1,0:T(8,128)S(1)}, u32[]{:S(2)}, u32[]{:S(2)}) collective-permute-start(f32[16,128]{1,0:T(8,128)S(1)} %get-tuple-element.43), channel_id=1, source_target_pairs={{4,0},{8,4},{12,8},{0,12},{5,1},{9,5},{13,9},{1,13},{6,2},{10,6},{... | collective-permute-start | bytes 24584 | tf_op jit(solution)/shard_map/ppermute | solution.py:469
  7.1 1.8 %copy-start.1 = (f32[12,32,128]{2,1,0:T(8,128)S(1)}, f32[12,32,128]{2,1,0:T(8,128)}, u32[]{:S(2)}) copy-start(f32[12,32,128]{2,1,0:T(8,128)} %cot_ref.1) | copy-start | bytes 589828
  9.3 1.7 %collective-permute-start.2 = (f32[384,128]{1,0:T(8,128)S(1)}, f32[384,128]{1,0:T(8,128)S(1)}, u32[]{:S(2)}, u32[]{:S(2)}) collective-permute-start(f32[384,128]{1,0:T(8,128)S(1)} %get-tuple-element.44.mine_ref), channel_id=1, source_target_pairs={{0,1},{1,0},{2,3},{3,2},{4,5},{5,4},{6,7},{7,6},{8,9},{9,8},{10,11... | collective-permute-start | bytes 589832 | tf_op jit(solution)/shard_map/ppermute | solution.py:499
  9.6 1.4 %collective-permute-start.3 = (f32[24,128]{1,0:T(8,128)S(1)}, f32[24,128]{1,0:T(8,128)S(1)}, u32[]{:S(2)}, u32[]{:S(2)}) collective-permute-start(f32[24,128]{1,0:T(8,128)S(1)} %get-tuple-element.48), channel_id=1, source_target_pairs={{0,1},{1,0},{2,3},{3,2},{4,5},{5,4},{6,7},{7,6},{8,9},{9,8},{10,11... | collective-permute-start | bytes 36872 | tf_op jit(solution)/shard_map/ppermute | solution.py:492
  11.1 4.7 %collective-permute-start.4 = (f32[192,128]{1,0:T(8,128)S(1)}, f32[192,128]{1,0:T(8,128)S(1)}, u32[]{:S(2)}, u32[]{:S(2)}) collective-permute-start(f32[192,128]{1,0:T(8,128)S(1)} %get-tuple-element.50.mine_ref), channel_id=1, source_target_pairs={{0,3},{1,2},{2,1},{3,0},{4,7},{5,6},{6,5},{7,4},{8,11},{9,10},{10,... | collective-permute-start | bytes 294920 | tf_op jit(solution)/shard_map/ppermute | solution.py:499
  12.7 6.8 %collective-permute-start.5 = (f32[2,32,128]{2,1,0:T(8,128)S(1)}, f32[2,32,128]{2,1,0:T(8,128)S(1)}, u32[]{:S(2)}, u32[]{:S(2)}) collective-permute-start(f32[2,32,128]{2,1,0:T(8,128)S(1)} %get-tuple-element.57.wet_pair_ref), channel_id=1, source_target_pairs={{0,9},{1,8},{2,11},{3,10},{4,13},{5,12},{6,15},{7,14},{8,1},{9,0},... | collective-permute-start | bytes 98312 | tf_op jit(solution)/shard_map/ppermute | solution.py:518
  15.9 6.5 %collective-permute-start.8 = (f32[40,128]{1,0:T(8,128)S(1)}, f32[40,128]{1,0:T(8,128)S(1)}, u32[]{:S(2)}, u32[]{:S(2)}) collective-permute-start(f32[40,128]{1,0:T(8,128)S(1)} %get-tuple-element.61), channel_id=1, source_target_pairs={{0,5},{1,4},{2,7},{3,6},{4,13},{5,12},{6,15},{7,14},{8,1},{9,0},{1... | collective-permute-start | bytes 61448 | tf_op jit(solution)/shard_map/ppermute | solution.py:534
  17.2 5.3 %collective-permute-start.7 = (f32[40,128]{1,0:T(8,128)S(1)}, f32[40,128]{1,0:T(8,128)S(1)}, u32[]{:S(2)}, u32[]{:S(2)}) collective-permute-start(f32[40,128]{1,0:T(8,128)S(1)} %get-tuple-element.61), channel_id=1, source_target_pairs={{0,13},{1,12},{2,15},{3,14},{4,9},{5,8},{6,11},{7,10},{8,5},{9,4},... | collective-permute-start | bytes 61448 | tf_op jit(solution)/shard_map/ppermute | solution.py:534
  19.5 3.3 %collective-permute-start.6 = (f32[40,128]{1,0:T(8,128)S(1)}, f32[40,128]{1,0:T(8,128)S(1)}, u32[]{:S(2)}, u32[]{:S(2)}) collective-permute-start(f32[40,128]{1,0:T(8,128)S(1)} %get-tuple-element.61), channel_id=1, source_target_pairs={{0,9},{1,8},{2,11},{3,10},{4,1},{5,0},{6,3},{7,2},{8,13},{9,12},{1... | collective-permute-start | bytes 61448 | tf_op jit(solution)/shard_map/ppermute | solution.py:534
